TPU v7x, 256 devices: a whole 4x4x8 slice. The times are simulated.
256 devices in a mesh: group: 8 (over x, core), dev: 32 (over z, y).
Axes of the slice: x: 4, y: 4, z: 8, core: 2. Of those that a mesh axis runs over, the one named last changes fastest.
Arguments:
- features: bfloat16 [1048576, 128], P(('group', 'dev')), may hold values from -6 to 6
- coords: bfloat16 [3, 1048576], P(None, ('group', 'dev')), may hold values from 0 to 1
- near_pairs: int32 [2, 8192], P(None, 'group'), may hold values from 0 to 511, as said below
- parent_two: int32 [4096], P(('group', 'dev')), may hold values from 0 to 127, as said below
- parent_three: int32 [1024], P('group'), may hold values from 0 to 7
- rates: float32 [4], replicated, may hold values from 6 to 40
- w_near: bfloat16 [128, 128], replicated, may hold values from -0.5 to 0.5
- restrict: bfloat16 [64, 256], replicated, may hold values from -0.375 to 0.375
- w_two: bfloat16 [128, 128], replicated, may hold values from -0.5 to 0.5
- w_three: bfloat16 [128, 128], replicated, may hold values from -0.5 to 0.5
- w_four: bfloat16 [128, 128], replicated, may hold values from -0.5 to 0.5
- coupling: bfloat16 [64, 64], replicated, may hold values from -0.75 to 0.75
- expand: bfloat16 [256, 64], replicated, may hold values from -0.75 to 0.75
- w_out: bfloat16 [128, 128], replicated, may hold values from -0.5 to 0.5
Outputs:
- mixed: bfloat16 [1048576, 128], P(('group', 'dev'))
Inputs may be any that keep to these rules, and one draw needn't show every extreme that they name: `near_pairs`: for any two devices A and P of dev in one region, at most 2 near pairs of that region have their first block on A and their second on P, and in each region some such two devices have exactly 2. `parent_two`: every level-two node of a region is named by exactly four blocks of that region.
All inputs are finite; a program needn't handle non-finite values.
Results may differ from a plain program's by a relative error of at most 0.008.
Values may be sent and summed in bfloat16 or wider, within the bound.
No kernel may reach another device: no remote copies, remote signals or barrier semaphores. Data moves between devices by JAX's collectives and lax.ppermute only.
A program may use at most 128 MiB of HBM per device.

v0:
```python
import functools
import math

import jax
import jax.numpy as jnp
from jax import lax
from jax.experimental import pallas as pl
from jax.experimental.pallas import tpu as pltpu
from jax.sharding import Mesh
from jax.sharding import PartitionSpec as P

NODES3_GROUP = 8
DEV = ("dev_0", "dev_1")
GROUP_DEV = ("group", "dev_0", "dev_1")
F32 = jnp.float32
BF16 = jnp.bfloat16
ROWS = 8
COLS = 4
BLK = 16
RBLK = BLK * COLS
B = 256
HC = 32
AUG = 16
VROWS = BLK * HC
MROWS = VROWS + 3 * BLK
UNROLL = 16
VMEM_LIMIT = 58 << 20
VMEM_SMALL = 20 << 20


def dot_t(a, b, dims):
    return lax.dot_general(a, b, (dims, ((), ())), preferred_element_type=F32)


def vmem():
    return pl.BlockSpec(memory_space=pltpu.VMEM)


def smem():
    return pl.BlockSpec(memory_space=pltpu.SMEM)


def params(limit=VMEM_LIMIT):
    return pltpu.CompilerParams(vmem_limit_bytes=limit)


def prep_kernel(y_ref, f_ref, xyz_ref, wn_ref, re_ref, *outs):
    m_refs, lev_ref = outs[:COLS], outs[COLS]
    shift = lax.rem(128 - HC * y_ref[0], 128)
    w_near = pltpu.roll(wn_ref[...].astype(F32), shift, 1).astype(BF16)
    for i in range(BLK):
        f = f_ref[i * B : (i + 1) * B, :]
        v = dot_t(w_near, f, ((0,), (1,))).astype(BF16)
        for s in range(COLS):
            m_refs[s][i * HC : (i + 1) * HC, :] = v[s * HC : (s + 1) * HC]
        lev_ref[i] = jnp.dot(re_ref[...], f, preferred_element_type=F32).astype(BF16)
    xyz = xyz_ref[...].astype(F32)
    rows = [xyz[k : k + 1, i * B : (i + 1) * B] for k in range(3) for i in range(BLK)]
    rows = jnp.concatenate(rows, axis=0).astype(BF16)
    for s in range(COLS):
        m_refs[s][VROWS:, :] = rows


def prep(y, features, xyz, w_near, restrict):
    *messages, level_one = pl.pallas_call(
        prep_kernel,
        in_specs=[smem()] + [vmem()] * 4,
        out_shape=[jax.ShapeDtypeStruct((MROWS, B), BF16)] * COLS
        + [jax.ShapeDtypeStruct((BLK, 64, 128), BF16)],
        compiler_params=params(),
        name="prep",
    )(y, features, xyz, w_near, restrict)
    return messages, level_one


def pack_kernel(*refs):
    for s in range(COLS):
        refs[COLS][s] = refs[s][...]


def pack(messages):
    return pl.pallas_call(
        pack_kernel,
        out_shape=jax.ShapeDtypeStruct((COLS, MROWS, B), BF16),
        compiler_params=params(VMEM_SMALL),
        name="pack",
    )(*messages)


def pieces(x):
    one = x.astype(BF16).astype(F32)
    rest = x - one
    two = rest.astype(BF16).astype(F32)
    three = (rest - two).astype(BF16).astype(F32)
    return (one, two, three)


def row_at(width):
    return lax.broadcasted_iota(jnp.int32, (AUG, width), 0)


def stacked(rows, at):
    out = jnp.zeros(at.shape, F32)
    for k, row in enumerate(rows):
        out = jnp.where(at == k, row, out)
    return out.astype(BF16)


def norm_of(axes):
    return axes[0] * axes[0] + axes[1] * axes[1] + axes[2] * axes[2]


def build_src(scale, xyz_of, count, src_ref):
    at = row_at(B)
    turn = [(at == k) | (at == k + 3) | (at == k + 6) for k in range(3)]
    base = jnp.where((at >= 9) & (at < 12), 1.0, 0.0)

    def body(y, carry):
        xyz = xyz_of(y)
        axes = [xyz[k * BLK : (k + 1) * BLK] for k in range(3)]
        norm = pieces(-scale * norm_of(axes))
        for b in range(BLK):
            out = base
            for k in range(3):
                out = jnp.where(turn[k], axes[k][b : b + 1], out)
                out = jnp.where(at == 12 + k, norm[k][b : b + 1], out)
            src_ref[y * BLK + b] = out.astype(BF16)
        return carry

    lax.fori_loop(0, count, body, 0)


def build_dst(scale, xyz_of, dst_ref):
    at = row_at(B)

    def body(y, carry):
        xyz = xyz_of(y)
        axes = [xyz[k * BLK : (k + 1) * BLK] for k in range(3)]
        norm = pieces(-scale * norm_of(axes))
        parts = [pieces(2.0 * scale * a) for a in axes]
        base = jnp.where((at >= 12) & (at < 15), 1.0, 0.0)
        for b in range(BLK):
            out = base
            for k in range(3):
                for i in range(3):
                    out = jnp.where(at == 3 * i + k, parts[k][i][b : b + 1], out)
                out = jnp.where(at == 9 + k, norm[k][b : b + 1], out)
            dst_ref[y * BLK + b] = out.astype(BF16)
        return carry

    lax.fori_loop(0, COLS, body, 0)


def near_kernel(number, lengths, first, last, scale_ref, cnt, lst, *refs):
    n = len(lengths)
    chunks = refs[:n]
    acc, buf, src_ref, dst_ref, sem, end_sem = refs[-6:]
    at, moves = 0, []
    for i, length in enumerate(lengths):
        moves.append(pltpu.make_async_copy(chunks[i], buf.at[pl.ds(at, length)], sem.at[i]))
        at += length
    late = []
    if not first:
        acc_in, dst_in = refs[n : n + 2]
        late.append(pltpu.make_async_copy(acc_in, acc, sem.at[2]))
        late.append(pltpu.make_async_copy(dst_in, dst_ref, sem.at[3]))
    for move in moves + late:
        move.start()
    if first:
        acc[...] = jnp.zeros_like(acc)
    for move in moves:
        move.wait()
    scale = scale_ref[0]

    def xyz_of(y):
        return buf[y, VROWS:, :].astype(F32)

    build_src(scale, xyz_of, at, src_ref)
    if first:
        build_dst(scale, xyz_of, dst_ref)
    for move in late:
        move.wait()

    def body(i, carry):
        done = []
        for u in range(UNROLL):
            code = lst[number, i * UNROLL + u]
            dst = code >> 7
            src = code & 127
            power = dot_t(dst_ref[jnp.minimum(dst, RBLK - 1)], src_ref[src], ((0,), (0,)))
            table = jnp.exp2(power).astype(BF16)
            start = pl.multiple_of((src & (BLK - 1)) * HC, HC)
            values = buf[src >> 4, pl.ds(start, HC), :]
            done.append((dst, dot_t(values, table, ((1,), (1,)))))
        for dst, term in done:
            acc[dst] += term
        return carry

    lax.fori_loop(0, (cnt[number] + UNROLL - 1) // UNROLL, body, 0)
    if last:
        outs = refs[n + 2 : n + 2 + COLS]
        ends = []
        for y in range(COLS):
            block = slice(y * BLK, (y + 1) * BLK)
            buf[y, :VROWS, :] = acc[block].reshape(VROWS, B).astype(BF16)
            ends.append(pltpu.make_async_copy(buf.at[y, :VROWS], outs[y], end_sem.at[y]))
    elif first:
        acc_out, dst_out = refs[n : n + 2]
        ends = [
            pltpu.make_async_copy(acc, acc_out, end_sem.at[0]),
            pltpu.make_async_copy(dst_ref, dst_out, end_sem.at[1]),
        ]
    else:
        ends = [pltpu.make_async_copy(acc, refs[n + 2], end_sem.at[0])]
    for move in ends:
        move.start()
    for move in ends:
        move.wait()


def near_step(scale, cnt, lst, number, chunks, sums=(), last=False):
    first = not sums
    anywhere = pl.BlockSpec(memory_space=pl.ANY)
    lengths = tuple(c.shape[0] for c in chunks)
    args = [scale, cnt, lst, *chunks, *sums]
    acc_shape = (RBLK + 1, HC, B)
    dst_shape = (RBLK, AUG, B)
    shapes = [jax.ShapeDtypeStruct(acc_shape, F32)]
    if first:
        shapes.append(jax.ShapeDtypeStruct(dst_shape, BF16))
    if last:
        shapes = [jax.ShapeDtypeStruct((VROWS, B), BF16)] * COLS
    sides = 9 * sum(lengths)
    return pl.pallas_call(
        functools.partial(near_kernel, number, lengths, first, last),
        in_specs=[smem()] * 3 + [anywhere] * (len(args) - 3),
        out_specs=[anywhere] * len(shapes),
        out_shape=shapes,
        scratch_shapes=[
            pltpu.VMEM(acc_shape, F32),
            pltpu.VMEM((sum(lengths), MROWS, B), BF16),
            pltpu.VMEM((sum(lengths) * BLK, AUG, B), BF16),
            pltpu.VMEM(dst_shape, BF16),
            pltpu.SemaphoreType.DMA((4,)),
            pltpu.SemaphoreType.DMA((COLS,)),
        ],
        compiler_params=params(VMEM_SMALL if last else VMEM_LIMIT),
        cost_estimate=pl.CostEstimate(
            flops=sides * 2 * B * B * 256, bytes_accessed=4 << 20, transcendentals=sides * B * B
        ),
        name="near",
    )(*args)


def cut_kernel(below, above, low, high):
    low[...] = below[...]
    high[...] = above[...]


def cut_halves(below, above):
    half = COLS // 2
    block = (1, MROWS, B)
    shape = jax.ShapeDtypeStruct((half, MROWS, B), BF16)
    return pl.pallas_call(
        cut_kernel,
        grid=(half,),
        in_specs=[
            pl.BlockSpec(block, lambda i: (i, 0, 0)),
            pl.BlockSpec(block, lambda i: (half + i, 0, 0)),
        ],
        out_specs=[pl.BlockSpec(block, lambda i: (i, 0, 0))] * 2,
        out_shape=[shape] * 2,
        compiler_params=params(),
        name="cut",
    )(below, above)


def side_lists(near_pairs, z, y):
    dst = jnp.concatenate([near_pairs[0], near_pairs[1]])
    src = jnp.concatenate([near_pairs[1], near_pairs[0]])
    n = dst.shape[0]
    rel = jnp.remainder(src // RBLK - z, ROWS)
    kind = jnp.where(dst // RBLK == z, jnp.minimum(rel, ROWS - rel), -1)
    slot = jnp.where((rel >= 1) & (rel <= 3), RBLK, 0)
    kinds = ROWS // 2 + 1
    cap = 2 * RBLK
    hit = kind[None, :] == jnp.arange(kinds, dtype=jnp.int32)[:, None]
    cells = hit.reshape(kinds, n // 128, 128).astype(BF16)
    lane = jnp.arange(128, dtype=jnp.int32)
    upto = (lane[:, None] < lane[None, :]).astype(BF16)
    within = jnp.einsum("kab,bc->kac", cells, upto, preferred_element_type=F32)
    total = jnp.sum(cells.astype(F32), axis=2)
    chunk = jnp.arange(n // 128, dtype=jnp.int32)
    before = jnp.sum(
        jnp.where(chunk[None, None, :] < chunk[None, :, None], total[:, None, :], 0.0), axis=2
    )
    rank = (within + before[:, :, None]).astype(jnp.int32).reshape(kinds, n)
    rank = jnp.where(hit, rank, -1)

    def local(block):
        return jnp.remainder(y - block // BLK, COLS) * BLK + block % BLK

    code = local(dst) * cap + slot + local(src)
    place = jnp.arange(cap, dtype=jnp.int32)
    lists = jnp.sum(
        jnp.where(rank[:, None, :] == place[None, :, None], code[None, None, :], 0), axis=2
    )
    count = jnp.sum(hit.astype(jnp.int32), axis=1)
    lists = jnp.where(place[None, :] < count[:, None], lists, RBLK * cap)
    return count.astype(jnp.int32), lists


def turned(y, channels_first):
    row = lax.broadcasted_iota(jnp.int32, (128, 128), 0)
    col = lax.broadcasted_iota(jnp.int32, (128, 128), 1)
    turn = jnp.where(lax.rem(row + HC * y, 128) == col, B ** (-0.5), 0.0).astype(BF16)
    return dot_t(channels_first, turn, ((0,), (0,)))


def home_kernel(y_ref, scale_ref, v0, v1, v2, v3, x_ref, y_row, z_ref, pd_ref, ex_ref, wo_ref, out_ref):
    y = y_ref[0]
    at = row_at(B)
    ones = [jnp.ones((1, B), F32)] * 3
    for i in range(4):
        b = pl.program_id(0) * 4 + i
        mine = lax.broadcasted_iota(jnp.int32, (BLK, B), 0) == b
        axes = [
            jnp.sum(jnp.where(mine, r[...].astype(F32), 0.0), axis=0, keepdims=True)
            for r in (x_ref, y_row, z_ref)
        ]
        norm = list(pieces(-norm_of(axes)))
        src = stacked(axes + ones + norm, at)
        dst = stacked([2.0 * a for a in axes] + norm + ones, at)
        power = dot_t(dst, src, ((0,), (0,)))
        near = []
        for s, v_ref in enumerate((v0, v1, v2, v3)):
            table = jnp.exp2(power * scale_ref[lax.rem(y + s, COLS)]).astype(BF16)
            near.append(dot_t(v_ref[i * HC : (i + 1) * HC, :], table, ((1,), (1,))))
        near = jnp.concatenate(near, axis=0).astype(BF16)
        far = jnp.dot(ex_ref[...], pd_ref[i], preferred_element_type=F32).astype(BF16)
        out_ref[i * B : (i + 1) * B, :] = turned(y, near) + jnp.dot(
            far, wo_ref[...], preferred_element_type=F32
        )


def home(y, scales, messages, parent_down, expand, w_out):
    row = VROWS // BLK
    return pl.pallas_call(
        home_kernel,
        grid=(BLK // 4,),
        in_specs=[smem(), smem()]
        + [pl.BlockSpec((4 * HC, B), lambda i: (i, 0))] * COLS
        + [
            pl.BlockSpec((BLK, B), lambda i: (row, 0)),
            pl.BlockSpec((BLK, B), lambda i: (row + 1, 0)),
            pl.BlockSpec((BLK, B), lambda i: (row + 2, 0)),
            pl.BlockSpec((4, 64, 128), lambda i: (i, 0, 0)),
            pl.BlockSpec((B, 64), lambda i: (0, 0)),
            pl.BlockSpec((128, 128), lambda i: (0, 0)),
        ],
        out_specs=pl.BlockSpec((4 * B, 128), lambda i: (i, 0)),
        out_shape=jax.ShapeDtypeStruct((BLK * B, 128), F32),
        compiler_params=params(VMEM_SMALL),
        cost_estimate=pl.CostEstimate(
            flops=64 * 2 * B * B * 256, bytes_accessed=3 << 20, transcendentals=64 * B * B
        ),
        name="home",
    )(y, scales, *messages, *[messages[0]] * 3, parent_down, expand, w_out)


def final_kernel(y_ref, home_ref, n0, n1, n2, n3, out_ref):
    for i in range(4):
        near = [n[i * HC : (i + 1) * HC, :] for n in (n0, n1, n2, n3)]
        near = jnp.concatenate(near, axis=0)
        block = slice(i * B, (i + 1) * B)
        out_ref[block, :] = (home_ref[block, :] + turned(y_ref[0], near)).astype(BF16)


def final(y, own, near):
    return pl.pallas_call(
        final_kernel,
        grid=(BLK // 4,),
        in_specs=[smem(), pl.BlockSpec((4 * B, 128), lambda i: (i, 0))]
        + [pl.BlockSpec((4 * HC, B), lambda i: (i, 0))] * COLS,
        out_specs=pl.BlockSpec((4 * B, 128), lambda i: (i, 0)),
        out_shape=jax.ShapeDtypeStruct((BLK * B, 128), BF16),
        compiler_params=params(VMEM_SMALL),
        name="final",
    )(y, own, *near)


def copies(array, axis):
    sent = jnp.broadcast_to(array, (lax.axis_size(axis), *array.shape))
    return lax.all_to_all(sent, axis, 0, 0, tiled=True)


def by_channel(array, weight):
    return jnp.dot(
        array.reshape(-1, weight.shape[0]), weight, preferred_element_type=F32
    )


def spread_summaries(level_one, parent_two):
    channels = level_one.shape[2]
    peers = ROWS * COLS
    sent = level_one.reshape(BLK, peers, 2, channels).transpose(1, 0, 2, 3)
    sent = sent.reshape(peers, BLK * 2, channels)
    row = jnp.pad(parent_two.astype(BF16)[None, :], ((0, 7), (0, channels - BLK)))
    sent = jnp.concatenate([sent, jnp.broadcast_to(row, (peers, 8, channels))], axis=1)
    return lax.all_to_all(sent, DEV, 0, 0, tiled=True)


def far_up(arrived, parent_three, w_two):
    peers = arrived.shape[0]
    nodes = parent_three.shape[0]
    rows = arrived[:, : BLK * 2].reshape(peers * BLK, -1)
    parents = arrived[:, BLK * 2, :BLK].reshape(-1).astype(jnp.int32)
    select = (jnp.arange(nodes, dtype=jnp.int32)[:, None] == parents[None, :]).astype(BF16)
    level_sum = jnp.dot(select, rows, preferred_element_type=F32).astype(BF16)
    level_two = jax.nn.gelu(by_channel(level_sum, w_two)).astype(BF16).reshape(nodes, -1)
    coarse = jnp.arange(NODES3_GROUP, dtype=jnp.int32)
    select_three = (coarse[:, None] == parent_three[None, :]).astype(BF16)
    level_three = jnp.dot(select_three, level_two, preferred_element_type=F32)
    level_three = (level_three * (NODES3_GROUP / nodes)).astype(BF16)
    return parents, level_two, level_three


def far_down(parents, level_two, three_all, parent_three, w_three, w_four, coupling):
    nodes = parent_three.shape[0]
    coarse = jnp.arange(NODES3_GROUP, dtype=jnp.int32)
    mine = lax.axis_index("group") * NODES3_GROUP
    coupling_rows = lax.dynamic_slice_in_dim(coupling, mine, NODES3_GROUP, 0)
    mixed = jnp.dot(coupling_rows, three_all, preferred_element_type=F32).astype(BF16)
    down_three = jax.nn.gelu(by_channel(mixed, w_three)).astype(BF16).reshape(NODES3_GROUP, -1)
    lift = (parent_three[:, None] == coarse[None, :]).astype(BF16)
    lifted = by_channel(level_two, w_four).reshape(nodes, -1)
    down_two = jax.nn.gelu(lifted + jnp.dot(lift, down_three, preferred_element_type=F32))
    down_two = down_two.astype(BF16)
    spread = (parents[:, None] == jnp.arange(nodes, dtype=jnp.int32)[None, :]).astype(BF16)
    down = jnp.dot(spread, down_two, preferred_element_type=F32).astype(BF16)
    return lax.all_to_all(down.reshape(-1, BLK, down.shape[1]), DEV, 0, 0, tiled=True)


def per_device(
    features,
    coords,
    near_pairs,
    parent_two,
    parent_three,
    rates,
    w_near,
    restrict,
    w_two,
    w_three,
    w_four,
    coupling,
    expand,
    w_out,
):
    z = lax.axis_index("dev_0").astype(jnp.int32)
    y = lax.axis_index("dev_1").astype(jnp.int32)
    y_one = y.reshape(1)
    messages, level_one = prep(y_one, features, coords, w_near, restrict)
    ahead = [[(i, (i + s) % COLS) for i in range(COLS)] for s in range(COLS)]
    back_to = [[(i, (i - s) % COLS) for i in range(COLS)] for s in range(COLS)]
    pieces_in = [messages[0]]
    pieces_in += [lax.ppermute(messages[s], "dev_1", ahead[s]) for s in range(1, COLS)]
    arrived = spread_summaries(level_one, parent_two)
    held = pack(pieces_in)
    scales = rates * math.log2(math.e)
    scale = jnp.sum(jnp.where(jnp.arange(COLS) == y, scales, 0.0)).reshape(1)
    cnt, lst = side_lists(near_pairs, z, y)
    held, cnt, lst = lax.optimization_barrier((held, cnt, lst))

    up = [(i, (i + 1) % ROWS) for i in range(ROWS)]
    down = [(i, (i - 1) % ROWS) for i in range(ROWS)]
    step = functools.partial(near_step, scale, cnt, lst)
    below = lax.ppermute(held, "dev_0", up)
    above = lax.ppermute(held, "dev_0", down)
    held, arrived = lax.optimization_barrier((held, arrived))
    acc, dst_aug = step(0, [held])
    parents, level_two, level_three = far_up(arrived, parent_three, w_two)
    below, above, acc, level_three = lax.optimization_barrier((below, above, acc, level_three))
    three_all = copies(level_three, "group").reshape(-1, level_three.shape[1])
    below_next = lax.ppermute(below, "dev_0", up)
    above_next = lax.ppermute(above, "dev_0", down)
    (acc,) = step(1, [below, above], (acc, dst_aug))
    below, above, acc, three_all = lax.optimization_barrier(
        (below_next, above_next, acc, three_all)
    )
    back = far_down(parents, level_two, three_all, parent_three, w_three, w_four, coupling)
    below_next = lax.ppermute(below, "dev_0", up)
    above_next = lax.ppermute(above, "dev_0", down)
    (acc,) = step(2, [below, above], (acc, dst_aug))
    below, above, acc = lax.optimization_barrier((below_next, above_next, acc))
    low, high = cut_halves(below, above)
    low = lax.ppermute(low, "dev_0", up)
    high = lax.ppermute(high, "dev_0", down)
    (acc,) = step(3, [below, above], (acc, dst_aug))
    low, high, acc, back = lax.optimization_barrier((low, high, acc, back))
    near = step(4, [low, high], (acc, dst_aug), last=True)
    parent_down = back.reshape(ROWS * COLS, BLK, 2, -1).transpose(1, 0, 2, 3)
    parent_down = parent_down.reshape(BLK, 2 * ROWS * COLS, -1)
    near, messages, parent_down = lax.optimization_barrier((near, messages, parent_down))
    own = home(y_one, scales, messages, parent_down, expand, w_out)
    returned = [near[0]]
    returned += [lax.ppermute(near[s], "dev_1", back_to[s]) for s in range(1, COLS)]
    return final(y_one, own, returned)


def solution(mesh):
    torus = Mesh(mesh.devices.reshape(mesh.shape["group"], ROWS, COLS), GROUP_DEV)
    in_specs = (
        P(GROUP_DEV, None),
        P(None, GROUP_DEV),
        P(None, "group"),
        P(GROUP_DEV),
        P("group"),
        P(),
        P(),
        P(),
        P(),
        P(),
        P(),
        P(),
        P(),
        P(),
    )
    out_specs = P(GROUP_DEV, None)
    return jax.shard_map(
        per_device, mesh=torus, in_specs=in_specs, out_specs=out_specs, check_vma=False
    )
```

profile of v0, /device:TPU:6, one launch (start us, length us, event | category | flops | bytes accessed | tf_op | source)
XLA Modules:
  0.0 164.5 jit_solution(5242129843593158856)
XLA Ops:
  0.0 3.1 %prep.1 = (bf16[560,256]{1,0:T(8,128)(2,1)}, bf16[560,256]{1,0:T(8,128)(2,1)}, bf16[560,256]{1,0:T(8,128)(2,1)}, bf16[560,256]{1,0:T(8,128)(2,1)}, bf16[16,64,128]{2,1,0:T(8,128)(2,1)}) custom-call(s32[1]{0:T(128)} %bitcast.y_ref, bf16[4096,128]{1,0:T(8,128)(2,1)} %f_ref.1, bf16[3,4096]{1,0:T(4,128)(2,1)} %xyz_ref.1, bf16[128,128]{1,0:T(8,128)(2,1)} %wn_ref.1, ...), custom_call_target="tpu_custom_call" | custom-call | tf_op jit(solution)/shard_map/prep/pallas_call | solution.py:65
  3.1 1.6 collective-permute-start
  4.7 2.9 %collective-permute-start.1 = (bf16[560,256]{1,0:T(8,128)(2,1)}, bf16[560,256]{1,0:T(8,128)(2,1)S(1)}, u32[]{:S(2)}, u32[]{:S(2)}) collective-permute-start(bf16[560,256]{1,0:T(8,128)(2,1)} %get-tuple-element.82.v2), channel_id=1, source_target_pairs={{0,2},{1,3},{2,0},{3,1},{4,6},{5,7},{6,4},{7,5},{8,10},{9,11},{10,... | collective-permute-start | bytes 860168 | tf_op jit(solution)/shard_map/ppermute | solution.py:467
  7.6 1.3 collective-permute-start.2
  11.5 9.0 %all-to-all-start = ((bf16[32,40,128]{2,1,0:T(8,128)(2,1)}), bf16[32,40,128]{2,1,0:T(8,128)(2,1)S(1)}, u32[]{:S(2)}, u32[]{:S(2)}) async-start(bf16[32,40,128]{2,1,0:T(8,128)(2,1)} %copy.29), calls=%async_computation | async-start | bytes 655360 | tf_op jit(solution)/shard_map/all_to_all | solution.py:410
  22.6 1.9 %collective-permute-start.3 = (bf16[4,560,256]{2,1,0:T(8,128)(2,1)S(1)}, bf16[4,560,256]{2,1,0:T(8,128)(2,1)}, u32[]{:S(2)}, u32[]{:S(2)}) collective-permute-start(bf16[4,560,256]{2,1,0:T(8,128)(2,1)S(1)} %pack.1.refs_0_), channel_id=1, source_target_pairs={{0,4},{4,8},{8,12},{12,16},{16,20},{20,24},{24,28},{28,0},{1,5},{5... | collective-permute-start | bytes 3440648 | tf_op jit(solution)/shard_map/ppermute | solution.py:478
  24.5 2.5 %collective-permute-start.4 = (bf16[4,560,256]{2,1,0:T(8,128)(2,1)S(1)}, bf16[4,560,256]{2,1,0:T(8,128)(2,1)}, u32[]{:S(2)}, u32[]{:S(2)}) collective-permute-start(bf16[4,560,256]{2,1,0:T(8,128)(2,1)S(1)} %pack.1.refs_0_), channel_id=1, source_target_pairs={{0,28},{4,0},{8,4},{12,8},{16,12},{20,16},{24,20},{28,24},{1,29},{... | collective-permute-start | bytes 3440648 | tf_op jit(solution)/shard_map/ppermute | solution.py:479
  27.6 7.7 %all-to-all-done = bf16[32,40,128]{2,1,0:T(8,128)(2,1)S(1)} async-done(((bf16[32,40,128]{2,1,0:T(8,128)(2,1)}), bf16[32,40,128]{2,1,0:T(8,128)(2,1)S(1)}, u32[]{:S(2)}, u32[]{:S(2)}) %all-to-all-start) | async-done | bytes 327712 | tf_op jit(solution)/shard_map/all_to_all | solution.py:410
  36.1 7.9 %near.5 = (f32[65,32,256]{2,1,0:T(8,128)}, bf16[64,16,256]{2,1,0:T(8,128)(2,1)}) custom-call(f32[1]{0:T(128)} %bitcast.1.scale_ref, s32[5]{0:T(128)} %copy-done.4, s32[5,128]{1,0:T(8,128)} %fusion.66.lst, bf16[4,560,256]{2,1,0:T(8,128)(2,1)} %copy-done.1), custom_call_target="tpu_custom_call" | custom-call | flops 1207959552 | bytes 4194304 | tf_op jit(solution)/shard_map/near/pallas_call | solution.py:234
  44.2 10.6 %collective-permute-done.3.refs_0_ = bf16[4,560,256]{2,1,0:T(8,128)(2,1)} collective-permute-done((bf16[4,560,256]{2,1,0:T(8,128)(2,1)S(1)}, bf16[4,560,256]{2,1,0:T(8,128)(2,1)}, u32[]{:S(2)}, u32[]{:S(2)}) %collective-permute-start.3) | collective-permute-done | bytes 1146912 | tf_op jit(solution)/shard_map/ppermute | solution.py:478
  54.8 3.2 %collective-permute-start.6 = (bf16[4,560,256]{2,1,0:T(8,128)(2,1)}, bf16[4,560,256]{2,1,0:T(8,128)(2,1)S(1)}, u32[]{:S(2)}, u32[]{:S(2)}) collective-permute-start(bf16[4,560,256]{2,1,0:T(8,128)(2,1)} %collective-permute-done.4.refs_1_), channel_id=1, source_target_pairs={{0,28},{4,0},{8,4},{12,8},{16,12},{20,16},{24,20},{28,24},{1,29},{... | collective-permute-start | bytes 3440648 | tf_op jit(solution)/shard_map/ppermute | solution.py:486
  58.6 4.8 %all-to-all-start.1 = ((bf16[8,8,256]{2,1,0:T(8,128)(2,1)}), bf16[8,8,256]{2,1,0:T(8,128)(2,1)S(1)}, u32[]{:S(2)}, u32[]{:S(2)}) async-start(bf16[8,8,256]{2,1,0:T(8,128)(2,1)} %broadcast_in_dim.90), calls=%async_computation.1 | async-start | bytes 65536 | tf_op jit(solution)/shard_map/all_to_all | solution.py:394
  63.4 10.8 %near.6.refs_2_ = f32[65,32,256]{2,1,0:T(8,128)} custom-call(f32[1]{0:T(128)} %bitcast.1.scale_ref, s32[5]{0:T(128)} %copy-done.4, s32[5,128]{1,0:T(8,128)} %fusion.66.lst, bf16[4,560,256]{2,1,0:T(8,128)(2,1)} %collective-permute-done.3.refs_0_, bf16[4,560,256]{2,1,0:T(8,128)(2,1)} %collective-permute-done.4.refs_1_, ...), custom_call_target="tpu_custom_call" | custom-call | flops 2415919104 | bytes 4194304 | tf_op jit(solution)/shard_map/near/pallas_call | solution.py:234
  74.2 8.6 %collective-permute-done.5.refs_0_ = bf16[4,560,256]{2,1,0:T(8,128)(2,1)} collective-permute-done((bf16[4,560,256]{2,1,0:T(8,128)(2,1)}, bf16[4,560,256]{2,1,0:T(8,128)(2,1)}, u32[]{:S(2)}, u32[]{:S(2)}) %collective-permute-start.5) | collective-permute-done | bytes 1146912 | tf_op jit(solution)/shard_map/ppermute | solution.py:485
  82.8 1.0 copy-done.20
  84.5 2.5 %collective-permute-start.8 = (bf16[4,560,256]{2,1,0:T(8,128)(2,1)}, bf16[4,560,256]{2,1,0:T(8,128)(2,1)S(1)}, u32[]{:S(2)}, u32[]{:S(2)}) collective-permute-start(bf16[4,560,256]{2,1,0:T(8,128)(2,1)} %copy-done.20), channel_id=1, source_target_pairs={{0,28},{4,0},{8,4},{12,8},{16,12},{20,16},{24,20},{28,24},{1,29},{... | collective-permute-start | bytes 3440648 | tf_op jit(solution)/shard_map/ppermute | solution.py:493
  88.2 10.8 %near.7.refs_2_ = f32[65,32,256]{2,1,0:T(8,128)} custom-call(f32[1]{0:T(128)} %bitcast.1.scale_ref, s32[5]{0:T(128)} %copy-done.4, s32[5,128]{1,0:T(8,128)} %fusion.66.lst, bf16[4,560,256]{2,1,0:T(8,128)(2,1)} %collective-permute-done.5.refs_0_, bf16[4,560,256]{2,1,0:T(8,128)(2,1)} %copy-done.20, f32[65,32,256]{2,1,0:T(8,128)} %near.6.refs_2_, ...), custom_call_target="tpu_custom_call" | custom-call | flops 2415919104 | bytes 4194304 | tf_op jit(solution)/shard_map/near/pallas_call | solution.py:234
  99.0 11.7 %collective-permute-done.7.below.refs_0_ = bf16[4,560,256]{2,1,0:T(8,128)(2,1)S(1)} collective-permute-done((bf16[4,560,256]{2,1,0:T(8,128)(2,1)}, bf16[4,560,256]{2,1,0:T(8,128)(2,1)S(1)}, u32[]{:S(2)}, u32[]{:S(2)}) %collective-permute-start.7) | collective-permute-done | bytes 1146912 | tf_op jit(solution)/shard_map/ppermute | solution.py:492
  110.8 1.0 copy-done.12
  112.8 2.1 %cut.1 = (bf16[2,560,256]{2,1,0:T(8,128)(2,1)}, bf16[2,560,256]{2,1,0:T(8,128)(2,1)}) custom-call(bf16[4,560,256]{2,1,0:T(8,128)(2,1)} %copy-done.12, bf16[4,560,256]{2,1,0:T(8,128)(2,1)} %copy-done.13), custom_call_target="tpu_custom_call" | custom-call | tf_op jit(solution)/shard_map/cut/pallas_call | solution.py:264
  114.9 1.9 %collective-permute-start.10 = (bf16[2,560,256]{2,1,0:T(8,128)(2,1)}, bf16[2,560,256]{2,1,0:T(8,128)(2,1)S(1)}, u32[]{:S(2)}, u32[]{:S(2)}) collective-permute-start(bf16[2,560,256]{2,1,0:T(8,128)(2,1)} %get-tuple-element.69), channel_id=1, source_target_pairs={{0,28},{4,0},{8,4},{12,8},{16,12},{20,16},{24,20},{28,24},{1,29},{... | collective-permute-start | bytes 1720328 | tf_op jit(solution)/shard_map/ppermute | solution.py:498
  116.9 1.2 convolution_convert_fusion
  118.1 8.1 %all-to-all-start.2 = ((bf16[32,16,256]{2,1,0:T(8,128)(2,1)}), bf16[32,16,256]{2,1,0:T(8,128)(2,1)S(1)}, u32[]{:S(2)}, u32[]{:S(2)}) async-start(bf16[32,16,256]{2,1,0:T(8,128)(2,1)} %bitcast.12), calls=%async_computation.2 | async-start | bytes 524288 | tf_op jit(solution)/shard_map/all_to_all | solution.py:441
  126.2 9.4 %near.8.refs_2_ = f32[65,32,256]{2,1,0:T(8,128)} custom-call(f32[1]{0:T(128)} %bitcast.1.scale_ref, s32[5]{0:T(128)} %copy-done.4, s32[5,128]{1,0:T(8,128)} %fusion.66.lst, bf16[4,560,256]{2,1,0:T(8,128)(2,1)} %copy-done.12, bf16[4,560,256]{2,1,0:T(8,128)(2,1)} %copy-done.13, f32[65,32,256]{2,1,0:T(8,128)} %near.7.refs_2_, ...), custom_call_target="tpu_custom_call" | custom-call | flops 2415919104 | bytes 4194304 | tf_op jit(solution)/shard_map/near/pallas_call | solution.py:234
  135.5 3.2 %all-to-all-done.2 = bf16[32,16,256]{2,1,0:T(8,128)(2,1)S(1)} async-done(((bf16[32,16,256]{2,1,0:T(8,128)(2,1)}), bf16[32,16,256]{2,1,0:T(8,128)(2,1)S(1)}, u32[]{:S(2)}, u32[]{:S(2)}) %all-to-all-start.2) | async-done | bytes 262176 | tf_op jit(solution)/shard_map/all_to_all | solution.py:441
  139.1 1.6 copy-done.10
  140.7 1.0 copy-done.11
  141.8 5.9 %near.9 = (bf16[512,256]{1,0:T(8,128)(2,1)S(1)}, bf16[512,256]{1,0:T(8,128)(2,1)}, bf16[512,256]{1,0:T(8,128)(2,1)}, bf16[512,256]{1,0:T(8,128)(2,1)S(1)}) custom-call(f32[1]{0:T(128)} %bitcast.1.scale_ref, s32[5]{0:T(128)S(1)} %copy-done.5, s32[5,128]{1,0:T(8,128)S(1)} %copy-done.3, bf16[2,560,256]{2,1,0:T(8,128)(2,1)S(1)} %collective-permute-done.9.refs_0_, ...), custom_call_target="tpu_custom_call" | custom-call | flops 1207959552 | bytes 4194304 | tf_op jit(solution)/shard_map/near/pallas_call | solution.py:234
  148.5 2.6 %collective-permute-start.12 = (bf16[512,256]{1,0:T(8,128)(2,1)}, bf16[512,256]{1,0:T(8,128)(2,1)S(1)}, u32[]{:S(2)}, u32[]{:S(2)}) collective-permute-start(bf16[512,256]{1,0:T(8,128)(2,1)} %get-tuple-element.87), channel_id=1, source_target_pairs={{0,2},{1,3},{2,0},{3,1},{4,6},{5,7},{6,4},{7,5},{8,10},{9,11},{10,... | collective-permute-start | bytes 786440 | tf_op jit(solution)/shard_map/ppermute | solution.py:507
  151.6 8.1 %home.1.home_ref = f32[4096,128]{1,0:T(8,128)S(1)} custom-call(s32[1]{0:T(128)} %bitcast.y_ref, f32[4]{0:T(128)S(1)} %get-tuple-element.98.scale_ref, bf16[560,256]{1,0:T(8,128)(2,1)S(1)} %copy-done.2, bf16[560,256]{1,0:T(8,128)(2,1)S(1)} %copy-done.6, bf16[560,256]{1,0:T(8,128)(2,1)S(1)} %copy-done.7, bf16[560,256]{1,0:T(8,128)(2,1)S(1)} %copy-done.8, ...), custom_call_target="tpu_custom_call" | custom-call | flops 2147483648 | bytes 3145728 | tf_op jit(solution)/shard_map/home/pallas_call | solution.py:348
  159.7 2.6 %collective-permute-done.13.n3 = bf16[512,256]{1,0:T(8,128)(2,1)S(1)} collective-permute-done((bf16[512,256]{1,0:T(8,128)(2,1)S(1)}, bf16[512,256]{1,0:T(8,128)(2,1)S(1)}, u32[]{:S(2)}, u32[]{:S(2)}) %collective-permute-start.13) | collective-permute-done | bytes 262176 | tf_op jit(solution)/shard_map/ppermute | solution.py:507
  162.3 2.2 %final.1 = bf16[4096,128]{1,0:T(8,128)(2,1)} custom-call(s32[1]{0:T(128)} %bitcast.y_ref, f32[4096,128]{1,0:T(8,128)S(1)} %home.1.home_ref, bf16[512,256]{1,0:T(8,128)(2,1)S(1)} %get-tuple-element.85.n0, bf16[512,256]{1,0:T(8,128)(2,1)S(1)} %collective-permute-done.11.n1, bf16[512,256]{1,0:T(8,128)(2,1)S(1)} %collective-permute-done.12.n2, ...), custom_call_target="tpu_custom_call" | custom-call | tf_op jit(solution)/shard_map/final/pallas_call | solution.py:380
  (92 shorter events, 11.4 us)
Async XLA Ops:
  0.0 35.9 %copy-start = (bf16[128,128]{1,0:T(8,128)(2,1)S(1)}, bf16[128,128]{1,0:T(8,128)(2,1)}, u32[]{:S(2)}) copy-start(bf16[128,128]{1,0:T(8,128)(2,1)} %param.22) | copy-start | bytes 98308
  0.0 20.5 %copy-start.17 = (s32[2,1024]{1,0:T(2,128)S(1)}, s32[2,1024]{1,0:T(2,128)}, u32[]{:S(2)}) copy-start(s32[2,1024]{1,0:T(2,128)} %param.16) | copy-start | bytes 24580
  3.1 19.4 %copy-start.2 = (bf16[560,256]{1,0:T(8,128)(2,1)S(1)}, bf16[560,256]{1,0:T(8,128)(2,1)}, u32[]{:S(2)}) copy-start(bf16[560,256]{1,0:T(8,128)(2,1)} %get-tuple-element.80.refs_0_.v0.x_ref.y_row.z_ref) | copy-start | bytes 860164
  3.1 19.4 %collective-permute-start = (bf16[560,256]{1,0:T(8,128)(2,1)}, bf16[560,256]{1,0:T(8,128)(2,1)S(1)}, u32[]{:S(2)}, u32[]{:S(2)}) collective-permute-start(bf16[560,256]{1,0:T(8,128)(2,1)} %get-tuple-element.81.v1), channel_id=1, source_target_pairs={{0,1},{1,2},{2,3},{3,0},{4,5},{5,6},{6,7},{7,4},{8,9},{9,10},{10,1... | collective-permute-start | bytes 860168 | tf_op jit(solution)/shard_map/ppermute | solution.py:467
  4.7 17.8 %collective-permute-start.1 = (bf16[560,256]{1,0:T(8,128)(2,1)}, bf16[560,256]{1,0:T(8,128)(2,1)S(1)}, u32[]{:S(2)}, u32[]{:S(2)}) collective-permute-start(bf16[560,256]{1,0:T(8,128)(2,1)} %get-tuple-element.82.v2), channel_id=1, source_target_pairs={{0,2},{1,3},{2,0},{3,1},{4,6},{5,7},{6,4},{7,5},{8,10},{9,11},{10,... | collective-permute-start | bytes 860168 | tf_op jit(solution)/shard_map/ppermute | solution.py:467
  7.6 14.9 %collective-permute-start.2 = (bf16[560,256]{1,0:T(8,128)(2,1)}, bf16[560,256]{1,0:T(8,128)(2,1)S(1)}, u32[]{:S(2)}, u32[]{:S(2)}) collective-permute-start(bf16[560,256]{1,0:T(8,128)(2,1)} %get-tuple-element.83.v3), channel_id=1, source_target_pairs={{0,3},{1,0},{2,1},{3,2},{4,7},{5,4},{6,5},{7,6},{8,11},{9,8},{10,9... | collective-permute-start | bytes 860168 | tf_op jit(solution)/shard_map/ppermute | solution.py:467
  10.7 16.3 %copy-start.19 = (f32[4]{0:T(128)S(1)}, f32[4]{0:T(128)}, u32[]{:S(2)}) copy-start(f32[4]{0:T(128)} %param.19) | copy-start | bytes 52
  11.5 23.8 %all-to-all-start = ((bf16[32,40,128]{2,1,0:T(8,128)(2,1)}), bf16[32,40,128]{2,1,0:T(8,128)(2,1)S(1)}, u32[]{:S(2)}, u32[]{:S(2)}) async-start(bf16[32,40,128]{2,1,0:T(8,128)(2,1)} %copy.29), calls=%async_computation | async-start | bytes 655360 | tf_op jit(solution)/shard_map/all_to_all | solution.py:410
  21.1 15.0 %copy-start.4 = (s32[5]{0:T(128)}, s32[5]{0:T(128)S(1)}, u32[]{:S(2)}) copy-start(s32[5]{0:T(128)S(1)} %get-tuple-element.51.cnt) | copy-start | bytes 64
  22.6 13.5 %copy-start.1 = (bf16[4,560,256]{2,1,0:T(8,128)(2,1)}, bf16[4,560,256]{2,1,0:T(8,128)(2,1)S(1)}, u32[]{:S(2)}) copy-start(bf16[4,560,256]{2,1,0:T(8,128)(2,1)S(1)} %pack.1.refs_0_) | copy-start | bytes 3440644
  22.6 32.2 %collective-permute-start.3 = (bf16[4,560,256]{2,1,0:T(8,128)(2,1)S(1)}, bf16[4,560,256]{2,1,0:T(8,128)(2,1)}, u32[]{:S(2)}, u32[]{:S(2)}) collective-permute-start(bf16[4,560,256]{2,1,0:T(8,128)(2,1)S(1)} %pack.1.refs_0_), channel_id=1, source_target_pairs={{0,4},{4,8},{8,12},{12,16},{16,20},{20,24},{24,28},{28,0},{1,5},{5... | collective-permute-start | bytes 3440648 | tf_op jit(solution)/shard_map/ppermute | solution.py:478
  24.5 30.3 %collective-permute-start.4 = (bf16[4,560,256]{2,1,0:T(8,128)(2,1)S(1)}, bf16[4,560,256]{2,1,0:T(8,128)(2,1)}, u32[]{:S(2)}, u32[]{:S(2)}) collective-permute-start(bf16[4,560,256]{2,1,0:T(8,128)(2,1)S(1)} %pack.1.refs_0_), channel_id=1, source_target_pairs={{0,28},{4,0},{8,4},{12,8},{16,12},{20,16},{24,20},{28,24},{1,29},{... | collective-permute-start | bytes 3440648 | tf_op jit(solution)/shard_map/ppermute | solution.py:479
  54.8 28.0 %collective-permute-start.5 = (bf16[4,560,256]{2,1,0:T(8,128)(2,1)}, bf16[4,560,256]{2,1,0:T(8,128)(2,1)}, u32[]{:S(2)}, u32[]{:S(2)}) collective-permute-start(bf16[4,560,256]{2,1,0:T(8,128)(2,1)} %collective-permute-done.3.refs_0_), channel_id=1, source_target_pairs={{0,4},{4,8},{8,12},{12,16},{16,20},{20,24},{24,28},{28,0},{1,5},{5... | collective-permute-start | bytes 3440648 | tf_op jit(solution)/shard_map/ppermute | solution.py:485
  54.8 27.9 %collective-permute-start.6 = (bf16[4,560,256]{2,1,0:T(8,128)(2,1)}, bf16[4,560,256]{2,1,0:T(8,128)(2,1)S(1)}, u32[]{:S(2)}, u32[]{:S(2)}) collective-permute-start(bf16[4,560,256]{2,1,0:T(8,128)(2,1)} %collective-permute-done.4.refs_1_), channel_id=1, source_target_pairs={{0,28},{4,0},{8,4},{12,8},{16,12},{20,16},{24,20},{28,24},{1,29},{... | collective-permute-start | bytes 3440648 | tf_op jit(solution)/shard_map/ppermute | solution.py:486
  58.6 15.6 %all-to-all-start.1 = ((bf16[8,8,256]{2,1,0:T(8,128)(2,1)}), bf16[8,8,256]{2,1,0:T(8,128)(2,1)S(1)}, u32[]{:S(2)}, u32[]{:S(2)}) async-start(bf16[8,8,256]{2,1,0:T(8,128)(2,1)} %broadcast_in_dim.90), calls=%async_computation.1 | async-start | bytes 65536 | tf_op jit(solution)/shard_map/all_to_all | solution.py:394
  63.4 23.6 %copy-start.14 = (bf16[128,128]{1,0:T(8,128)(2,1)S(1)}, bf16[128,128]{1,0:T(8,128)(2,1)}, u32[]{:S(2)}) copy-start(bf16[128,128]{1,0:T(8,128)(2,1)} %param.24) | copy-start | bytes 98308
  63.4 24.6 %copy-start.16 = (bf16[128,128]{1,0:T(8,128)(2,1)S(1)}, bf16[128,128]{1,0:T(8,128)(2,1)}, u32[]{:S(2)}) copy-start(bf16[128,128]{1,0:T(8,128)(2,1)} %param.23) | copy-start | bytes 98308
  83.8 27.0 %collective-permute-start.7 = (bf16[4,560,256]{2,1,0:T(8,128)(2,1)}, bf16[4,560,256]{2,1,0:T(8,128)(2,1)S(1)}, u32[]{:S(2)}, u32[]{:S(2)}) collective-permute-start(bf16[4,560,256]{2,1,0:T(8,128)(2,1)} %collective-permute-done.5.refs_0_), channel_id=1, source_target_pairs={{0,4},{4,8},{8,12},{12,16},{16,20},{20,24},{24,28},{28,0},{1,5},{5... | collective-permute-start | bytes 3440648 | tf_op jit(solution)/shard_map/ppermute | solution.py:492
  84.5 26.3 %collective-permute-start.8 = (bf16[4,560,256]{2,1,0:T(8,128)(2,1)}, bf16[4,560,256]{2,1,0:T(8,128)(2,1)S(1)}, u32[]{:S(2)}, u32[]{:S(2)}) collective-permute-start(bf16[4,560,256]{2,1,0:T(8,128)(2,1)} %copy-done.20), channel_id=1, source_target_pairs={{0,28},{4,0},{8,4},{12,8},{16,12},{20,16},{24,20},{28,24},{1,29},{... | collective-permute-start | bytes 3440648 | tf_op jit(solution)/shard_map/ppermute | solution.py:493
  114.9 23.9 %collective-permute-start.10 = (bf16[2,560,256]{2,1,0:T(8,128)(2,1)}, bf16[2,560,256]{2,1,0:T(8,128)(2,1)S(1)}, u32[]{:S(2)}, u32[]{:S(2)}) collective-permute-start(bf16[2,560,256]{2,1,0:T(8,128)(2,1)} %get-tuple-element.69), channel_id=1, source_target_pairs={{0,28},{4,0},{8,4},{12,8},{16,12},{20,16},{24,20},{28,24},{1,29},{... | collective-permute-start | bytes 1720328 | tf_op jit(solution)/shard_map/ppermute | solution.py:498
  116.8 22.0 %collective-permute-start.9 = (bf16[2,560,256]{2,1,0:T(8,128)(2,1)}, bf16[2,560,256]{2,1,0:T(8,128)(2,1)S(1)}, u32[]{:S(2)}, u32[]{:S(2)}) collective-permute-start(bf16[2,560,256]{2,1,0:T(8,128)(2,1)} %get-tuple-element.68), channel_id=1, source_target_pairs={{0,4},{4,8},{8,12},{12,16},{16,20},{20,24},{24,28},{28,0},{1,5},{5... | collective-permute-start | bytes 1720328 | tf_op jit(solution)/shard_map/ppermute | solution.py:497
  118.1 20.7 %all-to-all-start.2 = ((bf16[32,16,256]{2,1,0:T(8,128)(2,1)}), bf16[32,16,256]{2,1,0:T(8,128)(2,1)S(1)}, u32[]{:S(2)}, u32[]{:S(2)}) async-start(bf16[32,16,256]{2,1,0:T(8,128)(2,1)} %bitcast.12), calls=%async_computation.2 | async-start | bytes 524288 | tf_op jit(solution)/shard_map/all_to_all | solution.py:441
  126.1 12.9 %copy-start.3 = (s32[5,128]{1,0:T(8,128)S(1)}, s32[5,128]{1,0:T(8,128)}, u32[]{:S(2)}) copy-start(s32[5,128]{1,0:T(8,128)} %fusion.66.lst) | copy-start | bytes 7684
  126.2 12.9 %copy-start.5 = (s32[5]{0:T(128)S(1)}, s32[5]{0:T(128)}, u32[]{:S(2)}) copy-start(s32[5]{0:T(128)} %copy-done.4) | copy-start | bytes 64
  141.8 9.6 %copy-start.15 = (bf16[256,64]{0,1:T(8,128)(2,1)S(1)}, bf16[256,64]{0,1:T(8,128)(2,1)}, u32[]{:S(2)}) copy-start(bf16[256,64]{0,1:T(8,128)(2,1)} %param.26) | copy-start | bytes 98308
  141.8 9.8 %copy-start.6 = (bf16[560,256]{1,0:T(8,128)(2,1)S(1)}, bf16[560,256]{1,0:T(8,128)(2,1)}, u32[]{:S(2)}) copy-start(bf16[560,256]{1,0:T(8,128)(2,1)} %get-tuple-element.81.v1) | copy-start | bytes 860164
  141.8 9.8 %copy-start.7 = (bf16[560,256]{1,0:T(8,128)(2,1)S(1)}, bf16[560,256]{1,0:T(8,128)(2,1)}, u32[]{:S(2)}) copy-start(bf16[560,256]{1,0:T(8,128)(2,1)} %get-tuple-element.82.v2) | copy-start | bytes 860164
  141.8 9.8 %copy-start.8 = (bf16[560,256]{1,0:T(8,128)(2,1)S(1)}, bf16[560,256]{1,0:T(8,128)(2,1)}, u32[]{:S(2)}) copy-start(bf16[560,256]{1,0:T(8,128)(2,1)} %get-tuple-element.83.v3) | copy-start | bytes 860164
  141.8 9.8 %copy-start.9 = (bf16[128,128]{1,0:T(8,128)(2,1)S(1)}, bf16[128,128]{1,0:T(8,128)(2,1)}, u32[]{:S(2)}) copy-start(bf16[128,128]{1,0:T(8,128)(2,1)} %wo_ref.1) | copy-start | bytes 98308
  147.6 12.0 %collective-permute-start.11 = (bf16[512,256]{1,0:T(8,128)(2,1)}, bf16[512,256]{1,0:T(8,128)(2,1)S(1)}, u32[]{:S(2)}, u32[]{:S(2)}) collective-permute-start(bf16[512,256]{1,0:T(8,128)(2,1)} %get-tuple-element.86), channel_id=1, source_target_pairs={{0,3},{1,0},{2,1},{3,2},{4,7},{5,4},{6,5},{7,6},{8,11},{9,8},{10,9... | collective-permute-start | bytes 786440 | tf_op jit(solution)/shard_map/ppermute | solution.py:507
  148.5 11.2 %collective-permute-start.12 = (bf16[512,256]{1,0:T(8,128)(2,1)}, bf16[512,256]{1,0:T(8,128)(2,1)S(1)}, u32[]{:S(2)}, u32[]{:S(2)}) collective-permute-start(bf16[512,256]{1,0:T(8,128)(2,1)} %get-tuple-element.87), channel_id=1, source_target_pairs={{0,2},{1,3},{2,0},{3,1},{4,6},{5,7},{6,4},{7,5},{8,10},{9,11},{10,... | collective-permute-start | bytes 786440 | tf_op jit(solution)/shard_map/ppermute | solution.py:507
  151.1 11.2 %collective-permute-start.13 = (bf16[512,256]{1,0:T(8,128)(2,1)S(1)}, bf16[512,256]{1,0:T(8,128)(2,1)S(1)}, u32[]{:S(2)}, u32[]{:S(2)}) collective-permute-start(bf16[512,256]{1,0:T(8,128)(2,1)S(1)} %get-tuple-element.88), channel_id=1, source_target_pairs={{0,1},{1,2},{2,3},{3,0},{4,5},{5,6},{6,7},{7,4},{8,9},{9,10},{10,1... | collective-permute-start | bytes 786440 | tf_op jit(solution)/shard_map/ppermute | solution.py:507
  (6 other events, 13.7 us)
where the time goes:
time: 167 us; the launch traced here: 164 us
  Pallas kernels  60.2 us (36%)
  waiting for transfers between devices  44.5 us (27%)
  starting transfers between devices  44.2 us (26%)
  local copies, waits for them, and re-layouts  8.99 us (5%)
  other arithmetic  3.23 us (2%)
  matrix products  2.84 us (2%)
    pallas_call x5, Pallas kernels, near_step(): pl.pallas_call(functools.partial(near_kernel, number, lengths, first, las...  44.7 us
    ppermute x2, waiting for transfers between devices, per_device(): below_next = lax.ppermute(below, 'dev_0', up)  20.3 us
    ppermute x1, waiting for transfers between devices, per_device(): below = lax.ppermute(held, 'dev_0', up)  10.6 us
    all_to_all x1, starting transfers between devices, spread_summaries(): return lax.all_to_all(sent, DEV, 0, 0, tiled=True)  8.96 us
    pallas_call x1, Pallas kernels, home(): pl.pallas_call(home_kernel, grid=(BLK // 4,), in_specs=[smem(), smem()] +...  8.1 us
    all_to_all x1, starting transfers between devices, far_down(): lax.all_to_all(down.reshape(-1, BLK, down.shape[1]), DEV, 0, 0, tiled=True)  8.07 us
    all_to_all x1, waiting for transfers between devices, spread_summaries(): return lax.all_to_all(sent, DEV, 0, 0, tiled=True)  7.74 us
    unnamed x43, local copies, waits for them, and re-layouts  5.89 us
  transfers between devices with their start and end apart: 17, of which 6 were waited for; matrix products, arithmetic and copies ran while one was open for 5% of the time, Pallas kernels for 29%

commit v1 on v0

--- a/solution.py
+++ b/solution.py
@@ -16,6 +16,7 @@
 BF16 = jnp.bfloat16
 ROWS = 8
 COLS = 4
+HALF = COLS // 2
 BLK = 16
 RBLK = BLK * COLS
 B = 256
@@ -74,14 +75,14 @@
 
 
 def pack_kernel(*refs):
-    for s in range(COLS):
-        refs[COLS][s] = refs[s][...]
+    for s in range(HALF):
+        refs[HALF][s] = refs[s][...]
 
 
 def pack(messages):
     return pl.pallas_call(
         pack_kernel,
-        out_shape=jax.ShapeDtypeStruct((COLS, MROWS, B), BF16),
+        out_shape=jax.ShapeDtypeStruct((HALF, MROWS, B), BF16),
         compiler_params=params(VMEM_SMALL),
         name="pack",
     )(*messages)
@@ -162,8 +163,8 @@
     late = []
     if not first:
         acc_in, dst_in = refs[n : n + 2]
-        late.append(pltpu.make_async_copy(acc_in, acc, sem.at[2]))
-        late.append(pltpu.make_async_copy(dst_in, dst_ref, sem.at[3]))
+        late.append(pltpu.make_async_copy(acc_in, acc, sem.at[COLS]))
+        late.append(pltpu.make_async_copy(dst_in, dst_ref, sem.at[COLS + 1]))
     for move in moves + late:
         move.start()
     if first:
@@ -241,7 +242,7 @@
             pltpu.VMEM((sum(lengths), MROWS, B), BF16),
             pltpu.VMEM((sum(lengths) * BLK, AUG, B), BF16),
             pltpu.VMEM(dst_shape, BF16),
-            pltpu.SemaphoreType.DMA((4,)),
+            pltpu.SemaphoreType.DMA((COLS + 2,)),
             pltpu.SemaphoreType.DMA((COLS,)),
         ],
         compiler_params=params(VMEM_SMALL if last else VMEM_LIMIT),
@@ -250,29 +251,6 @@
         ),
         name="near",
     )(*args)
-
-
-def cut_kernel(below, above, low, high):
-    low[...] = below[...]
-    high[...] = above[...]
-
-
-def cut_halves(below, above):
-    half = COLS // 2
-    block = (1, MROWS, B)
-    shape = jax.ShapeDtypeStruct((half, MROWS, B), BF16)
-    return pl.pallas_call(
-        cut_kernel,
-        grid=(half,),
-        in_specs=[
-            pl.BlockSpec(block, lambda i: (i, 0, 0)),
-            pl.BlockSpec(block, lambda i: (half + i, 0, 0)),
-        ],
-        out_specs=[pl.BlockSpec(block, lambda i: (i, 0, 0))] * 2,
-        out_shape=[shape] * 2,
-        compiler_params=params(),
-        name="cut",
-    )(below, above)
 
 
 def side_lists(near_pairs, z, y):
@@ -441,6 +419,13 @@
     return lax.all_to_all(down.reshape(-1, BLK, down.shape[1]), DEV, 0, 0, tiled=True)
 
 
+def after(rows, acc, extra):
+    (below_a, below_b), (above_a, above_b) = rows
+    below_a, above_a, acc, extra = lax.optimization_barrier((below_a, above_a, acc, extra))
+    below_b, above_b, acc = lax.optimization_barrier((below_b, above_b, acc))
+    return ([below_a, below_b], [above_a, above_b]), acc, extra
+
+
 def per_device(
     features,
     coords,
@@ -463,41 +448,38 @@
     messages, level_one = prep(y_one, features, coords, w_near, restrict)
     ahead = [[(i, (i + s) % COLS) for i in range(COLS)] for s in range(COLS)]
     back_to = [[(i, (i - s) % COLS) for i in range(COLS)] for s in range(COLS)]
-    pieces_in = [messages[0]]
-    pieces_in += [lax.ppermute(messages[s], "dev_1", ahead[s]) for s in range(1, COLS)]
-    arrived = spread_summaries(level_one, parent_two)
-    held = pack(pieces_in)
+    slots = [messages[0]]
+    slots += [lax.ppermute(messages[s], "dev_1", ahead[s]) for s in range(1, COLS)]
+    held = [pack(slots[:HALF]), pack(slots[HALF:])]
     scales = rates * math.log2(math.e)
     scale = jnp.sum(jnp.where(jnp.arange(COLS) == y, scales, 0.0)).reshape(1)
     cnt, lst = side_lists(near_pairs, z, y)
-    held, cnt, lst = lax.optimization_barrier((held, cnt, lst))
+    arrived = spread_summaries(level_one, parent_two)
 
     up = [(i, (i + 1) % ROWS) for i in range(ROWS)]
     down = [(i, (i - 1) % ROWS) for i in range(ROWS)]
     step = functools.partial(near_step, scale, cnt, lst)
-    below = lax.ppermute(held, "dev_0", up)
-    above = lax.ppermute(held, "dev_0", down)
-    held, arrived = lax.optimization_barrier((held, arrived))
-    acc, dst_aug = step(0, [held])
+
+    def onward(below, above):
+        below = [lax.ppermute(half, "dev_0", up) for half in below]
+        return below, [lax.ppermute(half, "dev_0", down) for half in above]
+
+    rows_one = onward(held, held)
+    acc, dst_aug = step(0, held)
+    rows_one, acc, arrived = after(rows_one, acc, arrived)
     parents, level_two, level_three = far_up(arrived, parent_three, w_two)
-    below, above, acc, level_three = lax.optimization_barrier((below, above, acc, level_three))
     three_all = copies(level_three, "group").reshape(-1, level_three.shape[1])
-    below_next = lax.ppermute(below, "dev_0", up)
-    above_next = lax.ppermute(above, "dev_0", down)
-    (acc,) = step(1, [below, above], (acc, dst_aug))
-    below, above, acc, three_all = lax.optimization_barrier(
-        (below_next, above_next, acc, three_all)
-    )
+    rows_two = onward(*rows_one)
+    (acc,) = step(1, [*rows_one[0], *rows_one[1]], (acc, dst_aug))
+    rows_two, acc, three_all = after(rows_two, acc, three_all)
     back = far_down(parents, level_two, three_all, parent_three, w_three, w_four, coupling)
-    below_next = lax.ppermute(below, "dev_0", up)
-    above_next = lax.ppermute(above, "dev_0", down)
-    (acc,) = step(2, [below, above], (acc, dst_aug))
-    below, above, acc = lax.optimization_barrier((below_next, above_next, acc))
-    low, high = cut_halves(below, above)
-    low = lax.ppermute(low, "dev_0", up)
-    high = lax.ppermute(high, "dev_0", down)
-    (acc,) = step(3, [below, above], (acc, dst_aug))
-    low, high, acc, back = lax.optimization_barrier((low, high, acc, back))
+    rows_three = onward(*rows_two)
+    (acc,) = step(2, [*rows_two[0], *rows_two[1]], (acc, dst_aug))
+    rows_three, acc, _ = after(rows_three, acc, acc)
+    low = lax.ppermute(rows_three[0][0], "dev_0", up)
+    high = lax.ppermute(rows_three[1][1], "dev_0", down)
+    acc, back = lax.optimization_barrier((acc, back))
+    (acc,) = step(3, [*rows_three[0], *rows_three[1]], (acc, dst_aug))
     near = step(4, [low, high], (acc, dst_aug), last=True)
     parent_down = back.reshape(ROWS * COLS, BLK, 2, -1).transpose(1, 0, 2, 3)
     parent_down = parent_down.reshape(BLK, 2 * ROWS * COLS, -1)

time: 167 us -> 156 us (0.934)
  waiting for transfers between devices: 44.5 us -> 27 us
  starting transfers between devices: 44.2 us -> 53.2 us
  local copies, waits for them, and re-layouts: 8.99 us -> 5.78 us
    ppermute x8 -> x14, waiting for transfers between devices: 30.9 us -> 21.3 us  [the longest x6 21.3 us: onward(): below = [lax.ppermute(half, 'dev_0', up) for half in below]]
    ppermute x8 -> x14, starting transfers between devices: 12.9 us -> 20.6 us  [the longest x6 15.1 us: onward(): return (below, [lax.ppermute(half, 'dev_0', down) for half in above])]
    all_to_all x1, waiting for transfers between devices: 7.74 us -> 0.01 us  [spread_summaries(): return lax.all_to_all(sent, DEV, 0, 0, tiled=True)]
    unnamed x43 -> x49, local copies, waits for them, and re-layouts: 5.89 us -> 2.67 us
    pallas_call x5, Pallas kernels: 44.7 us -> 47.5 us  [near_step(): pl.pallas_call(functools.partial(near_kernel, number, lengths, first, las...]
    pallas_call x2, Pallas kernels: 2.15 us -> 0.08 us  [pack(): pl.pallas_call(pack_kernel, out_shape=jax.ShapeDtypeStruct((HALF, MROWS,...]
  transfers between devices with their start and end apart: 17 -> 23, of which waited for: 6 -> 7; matrix products, arithmetic and copies ran while one was open for 5% -> 6% of each run, Pallas kernels for 29% -> 32%
where the time goes in v1:
time: 156 us; the launch traced here: 153 us
  Pallas kernels  60.9 us (39%)
  starting transfers between devices  53.2 us (34%)
  waiting for transfers between devices  27 us (17%)
  local copies, waits for them, and re-layouts  5.78 us (4%)
  other arithmetic  3.16 us (2%)
  matrix products  2.85 us (2%)
    pallas_call x5, Pallas kernels, near_step(): pl.pallas_call(functools.partial(near_kernel, number, lengths, first, las...  47.5 us
    ppermute x6, waiting for transfers between devices, onward(): below = [lax.ppermute(half, 'dev_0', up) for half in below]  21.3 us
    ppermute x6, starting transfers between devices, onward(): return (below, [lax.ppermute(half, 'dev_0', down) for half in above])  15.1 us
    all_to_all x1, starting transfers between devices, spread_summaries(): return lax.all_to_all(sent, DEV, 0, 0, tiled=True)  10.6 us
    pallas_call x1, Pallas kernels, home(): pl.pallas_call(home_kernel, grid=(BLK // 4,), in_specs=[smem(), smem()] +...  8.08 us
    all_to_all x1, starting transfers between devices, far_down(): lax.all_to_all(down.reshape(-1, BLK, down.shape[1]), DEV, 0, 0, tiled=True)  7.94 us
    ppermute x3, starting transfers between devices, per_device(): lax.ppermute(messages[s], 'dev_1', ahead[s])  5.22 us
    all_to_all x1, starting transfers between devices, copies(): return lax.all_to_all(sent, axis, 0, 0, tiled=True)  4.78 us
  transfers between devices with their start and end apart: 23, of which 7 were waited for; matrix products, arithmetic and copies ran while one was open for 6% of the time, Pallas kernels for 32%

profile of v1, /device:TPU:6, one launch (start us, length us, event | category | flops | bytes accessed | tf_op | source)
XLA Modules:
  0.0 153.4 jit_solution(8367397234715959072)
XLA Ops:
  0.0 3.1 %prep.1 = (bf16[560,256]{1,0:T(8,128)(2,1)}, bf16[560,256]{1,0:T(8,128)(2,1)}, bf16[560,256]{1,0:T(8,128)(2,1)}, bf16[560,256]{1,0:T(8,128)(2,1)}, bf16[16,64,128]{2,1,0:T(8,128)(2,1)}) custom-call(s32[1]{0:T(128)} %bitcast.y_ref, bf16[4096,128]{1,0:T(8,128)(2,1)} %f_ref.1, bf16[3,4096]{1,0:T(4,128)(2,1)} %xyz_ref.1, bf16[128,128]{1,0:T(8,128)(2,1)} %wn_ref.1, ...), custom_call_target="tpu_custom_call" | custom-call | tf_op jit(solution)/shard_map/prep/pallas_call | solution.py:66
  3.1 3.2 %collective-permute-start.3 = (bf16[560,256]{1,0:T(8,128)(2,1)}, bf16[560,256]{1,0:T(8,128)(2,1)S(1)}, u32[]{:S(2)}, u32[]{:S(2)}) collective-permute-start(bf16[560,256]{1,0:T(8,128)(2,1)} %get-tuple-element.82.v2), channel_id=1, source_target_pairs={{0,2},{1,3},{2,0},{3,1},{4,6},{5,7},{6,4},{7,5},{8,10},{9,11},{10,... | collective-permute-start | bytes 860168 | tf_op jit(solution)/shard_map/ppermute | solution.py:452
  6.3 1.1 collective-permute-start.4
  8.3 1.0 copy.28
  10.9 10.6 %all-to-all-start = ((bf16[32,40,128]{2,1,0:T(8,128)(2,1)}), bf16[32,40,128]{2,1,0:T(8,128)(2,1)S(1)}, u32[]{:S(2)}, u32[]{:S(2)}) async-start(bf16[32,40,128]{2,1,0:T(8,128)(2,1)} %copy.29), calls=%async_computation | async-start | bytes 655360 | tf_op jit(solution)/shard_map/all_to_all | solution.py:388
  22.2 1.9 %collective-permute-start.1 = (bf16[2,560,256]{2,1,0:T(8,128)(2,1)S(1)}, bf16[2,560,256]{2,1,0:T(8,128)(2,1)S(1)}, u32[]{:S(2)}, u32[]{:S(2)}) collective-permute-start(bf16[2,560,256]{2,1,0:T(8,128)(2,1)S(1)} %pack.2.refs_0_), channel_id=1, source_target_pairs={{0,4},{4,8},{8,12},{12,16},{16,20},{20,24},{24,28},{28,0},{1,5},{5... | collective-permute-start | bytes 1720328 | tf_op jit(solution)/shard_map/ppermute | solution.py:464
  24.0 1.6 %collective-permute-start.2 = (bf16[2,560,256]{2,1,0:T(8,128)(2,1)S(1)}, bf16[2,560,256]{2,1,0:T(8,128)(2,1)S(1)}, u32[]{:S(2)}, u32[]{:S(2)}) collective-permute-start(bf16[2,560,256]{2,1,0:T(8,128)(2,1)S(1)} %pack.2.refs_0_), channel_id=1, source_target_pairs={{0,28},{4,0},{8,4},{12,8},{16,12},{20,16},{24,20},{28,24},{1,29},{... | collective-permute-start | bytes 1720328 | tf_op jit(solution)/shard_map/ppermute | solution.py:465
  28.2 2.8 %collective-permute-start.8 = (bf16[2,560,256]{2,1,0:T(8,128)(2,1)S(1)}, bf16[2,560,256]{2,1,0:T(8,128)(2,1)}, u32[]{:S(2)}, u32[]{:S(2)}) collective-permute-start(bf16[2,560,256]{2,1,0:T(8,128)(2,1)S(1)} %pack.3.refs_1_), channel_id=1, source_target_pairs={{0,28},{4,0},{8,4},{12,8},{16,12},{20,16},{24,20},{28,24},{1,29},{... | collective-permute-start | bytes 1720328 | tf_op jit(solution)/shard_map/ppermute | solution.py:465
  31.0 7.9 %near.5 = (f32[65,32,256]{2,1,0:T(8,128)}, bf16[64,16,256]{2,1,0:T(8,128)(2,1)}) custom-call(f32[1]{0:T(128)} %bitcast.1.scale_ref, s32[5]{0:T(128)} %copy-done.5, s32[5,128]{1,0:T(8,128)} %fusion.66.lst, bf16[2,560,256]{2,1,0:T(8,128)(2,1)} %copy-done.1, bf16[2,560,256]{2,1,0:T(8,128)(2,1)} %copy-done.2), custom_call_target="tpu_custom_call" | custom-call | flops 1207959552 | bytes 4194304 | tf_op jit(solution)/shard_map/near/pallas_call | solution.py:235
  38.9 5.7 %collective-permute-done.1.refs_0_ = bf16[2,560,256]{2,1,0:T(8,128)(2,1)S(1)} collective-permute-done((bf16[2,560,256]{2,1,0:T(8,128)(2,1)S(1)}, bf16[2,560,256]{2,1,0:T(8,128)(2,1)S(1)}, u32[]{:S(2)}, u32[]{:S(2)}) %collective-permute-start.1) | collective-permute-done | bytes 573472 | tf_op jit(solution)/shard_map/ppermute | solution.py:464
  45.6 3.1 %collective-permute-start.6 = (bf16[2,560,256]{2,1,0:T(8,128)(2,1)S(1)}, bf16[2,560,256]{2,1,0:T(8,128)(2,1)}, u32[]{:S(2)}, u32[]{:S(2)}) collective-permute-start(bf16[2,560,256]{2,1,0:T(8,128)(2,1)S(1)} %collective-permute-done.2.refs_2_), channel_id=1, source_target_pairs={{0,28},{4,0},{8,4},{12,8},{16,12},{20,16},{24,20},{28,24},{1,29},{... | collective-permute-start | bytes 1720328 | tf_op jit(solution)/shard_map/ppermute | solution.py:465
  49.5 4.8 %all-to-all-start.1 = ((bf16[8,8,256]{2,1,0:T(8,128)(2,1)}), bf16[8,8,256]{2,1,0:T(8,128)(2,1)S(1)}, u32[]{:S(2)}, u32[]{:S(2)}) async-start(bf16[8,8,256]{2,1,0:T(8,128)(2,1)} %broadcast_in_dim.90), calls=%async_computation.1 | async-start | bytes 65536 | tf_op jit(solution)/shard_map/all_to_all | solution.py:372
  54.2 2.8 %collective-permute-done.7.refs_1_ = bf16[2,560,256]{2,1,0:T(8,128)(2,1)} collective-permute-done((bf16[2,560,256]{2,1,0:T(8,128)(2,1)S(1)}, bf16[2,560,256]{2,1,0:T(8,128)(2,1)}, u32[]{:S(2)}, u32[]{:S(2)}) %collective-permute-start.7) | collective-permute-done | bytes 573472 | tf_op jit(solution)/shard_map/ppermute | solution.py:464
  57.1 3.1 %collective-permute-start.12 = (bf16[2,560,256]{2,1,0:T(8,128)(2,1)}, bf16[2,560,256]{2,1,0:T(8,128)(2,1)}, u32[]{:S(2)}, u32[]{:S(2)}) collective-permute-start(bf16[2,560,256]{2,1,0:T(8,128)(2,1)} %collective-permute-done.8.refs_3_), channel_id=1, source_target_pairs={{0,28},{4,0},{8,4},{12,8},{16,12},{20,16},{24,20},{28,24},{1,29},{... | collective-permute-start | bytes 1720328 | tf_op jit(solution)/shard_map/ppermute | solution.py:465
  60.5 12.1 %near.6.refs_4_ = f32[65,32,256]{2,1,0:T(8,128)} custom-call(f32[1]{0:T(128)} %bitcast.1.scale_ref, s32[5]{0:T(128)} %copy-done.5, s32[5,128]{1,0:T(8,128)} %fusion.66.lst, bf16[2,560,256]{2,1,0:T(8,128)(2,1)} %copy-done.19, bf16[2,560,256]{2,1,0:T(8,128)(2,1)} %collective-permute-done.7.refs_1_, bf16[2,560,256]{2,1,0:T(8,128)(2,1)} %copy-done.20, ...), custom_call_target="tpu_custom_call" | custom-call | flops 2415919104 | bytes 4194304 | tf_op jit(solution)/shard_map/near/pallas_call | solution.py:235
  73.5 6.7 %collective-permute-done.11.refs_1_ = bf16[2,560,256]{2,1,0:T(8,128)(2,1)S(1)} collective-permute-done((bf16[2,560,256]{2,1,0:T(8,128)(2,1)}, bf16[2,560,256]{2,1,0:T(8,128)(2,1)S(1)}, u32[]{:S(2)}, u32[]{:S(2)}) %collective-permute-start.11) | collective-permute-done | bytes 573472 | tf_op jit(solution)/shard_map/ppermute | solution.py:464
  80.2 1.3 collective-permute-start.10
  82.4 3.1 %collective-permute-start.15 = (bf16[2,560,256]{2,1,0:T(8,128)(2,1)}, bf16[2,560,256]{2,1,0:T(8,128)(2,1)}, u32[]{:S(2)}, u32[]{:S(2)}) collective-permute-start(bf16[2,560,256]{2,1,0:T(8,128)(2,1)} %collective-permute-done.12.refs_3_), channel_id=1, source_target_pairs={{0,28},{4,0},{8,4},{12,8},{16,12},{20,16},{24,20},{28,24},{1,29},{... | collective-permute-start | bytes 1720328 | tf_op jit(solution)/shard_map/ppermute | solution.py:465
  85.6 1.2 convolution_convert_fusion
  86.8 7.9 %all-to-all-start.2 = ((bf16[32,16,256]{2,1,0:T(8,128)(2,1)}), bf16[32,16,256]{2,1,0:T(8,128)(2,1)S(1)}, u32[]{:S(2)}, u32[]{:S(2)}) async-start(bf16[32,16,256]{2,1,0:T(8,128)(2,1)} %bitcast.12), calls=%async_computation.2 | async-start | bytes 524288 | tf_op jit(solution)/shard_map/all_to_all | solution.py:419
  94.8 10.8 %near.7.refs_4_ = f32[65,32,256]{2,1,0:T(8,128)} custom-call(f32[1]{0:T(128)} %bitcast.1.scale_ref, s32[5]{0:T(128)} %copy-done.5, s32[5,128]{1,0:T(8,128)} %fusion.66.lst, bf16[2,560,256]{2,1,0:T(8,128)(2,1)} %collective-permute-done.5.refs_0_, bf16[2,560,256]{2,1,0:T(8,128)(2,1)} %copy-done.21, bf16[2,560,256]{2,1,0:T(8,128)(2,1)} %collective-permute-done.6.refs_2_, ...), custom_call_target="tpu_custom_call" | custom-call | flops 2415919104 | bytes 4194304 | tf_op jit(solution)/shard_map/near/pallas_call | solution.py:235
  105.6 6.0 %collective-permute-done.14.refs_1_ = bf16[2,560,256]{2,1,0:T(8,128)(2,1)S(1)} collective-permute-done((bf16[2,560,256]{2,1,0:T(8,128)(2,1)S(1)}, bf16[2,560,256]{2,1,0:T(8,128)(2,1)S(1)}, u32[]{:S(2)}, u32[]{:S(2)}) %collective-permute-start.14) | collective-permute-done | bytes 573472 | tf_op jit(solution)/shard_map/ppermute | solution.py:464
  112.5 2.0 %collective-permute-start.13 = (bf16[2,560,256]{2,1,0:T(8,128)(2,1)}, bf16[2,560,256]{2,1,0:T(8,128)(2,1)S(1)}, u32[]{:S(2)}, u32[]{:S(2)}) collective-permute-start(bf16[2,560,256]{2,1,0:T(8,128)(2,1)} %collective-permute-done.9.refs_0_), channel_id=1, source_target_pairs={{0,4},{4,8},{8,12},{12,16},{16,20},{20,24},{24,28},{28,0},{1,5},{5... | collective-permute-start | bytes 1720328 | tf_op jit(solution)/shard_map/ppermute | solution.py:479
  114.4 2.0 %all-to-all-done.2 = bf16[32,16,256]{2,1,0:T(8,128)(2,1)S(1)} async-done(((bf16[32,16,256]{2,1,0:T(8,128)(2,1)}), bf16[32,16,256]{2,1,0:T(8,128)(2,1)S(1)}, u32[]{:S(2)}, u32[]{:S(2)}) %all-to-all-start.2) | async-done | bytes 262176 | tf_op jit(solution)/shard_map/all_to_all | solution.py:419
  116.8 10.8 %near.8.refs_2_ = f32[65,32,256]{2,1,0:T(8,128)} custom-call(f32[1]{0:T(128)} %bitcast.1.scale_ref, s32[5]{0:T(128)} %copy-done.5, s32[5,128]{1,0:T(8,128)} %fusion.66.lst, bf16[2,560,256]{2,1,0:T(8,128)(2,1)} %collective-permute-done.9.refs_0_, bf16[2,560,256]{2,1,0:T(8,128)(2,1)} %copy-done.23, bf16[2,560,256]{2,1,0:T(8,128)(2,1)} %copy-done.22, ...), custom_call_target="tpu_custom_call" | custom-call | flops 2415919104 | bytes 4194304 | tf_op jit(solution)/shard_map/near/pallas_call | solution.py:235
  127.7 1.7 %copy-done.11 = f32[65,32,256]{2,1,0:T(8,128)S(1)} copy-done((f32[65,32,256]{2,1,0:T(8,128)S(1)}, f32[65,32,256]{2,1,0:T(8,128)}, u32[]{:S(2)}) %copy-start.11) | copy-done | bytes 2129944
  129.4 5.9 %near.9 = (bf16[512,256]{1,0:T(8,128)(2,1)S(1)}, bf16[512,256]{1,0:T(8,128)(2,1)}, bf16[512,256]{1,0:T(8,128)(2,1)}, bf16[512,256]{1,0:T(8,128)(2,1)S(1)}) custom-call(f32[1]{0:T(128)} %bitcast.1.scale_ref, s32[5]{0:T(128)S(1)} %copy-done.6, s32[5,128]{1,0:T(8,128)S(1)} %copy-done.4, bf16[2,560,256]{2,1,0:T(8,128)(2,1)S(1)} %collective-permute-done.13.refs_0_, ...), custom_call_target="tpu_custom_call" | custom-call | flops 1207959552 | bytes 4194304 | tf_op jit(solution)/shard_map/near/pallas_call | solution.py:235
  135.3 1.6 %collective-permute-start.17 = (bf16[512,256]{1,0:T(8,128)(2,1)}, bf16[512,256]{1,0:T(8,128)(2,1)S(1)}, u32[]{:S(2)}, u32[]{:S(2)}) collective-permute-start(bf16[512,256]{1,0:T(8,128)(2,1)} %get-tuple-element.86), channel_id=1, source_target_pairs={{0,3},{1,0},{2,1},{3,2},{4,7},{5,4},{6,5},{7,6},{8,11},{9,8},{10,9... | collective-permute-start | bytes 786440 | tf_op jit(solution)/shard_map/ppermute | solution.py:489
  136.9 1.7 %collective-permute-start.18 = (bf16[512,256]{1,0:T(8,128)(2,1)}, bf16[512,256]{1,0:T(8,128)(2,1)S(1)}, u32[]{:S(2)}, u32[]{:S(2)}) collective-permute-start(bf16[512,256]{1,0:T(8,128)(2,1)} %get-tuple-element.87), channel_id=1, source_target_pairs={{0,2},{1,3},{2,0},{3,1},{4,6},{5,7},{6,4},{7,5},{8,10},{9,11},{10,... | collective-permute-start | bytes 786440 | tf_op jit(solution)/shard_map/ppermute | solution.py:489
  139.5 8.1 %home.1.home_ref = f32[4096,128]{1,0:T(8,128)S(1)} custom-call(s32[1]{0:T(128)} %bitcast.y_ref, f32[4]{0:T(128)S(1)} %get-tuple-element.98.scale_ref, bf16[560,256]{1,0:T(8,128)(2,1)S(1)} %copy-done.3, bf16[560,256]{1,0:T(8,128)(2,1)S(1)} %copy-done.7, bf16[560,256]{1,0:T(8,128)(2,1)S(1)} %copy-done.8, bf16[560,256]{1,0:T(8,128)(2,1)S(1)} %copy-done.9, ...), custom_call_target="tpu_custom_call" | custom-call | flops 2147483648 | bytes 3145728 | tf_op jit(solution)/shard_map/home/pallas_call | solution.py:326
  147.9 3.4 %collective-permute-done.19.n3 = bf16[512,256]{1,0:T(8,128)(2,1)S(1)} collective-permute-done((bf16[512,256]{1,0:T(8,128)(2,1)S(1)}, bf16[512,256]{1,0:T(8,128)(2,1)S(1)}, u32[]{:S(2)}, u32[]{:S(2)}) %collective-permute-start.19) | collective-permute-done | bytes 262176 | tf_op jit(solution)/shard_map/ppermute | solution.py:489
  151.2 2.2 %final.1 = bf16[4096,128]{1,0:T(8,128)(2,1)} custom-call(s32[1]{0:T(128)} %bitcast.y_ref, f32[4096,128]{1,0:T(8,128)S(1)} %home.1.home_ref, bf16[512,256]{1,0:T(8,128)(2,1)S(1)} %get-tuple-element.85.n0, bf16[512,256]{1,0:T(8,128)(2,1)S(1)} %collective-permute-done.17.n1, bf16[512,256]{1,0:T(8,128)(2,1)S(1)} %collective-permute-done.18.n2, ...), custom_call_target="tpu_custom_call" | custom-call | tf_op jit(solution)/shard_map/final/pallas_call | solution.py:358
  (110 shorter events, 11.8 us)
Async XLA Ops:
  0.0 45.2 %copy-start = (bf16[128,128]{1,0:T(8,128)(2,1)S(1)}, bf16[128,128]{1,0:T(8,128)(2,1)}, u32[]{:S(2)}) copy-start(bf16[128,128]{1,0:T(8,128)(2,1)} %param.22) | copy-start | bytes 98308
  0.0 21.5 %copy-start.16 = (s32[2,1024]{1,0:T(2,128)S(1)}, s32[2,1024]{1,0:T(2,128)}, u32[]{:S(2)}) copy-start(s32[2,1024]{1,0:T(2,128)} %param.16) | copy-start | bytes 24580
  3.1 19.0 %copy-start.3 = (bf16[560,256]{1,0:T(8,128)(2,1)S(1)}, bf16[560,256]{1,0:T(8,128)(2,1)}, u32[]{:S(2)}) copy-start(bf16[560,256]{1,0:T(8,128)(2,1)} %get-tuple-element.80.refs_0_.v0.x_ref.y_row.z_ref) | copy-start | bytes 860164
  3.1 23.2 %copy-start.18 = (f32[4]{0:T(128)S(1)}, f32[4]{0:T(128)}, u32[]{:S(2)}) copy-start(f32[4]{0:T(128)} %param.19) | copy-start | bytes 52
  3.1 24.5 %collective-permute-start.3 = (bf16[560,256]{1,0:T(8,128)(2,1)}, bf16[560,256]{1,0:T(8,128)(2,1)S(1)}, u32[]{:S(2)}, u32[]{:S(2)}) collective-permute-start(bf16[560,256]{1,0:T(8,128)(2,1)} %get-tuple-element.82.v2), channel_id=1, source_target_pairs={{0,2},{1,3},{2,0},{3,1},{4,6},{5,7},{6,4},{7,5},{8,10},{9,11},{10,... | collective-permute-start | bytes 860168 | tf_op jit(solution)/shard_map/ppermute | solution.py:452
  6.3 21.3 %collective-permute-start.4 = (bf16[560,256]{1,0:T(8,128)(2,1)}, bf16[560,256]{1,0:T(8,128)(2,1)S(1)}, u32[]{:S(2)}, u32[]{:S(2)}) collective-permute-start(bf16[560,256]{1,0:T(8,128)(2,1)} %get-tuple-element.83.v3), channel_id=1, source_target_pairs={{0,3},{1,0},{2,1},{3,2},{4,7},{5,4},{6,5},{7,6},{8,11},{9,8},{10,9... | collective-permute-start | bytes 860168 | tf_op jit(solution)/shard_map/ppermute | solution.py:452
  7.4 14.7 %collective-permute-start = (bf16[560,256]{1,0:T(8,128)(2,1)}, bf16[560,256]{1,0:T(8,128)(2,1)S(1)}, u32[]{:S(2)}, u32[]{:S(2)}) collective-permute-start(bf16[560,256]{1,0:T(8,128)(2,1)} %get-tuple-element.81.v1), channel_id=1, source_target_pairs={{0,1},{1,2},{2,3},{3,0},{4,5},{5,6},{6,7},{7,4},{8,9},{9,10},{10,1... | collective-permute-start | bytes 860168 | tf_op jit(solution)/shard_map/ppermute | solution.py:452
  10.9 28.0 %all-to-all-start = ((bf16[32,40,128]{2,1,0:T(8,128)(2,1)}), bf16[32,40,128]{2,1,0:T(8,128)(2,1)S(1)}, u32[]{:S(2)}, u32[]{:S(2)}) async-start(bf16[32,40,128]{2,1,0:T(8,128)(2,1)} %copy.29), calls=%async_computation | async-start | bytes 655360 | tf_op jit(solution)/shard_map/all_to_all | solution.py:388
  22.2 22.5 %collective-permute-start.1 = (bf16[2,560,256]{2,1,0:T(8,128)(2,1)S(1)}, bf16[2,560,256]{2,1,0:T(8,128)(2,1)S(1)}, u32[]{:S(2)}, u32[]{:S(2)}) collective-permute-start(bf16[2,560,256]{2,1,0:T(8,128)(2,1)S(1)} %pack.2.refs_0_), channel_id=1, source_target_pairs={{0,4},{4,8},{8,12},{12,16},{16,20},{20,24},{24,28},{28,0},{1,5},{5... | collective-permute-start | bytes 1720328 | tf_op jit(solution)/shard_map/ppermute | solution.py:464
  24.0 20.6 %collective-permute-start.2 = (bf16[2,560,256]{2,1,0:T(8,128)(2,1)S(1)}, bf16[2,560,256]{2,1,0:T(8,128)(2,1)S(1)}, u32[]{:S(2)}, u32[]{:S(2)}) collective-permute-start(bf16[2,560,256]{2,1,0:T(8,128)(2,1)S(1)} %pack.2.refs_0_), channel_id=1, source_target_pairs={{0,28},{4,0},{8,4},{12,8},{16,12},{20,16},{24,20},{28,24},{1,29},{... | collective-permute-start | bytes 1720328 | tf_op jit(solution)/shard_map/ppermute | solution.py:465
  27.7 29.4 %collective-permute-start.7 = (bf16[2,560,256]{2,1,0:T(8,128)(2,1)S(1)}, bf16[2,560,256]{2,1,0:T(8,128)(2,1)}, u32[]{:S(2)}, u32[]{:S(2)}) collective-permute-start(bf16[2,560,256]{2,1,0:T(8,128)(2,1)S(1)} %pack.3.refs_1_), channel_id=1, source_target_pairs={{0,4},{4,8},{8,12},{12,16},{16,20},{20,24},{24,28},{28,0},{1,5},{5... | collective-permute-start | bytes 1720328 | tf_op jit(solution)/shard_map/ppermute | solution.py:464
  28.2 28.9 %collective-permute-start.8 = (bf16[2,560,256]{2,1,0:T(8,128)(2,1)S(1)}, bf16[2,560,256]{2,1,0:T(8,128)(2,1)}, u32[]{:S(2)}, u32[]{:S(2)}) collective-permute-start(bf16[2,560,256]{2,1,0:T(8,128)(2,1)S(1)} %pack.3.refs_1_), channel_id=1, source_target_pairs={{0,28},{4,0},{8,4},{12,8},{16,12},{20,16},{24,20},{28,24},{1,29},{... | collective-permute-start | bytes 1720328 | tf_op jit(solution)/shard_map/ppermute | solution.py:465
  31.0 17.7 %copy-start.17 = (s32[128]{0:T(128)S(1)}, s32[128]{0:T(128)}, u32[]{:S(2)}) copy-start(s32[128]{0:T(128)} %param.18) | copy-start | bytes 1540
  38.9 21.4 %copy-start.13 = (bf16[128,128]{1,0:T(8,128)(2,1)S(1)}, bf16[128,128]{1,0:T(8,128)(2,1)}, u32[]{:S(2)}) copy-start(bf16[128,128]{1,0:T(8,128)(2,1)} %param.24) | copy-start | bytes 98308
  44.7 15.8 %copy-start.20 = (bf16[2,560,256]{2,1,0:T(8,128)(2,1)}, bf16[2,560,256]{2,1,0:T(8,128)(2,1)S(1)}, u32[]{:S(2)}) copy-start(bf16[2,560,256]{2,1,0:T(8,128)(2,1)S(1)} %collective-permute-done.2.refs_2_) | copy-start | bytes 1720324
  45.4 27.3 %collective-permute-start.5 = (bf16[2,560,256]{2,1,0:T(8,128)(2,1)S(1)}, bf16[2,560,256]{2,1,0:T(8,128)(2,1)}, u32[]{:S(2)}, u32[]{:S(2)}) collective-permute-start(bf16[2,560,256]{2,1,0:T(8,128)(2,1)S(1)} %collective-permute-done.1.refs_0_), channel_id=1, source_target_pairs={{0,4},{4,8},{8,12},{12,16},{16,20},{20,24},{24,28},{28,0},{1,5},{5... | collective-permute-start | bytes 1720328 | tf_op jit(solution)/shard_map/ppermute | solution.py:464
  45.6 27.1 %collective-permute-start.6 = (bf16[2,560,256]{2,1,0:T(8,128)(2,1)S(1)}, bf16[2,560,256]{2,1,0:T(8,128)(2,1)}, u32[]{:S(2)}, u32[]{:S(2)}) collective-permute-start(bf16[2,560,256]{2,1,0:T(8,128)(2,1)S(1)} %collective-permute-done.2.refs_2_), channel_id=1, source_target_pairs={{0,28},{4,0},{8,4},{12,8},{16,12},{20,16},{24,20},{28,24},{1,29},{... | collective-permute-start | bytes 1720328 | tf_op jit(solution)/shard_map/ppermute | solution.py:465
  49.5 23.2 %all-to-all-start.1 = ((bf16[8,8,256]{2,1,0:T(8,128)(2,1)}), bf16[8,8,256]{2,1,0:T(8,128)(2,1)S(1)}, u32[]{:S(2)}, u32[]{:S(2)}) async-start(bf16[8,8,256]{2,1,0:T(8,128)(2,1)} %broadcast_in_dim.90), calls=%async_computation.1 | async-start | bytes 65536 | tf_op jit(solution)/shard_map/all_to_all | solution.py:372
  57.0 23.2 %collective-permute-start.11 = (bf16[2,560,256]{2,1,0:T(8,128)(2,1)}, bf16[2,560,256]{2,1,0:T(8,128)(2,1)S(1)}, u32[]{:S(2)}, u32[]{:S(2)}) collective-permute-start(bf16[2,560,256]{2,1,0:T(8,128)(2,1)} %collective-permute-done.7.refs_1_), channel_id=1, source_target_pairs={{0,4},{4,8},{8,12},{12,16},{16,20},{20,24},{24,28},{28,0},{1,5},{5... | collective-permute-start | bytes 1720328 | tf_op jit(solution)/shard_map/ppermute | solution.py:464
  57.1 23.1 %collective-permute-start.12 = (bf16[2,560,256]{2,1,0:T(8,128)(2,1)}, bf16[2,560,256]{2,1,0:T(8,128)(2,1)}, u32[]{:S(2)}, u32[]{:S(2)}) collective-permute-start(bf16[2,560,256]{2,1,0:T(8,128)(2,1)} %collective-permute-done.8.refs_3_), channel_id=1, source_target_pairs={{0,28},{4,0},{8,4},{12,8},{16,12},{20,16},{24,20},{28,24},{1,29},{... | collective-permute-start | bytes 1720328 | tf_op jit(solution)/shard_map/ppermute | solution.py:465
  60.5 25.0 %copy-start.15 = (bf16[128,128]{1,0:T(8,128)(2,1)S(1)}, bf16[128,128]{1,0:T(8,128)(2,1)}, u32[]{:S(2)}) copy-start(bf16[128,128]{1,0:T(8,128)(2,1)} %param.23) | copy-start | bytes 98308
  80.2 25.3 %collective-permute-start.10 = (bf16[2,560,256]{2,1,0:T(8,128)(2,1)}, bf16[2,560,256]{2,1,0:T(8,128)(2,1)S(1)}, u32[]{:S(2)}, u32[]{:S(2)}) collective-permute-start(bf16[2,560,256]{2,1,0:T(8,128)(2,1)} %collective-permute-done.6.refs_2_), channel_id=1, source_target_pairs={{0,28},{4,0},{8,4},{12,8},{16,12},{20,16},{24,20},{28,24},{1,29},{... | collective-permute-start | bytes 1720328 | tf_op jit(solution)/shard_map/ppermute | solution.py:465
  81.5 24.0 %collective-permute-start.9 = (bf16[2,560,256]{2,1,0:T(8,128)(2,1)}, bf16[2,560,256]{2,1,0:T(8,128)(2,1)}, u32[]{:S(2)}, u32[]{:S(2)}) collective-permute-start(bf16[2,560,256]{2,1,0:T(8,128)(2,1)} %collective-permute-done.5.refs_0_), channel_id=1, source_target_pairs={{0,4},{4,8},{8,12},{12,16},{16,20},{20,24},{24,28},{28,0},{1,5},{5... | collective-permute-start | bytes 1720328 | tf_op jit(solution)/shard_map/ppermute | solution.py:464
  82.2 29.4 %collective-permute-start.14 = (bf16[2,560,256]{2,1,0:T(8,128)(2,1)S(1)}, bf16[2,560,256]{2,1,0:T(8,128)(2,1)S(1)}, u32[]{:S(2)}, u32[]{:S(2)}) collective-permute-start(bf16[2,560,256]{2,1,0:T(8,128)(2,1)S(1)} %collective-permute-done.11.refs_1_), channel_id=1, source_target_pairs={{0,4},{4,8},{8,12},{12,16},{16,20},{20,24},{24,28},{28,0},{1,5},{5... | collective-permute-start | bytes 1720328 | tf_op jit(solution)/shard_map/ppermute | solution.py:464
  82.4 29.2 %collective-permute-start.15 = (bf16[2,560,256]{2,1,0:T(8,128)(2,1)}, bf16[2,560,256]{2,1,0:T(8,128)(2,1)}, u32[]{:S(2)}, u32[]{:S(2)}) collective-permute-start(bf16[2,560,256]{2,1,0:T(8,128)(2,1)} %collective-permute-done.12.refs_3_), channel_id=1, source_target_pairs={{0,28},{4,0},{8,4},{12,8},{16,12},{20,16},{24,20},{28,24},{1,29},{... | collective-permute-start | bytes 1720328 | tf_op jit(solution)/shard_map/ppermute | solution.py:465
  86.8 29.7 %all-to-all-start.2 = ((bf16[32,16,256]{2,1,0:T(8,128)(2,1)}), bf16[32,16,256]{2,1,0:T(8,128)(2,1)S(1)}, u32[]{:S(2)}, u32[]{:S(2)}) async-start(bf16[32,16,256]{2,1,0:T(8,128)(2,1)} %bitcast.12), calls=%async_computation.2 | async-start | bytes 524288 | tf_op jit(solution)/shard_map/all_to_all | solution.py:419
  112.4 15.2 %collective-permute-start.16 = (bf16[2,560,256]{2,1,0:T(8,128)(2,1)}, bf16[2,560,256]{2,1,0:T(8,128)(2,1)S(1)}, u32[]{:S(2)}, u32[]{:S(2)}) collective-permute-start(bf16[2,560,256]{2,1,0:T(8,128)(2,1)} %collective-permute-done.15.refs_3_), channel_id=1, source_target_pairs={{0,28},{4,0},{8,4},{12,8},{16,12},{20,16},{24,20},{28,24},{1,29},{... | collective-permute-start | bytes 1720328 | tf_op jit(solution)/shard_map/ppermute | solution.py:480
  112.5 15.2 %collective-permute-start.13 = (bf16[2,560,256]{2,1,0:T(8,128)(2,1)}, bf16[2,560,256]{2,1,0:T(8,128)(2,1)S(1)}, u32[]{:S(2)}, u32[]{:S(2)}) collective-permute-start(bf16[2,560,256]{2,1,0:T(8,128)(2,1)} %collective-permute-done.9.refs_0_), channel_id=1, source_target_pairs={{0,4},{4,8},{8,12},{12,16},{16,20},{20,24},{24,28},{28,0},{1,5},{5... | collective-permute-start | bytes 1720328 | tf_op jit(solution)/shard_map/ppermute | solution.py:479
  116.8 22.5 %copy-start.14 = (bf16[256,64]{0,1:T(8,128)(2,1)S(1)}, bf16[256,64]{0,1:T(8,128)(2,1)}, u32[]{:S(2)}) copy-start(bf16[256,64]{0,1:T(8,128)(2,1)} %param.26) | copy-start | bytes 98308
  135.3 12.3 %collective-permute-start.17 = (bf16[512,256]{1,0:T(8,128)(2,1)}, bf16[512,256]{1,0:T(8,128)(2,1)S(1)}, u32[]{:S(2)}, u32[]{:S(2)}) collective-permute-start(bf16[512,256]{1,0:T(8,128)(2,1)} %get-tuple-element.86), channel_id=1, source_target_pairs={{0,3},{1,0},{2,1},{3,2},{4,7},{5,4},{6,5},{7,6},{8,11},{9,8},{10,9... | collective-permute-start | bytes 786440 | tf_op jit(solution)/shard_map/ppermute | solution.py:489
  136.9 11.0 %collective-permute-start.18 = (bf16[512,256]{1,0:T(8,128)(2,1)}, bf16[512,256]{1,0:T(8,128)(2,1)S(1)}, u32[]{:S(2)}, u32[]{:S(2)}) collective-permute-start(bf16[512,256]{1,0:T(8,128)(2,1)} %get-tuple-element.87), channel_id=1, source_target_pairs={{0,2},{1,3},{2,0},{3,1},{4,6},{5,7},{6,4},{7,5},{8,10},{9,11},{10,... | collective-permute-start | bytes 786440 | tf_op jit(solution)/shard_map/ppermute | solution.py:489
  138.6 12.6 %collective-permute-start.19 = (bf16[512,256]{1,0:T(8,128)(2,1)S(1)}, bf16[512,256]{1,0:T(8,128)(2,1)S(1)}, u32[]{:S(2)}, u32[]{:S(2)}) collective-permute-start(bf16[512,256]{1,0:T(8,128)(2,1)S(1)} %get-tuple-element.88), channel_id=1, source_target_pairs={{0,1},{1,2},{2,3},{3,0},{4,5},{5,6},{6,7},{7,4},{8,9},{9,10},{10,1... | collective-permute-start | bytes 786440 | tf_op jit(solution)/shard_map/ppermute | solution.py:489
  (15 other events, 145.2 us)

commit v2 on v1

--- a/solution.py
+++ b/solution.py
@@ -222,6 +222,7 @@
 def near_step(scale, cnt, lst, number, chunks, sums=(), last=False):
     first = not sums
     anywhere = pl.BlockSpec(memory_space=pl.ANY)
+    hbm = pl.BlockSpec(memory_space=pltpu.HBM)
     lengths = tuple(c.shape[0] for c in chunks)
     args = [scale, cnt, lst, *chunks, *sums]
     acc_shape = (RBLK + 1, HC, B)
@@ -234,8 +235,8 @@
     sides = 9 * sum(lengths)
     return pl.pallas_call(
         functools.partial(near_kernel, number, lengths, first, last),
-        in_specs=[smem()] * 3 + [anywhere] * (len(args) - 3),
-        out_specs=[anywhere] * len(shapes),
+        in_specs=[smem()] * 3 + [anywhere] * len(chunks) + [hbm] * len(sums),
+        out_specs=[anywhere if last else hbm] * len(shapes),
         out_shape=shapes,
         scratch_shapes=[
             pltpu.VMEM(acc_shape, F32),
@@ -421,8 +422,8 @@
 
 def after(rows, acc, extra):
     (below_a, below_b), (above_a, above_b) = rows
-    below_a, above_a, acc, extra = lax.optimization_barrier((below_a, above_a, acc, extra))
-    below_b, above_b, acc = lax.optimization_barrier((below_b, above_b, acc))
+    below_a, above_a, acc = lax.optimization_barrier((below_a, above_a, acc))
+    below_b, above_b, acc, extra = lax.optimization_barrier((below_b, above_b, acc, extra))
     return ([below_a, below_b], [above_a, above_b]), acc, extra
 
 
@@ -478,8 +479,8 @@
     rows_three, acc, _ = after(rows_three, acc, acc)
     low = lax.ppermute(rows_three[0][0], "dev_0", up)
     high = lax.ppermute(rows_three[1][1], "dev_0", down)
-    acc, back = lax.optimization_barrier((acc, back))
     (acc,) = step(3, [*rows_three[0], *rows_three[1]], (acc, dst_aug))
+    low, high, acc, back = lax.optimization_barrier((low, high, acc, back))
     near = step(4, [low, high], (acc, dst_aug), last=True)
     parent_down = back.reshape(ROWS * COLS, BLK, 2, -1).transpose(1, 0, 2, 3)
     parent_down = parent_down.reshape(BLK, 2 * ROWS * COLS, -1)

time: 156 us -> 163 us (1.045)
  Pallas kernels: 60.9 us -> 66.5 us
  starting transfers between devices: 53.2 us -> 54.9 us
    pallas_call x5, Pallas kernels: 47.5 us -> 53 us  [near_step(): pl.pallas_call(functools.partial(near_kernel, number, lengths, first, las...]
    ppermute x6, waiting for transfers between devices: 21.3 us -> 26.3 us  [onward(): below = [lax.ppermute(half, 'dev_0', up) for half in below]]
    ppermute x3, waiting for transfers between devices: 3.63 us -> 0.01 us  [per_device(): lax.ppermute(near[s], 'dev_1', back_to[s])]
    all_to_all x1, waiting for transfers between devices: 2.01 us -> 0.01 us  [far_down(): lax.all_to_all(down.reshape(-1, BLK, down.shape[1]), DEV, 0, 0, tiled=True)]
    unnamed x49 -> x51, local copies, waits for them, and re-layouts: 2.67 us -> 3.57 us
  transfers between devices with their start and end apart: 23 -> 23, of which waited for: 7 -> 4; matrix products, arithmetic and copies ran while one was open for 6% -> 5% of each run, Pallas kernels for 32% -> 34%
where the time goes in v2:
time: 163 us; the launch traced here: 161 us
  Pallas kernels  66.5 us (41%)
  starting transfers between devices  54.9 us (34%)
  waiting for transfers between devices  26.4 us (16%)
  local copies, waits for them, and re-layouts  6.67 us (4%)
  other arithmetic  3.18 us (2%)
  matrix products  2.83 us (2%)
    pallas_call x5, Pallas kernels, near_step(): pl.pallas_call(functools.partial(near_kernel, number, lengths, first, las...  53 us
    ppermute x6, waiting for transfers between devices, onward(): below = [lax.ppermute(half, 'dev_0', up) for half in below]  26.3 us
    ppermute x6, starting transfers between devices, onward(): return (below, [lax.ppermute(half, 'dev_0', down) for half in above])  16.2 us
    all_to_all x1, starting transfers between devices, spread_summaries(): return lax.all_to_all(sent, DEV, 0, 0, tiled=True)  10.6 us
    pallas_call x1, Pallas kernels, home(): pl.pallas_call(home_kernel, grid=(BLK // 4,), in_specs=[smem(), smem()] +...  8.09 us
    all_to_all x1, starting transfers between devices, far_down(): lax.all_to_all(down.reshape(-1, BLK, down.shape[1]), DEV, 0, 0, tiled=True)  7.89 us
    ppermute x3, starting transfers between devices, per_device(): lax.ppermute(messages[s], 'dev_1', ahead[s])  5.22 us
    ppermute x3, starting transfers between devices, per_device(): lax.ppermute(near[s], 'dev_1', back_to[s])  5.01 us
  transfers between devices with their start and end apart: 23, of which 4 were waited for; matrix products, arithmetic and copies ran while one was open for 5% of the time, Pallas kernels for 34%

profile of v2, /device:TPU:6, one launch (start us, length us, event | category | flops | bytes accessed | tf_op | source)
XLA Modules:
  0.0 161.0 jit_solution(9891451817508866263)
XLA Ops:
  0.0 3.1 %prep.1 = (bf16[560,256]{1,0:T(8,128)(2,1)}, bf16[560,256]{1,0:T(8,128)(2,1)}, bf16[560,256]{1,0:T(8,128)(2,1)}, bf16[560,256]{1,0:T(8,128)(2,1)}, bf16[16,64,128]{2,1,0:T(8,128)(2,1)}) custom-call(s32[1]{0:T(128)} %bitcast.y_ref, bf16[4096,128]{1,0:T(8,128)(2,1)} %f_ref.1, bf16[3,4096]{1,0:T(4,128)(2,1)} %xyz_ref.1, bf16[128,128]{1,0:T(8,128)(2,1)} %wn_ref.1, ...), custom_call_target="tpu_custom_call" | custom-call | tf_op jit(solution)/shard_map/prep/pallas_call | solution.py:66
  3.1 3.2 %collective-permute-start.3 = (bf16[560,256]{1,0:T(8,128)(2,1)}, bf16[560,256]{1,0:T(8,128)(2,1)S(1)}, u32[]{:S(2)}, u32[]{:S(2)}) collective-permute-start(bf16[560,256]{1,0:T(8,128)(2,1)} %get-tuple-element.86.v2), channel_id=1, source_target_pairs={{0,2},{1,3},{2,0},{3,1},{4,6},{5,7},{6,4},{7,5},{8,10},{9,11},{10,... | collective-permute-start | bytes 860168 | tf_op jit(solution)/shard_map/ppermute | solution.py:453
  6.3 1.1 collective-permute-start.4
  7.4 1.0 collective-permute-start
  8.3 1.0 copy.28
  10.1 0.9 copy.29
  10.9 10.6 %all-to-all-start = ((bf16[32,40,128]{2,1,0:T(8,128)(2,1)}), bf16[32,40,128]{2,1,0:T(8,128)(2,1)S(1)}, u32[]{:S(2)}, u32[]{:S(2)}) async-start(bf16[32,40,128]{2,1,0:T(8,128)(2,1)} %copy.29), calls=%async_computation | async-start | bytes 655360 | tf_op jit(solution)/shard_map/all_to_all | solution.py:389
  22.8 1.9 %collective-permute-start.1 = (bf16[2,560,256]{2,1,0:T(8,128)(2,1)S(1)}, bf16[2,560,256]{2,1,0:T(8,128)(2,1)S(1)}, u32[]{:S(2)}, u32[]{:S(2)}) collective-permute-start(bf16[2,560,256]{2,1,0:T(8,128)(2,1)S(1)} %pack.2.refs_0_), channel_id=1, source_target_pairs={{0,4},{4,8},{8,12},{12,16},{16,20},{20,24},{24,28},{28,0},{1,5},{5... | collective-permute-start | bytes 1720328 | tf_op jit(solution)/shard_map/ppermute | solution.py:465
  24.7 1.4 collective-permute-start.2
  26.8 2.7 %collective-permute-start.8 = (bf16[2,560,256]{2,1,0:T(8,128)(2,1)S(1)}, bf16[2,560,256]{2,1,0:T(8,128)(2,1)}, u32[]{:S(2)}, u32[]{:S(2)}) collective-permute-start(bf16[2,560,256]{2,1,0:T(8,128)(2,1)S(1)} %pack.3.refs_1_), channel_id=1, source_target_pairs={{0,28},{4,0},{8,4},{12,8},{16,12},{20,16},{24,20},{28,24},{1,29},{... | collective-permute-start | bytes 1720328 | tf_op jit(solution)/shard_map/ppermute | solution.py:466
  30.9 9.3 %near.5 = (f32[65,32,256]{2,1,0:T(8,128)}, bf16[64,16,256]{2,1,0:T(8,128)(2,1)}) custom-call(f32[1]{0:T(128)} %bitcast.1.scale_ref, s32[5]{0:T(128)} %copy-done.5, s32[5,128]{1,0:T(8,128)} %fusion.66.lst, bf16[2,560,256]{2,1,0:T(8,128)(2,1)} %copy-done.1, bf16[2,560,256]{2,1,0:T(8,128)(2,1)} %copy-done.2), custom_call_target="tpu_custom_call" | custom-call | flops 1207959552 | bytes 4194304 | tf_op jit(solution)/shard_map/near/pallas_call | solution.py:236
  40.2 4.5 %collective-permute-done.1.refs_0_ = bf16[2,560,256]{2,1,0:T(8,128)(2,1)S(1)} collective-permute-done((bf16[2,560,256]{2,1,0:T(8,128)(2,1)S(1)}, bf16[2,560,256]{2,1,0:T(8,128)(2,1)S(1)}, u32[]{:S(2)}, u32[]{:S(2)}) %collective-permute-start.1) | collective-permute-done | bytes 573472 | tf_op jit(solution)/shard_map/ppermute | solution.py:465
  44.7 11.1 %collective-permute-done.7.refs_1_ = bf16[2,560,256]{2,1,0:T(8,128)(2,1)} collective-permute-done((bf16[2,560,256]{2,1,0:T(8,128)(2,1)S(1)}, bf16[2,560,256]{2,1,0:T(8,128)(2,1)}, u32[]{:S(2)}, u32[]{:S(2)}) %collective-permute-start.7) | collective-permute-done | bytes 573472 | tf_op jit(solution)/shard_map/ppermute | solution.py:465
  56.6 3.2 %collective-permute-start.6 = (bf16[2,560,256]{2,1,0:T(8,128)(2,1)S(1)}, bf16[2,560,256]{2,1,0:T(8,128)(2,1)}, u32[]{:S(2)}, u32[]{:S(2)}) collective-permute-start(bf16[2,560,256]{2,1,0:T(8,128)(2,1)S(1)} %collective-permute-done.2.refs_2_), channel_id=1, source_target_pairs={{0,28},{4,0},{8,4},{12,8},{16,12},{20,16},{24,20},{28,24},{1,29},{... | collective-permute-start | bytes 1720328 | tf_op jit(solution)/shard_map/ppermute | solution.py:466
  59.8 3.2 %collective-permute-start.12 = (bf16[2,560,256]{2,1,0:T(8,128)(2,1)}, bf16[2,560,256]{2,1,0:T(8,128)(2,1)}, u32[]{:S(2)}, u32[]{:S(2)}) collective-permute-start(bf16[2,560,256]{2,1,0:T(8,128)(2,1)} %collective-permute-done.8.refs_3_), channel_id=1, source_target_pairs={{0,28},{4,0},{8,4},{12,8},{16,12},{20,16},{24,20},{28,24},{1,29},{... | collective-permute-start | bytes 1720328 | tf_op jit(solution)/shard_map/ppermute | solution.py:466
  63.8 4.8 %all-to-all-start.1 = ((bf16[8,8,256]{2,1,0:T(8,128)(2,1)}), bf16[8,8,256]{2,1,0:T(8,128)(2,1)S(1)}, u32[]{:S(2)}, u32[]{:S(2)}) async-start(bf16[8,8,256]{2,1,0:T(8,128)(2,1)} %broadcast_in_dim.90), calls=%async_computation.1 | async-start | bytes 65536 | tf_op jit(solution)/shard_map/all_to_all | solution.py:373
  68.7 12.1 %near.6.refs_4_ = f32[65,32,256]{2,1,0:T(8,128)} custom-call(f32[1]{0:T(128)} %bitcast.1.scale_ref, s32[5]{0:T(128)} %copy-done.5, s32[5,128]{1,0:T(8,128)} %fusion.66.lst, bf16[2,560,256]{2,1,0:T(8,128)(2,1)} %copy-done.19, bf16[2,560,256]{2,1,0:T(8,128)(2,1)} %collective-permute-done.7.refs_1_, bf16[2,560,256]{2,1,0:T(8,128)(2,1)} %copy-done.20, ...), custom_call_target="tpu_custom_call" | custom-call | flops 2415919104 | bytes 4194304 | tf_op jit(solution)/shard_map/near/pallas_call | solution.py:236
  81.0 2.9 %collective-permute-done.11.refs_1_ = bf16[2,560,256]{2,1,0:T(8,128)(2,1)} collective-permute-done((bf16[2,560,256]{2,1,0:T(8,128)(2,1)}, bf16[2,560,256]{2,1,0:T(8,128)(2,1)}, u32[]{:S(2)}, u32[]{:S(2)}) %collective-permute-start.11) | collective-permute-done | bytes 573472 | tf_op jit(solution)/shard_map/ppermute | solution.py:465
  83.9 3.0 %collective-permute-start.10 = (bf16[2,560,256]{2,1,0:T(8,128)(2,1)}, bf16[2,560,256]{2,1,0:T(8,128)(2,1)S(1)}, u32[]{:S(2)}, u32[]{:S(2)}) collective-permute-start(bf16[2,560,256]{2,1,0:T(8,128)(2,1)} %collective-permute-done.6.refs_2_), channel_id=1, source_target_pairs={{0,28},{4,0},{8,4},{12,8},{16,12},{20,16},{24,20},{28,24},{1,29},{... | collective-permute-start | bytes 1720328 | tf_op jit(solution)/shard_map/ppermute | solution.py:466
  87.3 2.8 %collective-permute-start.15 = (bf16[2,560,256]{2,1,0:T(8,128)(2,1)}, bf16[2,560,256]{2,1,0:T(8,128)(2,1)}, u32[]{:S(2)}, u32[]{:S(2)}) collective-permute-start(bf16[2,560,256]{2,1,0:T(8,128)(2,1)} %collective-permute-done.12.refs_3_), channel_id=1, source_target_pairs={{0,28},{4,0},{8,4},{12,8},{16,12},{20,16},{24,20},{28,24},{1,29},{... | collective-permute-start | bytes 1720328 | tf_op jit(solution)/shard_map/ppermute | solution.py:466
  91.1 13.5 %near.7.refs_4_ = f32[65,32,256]{2,1,0:T(8,128)} custom-call(f32[1]{0:T(128)} %bitcast.1.scale_ref, s32[5]{0:T(128)} %copy-done.5, s32[5,128]{1,0:T(8,128)} %fusion.66.lst, bf16[2,560,256]{2,1,0:T(8,128)(2,1)} %copy-done.21, bf16[2,560,256]{2,1,0:T(8,128)(2,1)} %collective-permute-done.11.refs_1_, bf16[2,560,256]{2,1,0:T(8,128)(2,1)} %collective-permute-done.6.refs_2_, ...), custom_call_target="tpu_custom_call" | custom-call | flops 2415919104 | bytes 4194304 | tf_op jit(solution)/shard_map/near/pallas_call | solution.py:236
  104.7 7.8 %collective-permute-done.14.refs_1_ = bf16[2,560,256]{2,1,0:T(8,128)(2,1)S(1)} collective-permute-done((bf16[2,560,256]{2,1,0:T(8,128)(2,1)}, bf16[2,560,256]{2,1,0:T(8,128)(2,1)S(1)}, u32[]{:S(2)}, u32[]{:S(2)}) %collective-permute-start.14) | collective-permute-done | bytes 573472 | tf_op jit(solution)/shard_map/ppermute | solution.py:465
  113.3 2.0 %collective-permute-start.13 = (bf16[2,560,256]{2,1,0:T(8,128)(2,1)S(1)}, bf16[2,560,256]{2,1,0:T(8,128)(2,1)S(1)}, u32[]{:S(2)}, u32[]{:S(2)}) collective-permute-start(bf16[2,560,256]{2,1,0:T(8,128)(2,1)S(1)} %collective-permute-done.9.refs_0_), channel_id=1, source_target_pairs={{0,4},{4,8},{8,12},{12,16},{16,20},{20,24},{24,28},{28,0},{1,5},{5... | collective-permute-start | bytes 1720328 | tf_op jit(solution)/shard_map/ppermute | solution.py:480
  115.4 1.1 convolution_convert_fusion
  116.5 7.9 %all-to-all-start.2 = ((bf16[32,16,256]{2,1,0:T(8,128)(2,1)}), bf16[32,16,256]{2,1,0:T(8,128)(2,1)S(1)}, u32[]{:S(2)}, u32[]{:S(2)}) async-start(bf16[32,16,256]{2,1,0:T(8,128)(2,1)} %bitcast.12), calls=%async_computation.2 | async-start | bytes 524288 | tf_op jit(solution)/shard_map/all_to_all | solution.py:420
  124.4 12.2 %near.8.refs_2_ = f32[65,32,256]{2,1,0:T(8,128)} custom-call(f32[1]{0:T(128)} %bitcast.1.scale_ref, s32[5]{0:T(128)} %copy-done.5, s32[5,128]{1,0:T(8,128)} %fusion.66.lst, bf16[2,560,256]{2,1,0:T(8,128)(2,1)} %copy-done.22, bf16[2,560,256]{2,1,0:T(8,128)(2,1)} %copy-done.24, bf16[2,560,256]{2,1,0:T(8,128)(2,1)} %copy-done.23, ...), custom_call_target="tpu_custom_call" | custom-call | flops 2415919104 | bytes 4194304 | tf_op jit(solution)/shard_map/near/pallas_call | solution.py:236
  137.0 1.6 copy-done.11
  138.6 5.9 %near.9 = (bf16[512,256]{1,0:T(8,128)(2,1)S(1)}, bf16[512,256]{1,0:T(8,128)(2,1)}, bf16[512,256]{1,0:T(8,128)(2,1)}, bf16[512,256]{1,0:T(8,128)(2,1)}) custom-call(f32[1]{0:T(128)} %bitcast.1.scale_ref, s32[5]{0:T(128)S(1)} %copy-done.6, s32[5,128]{1,0:T(8,128)S(1)} %copy-done.4, bf16[2,560,256]{2,1,0:T(8,128)(2,1)S(1)} %collective-permute-done.13.refs_0_, ...), custom_call_target="tpu_custom_call" | custom-call | flops 1207959552 | bytes 4194304 | tf_op jit(solution)/shard_map/near/pallas_call | solution.py:236
  144.5 3.3 %collective-permute-start.17 = (bf16[512,256]{1,0:T(8,128)(2,1)}, bf16[512,256]{1,0:T(8,128)(2,1)S(1)}, u32[]{:S(2)}, u32[]{:S(2)}) collective-permute-start(bf16[512,256]{1,0:T(8,128)(2,1)} %get-tuple-element.90), channel_id=1, source_target_pairs={{0,3},{1,0},{2,1},{3,2},{4,7},{5,4},{6,5},{7,6},{8,11},{9,8},{10,9... | collective-permute-start | bytes 786440 | tf_op jit(solution)/shard_map/ppermute | solution.py:490
  149.7 0.9 copy-done.9
  150.6 8.1 %home.1.home_ref = f32[4096,128]{1,0:T(8,128)S(1)} custom-call(s32[1]{0:T(128)} %bitcast.y_ref, f32[4]{0:T(128)S(1)} %get-tuple-element.102.scale_ref, bf16[560,256]{1,0:T(8,128)(2,1)S(1)} %copy-done.3, bf16[560,256]{1,0:T(8,128)(2,1)S(1)} %copy-done.7, bf16[560,256]{1,0:T(8,128)(2,1)S(1)} %copy-done.8, bf16[560,256]{1,0:T(8,128)(2,1)S(1)} %copy-done.9, ...), custom_call_target="tpu_custom_call" | custom-call | flops 2147483648 | bytes 3145728 | tf_op jit(solution)/shard_map/home/pallas_call | solution.py:327
  158.8 2.2 %final.1 = bf16[4096,128]{1,0:T(8,128)(2,1)} custom-call(s32[1]{0:T(128)} %bitcast.y_ref, f32[4096,128]{1,0:T(8,128)S(1)} %home.1.home_ref, bf16[512,256]{1,0:T(8,128)(2,1)S(1)} %get-tuple-element.89.n0, bf16[512,256]{1,0:T(8,128)(2,1)S(1)} %collective-permute-done.17.n1, bf16[512,256]{1,0:T(8,128)(2,1)S(1)} %collective-permute-done.18.n2, ...), custom_call_target="tpu_custom_call" | custom-call | tf_op jit(solution)/shard_map/final/pallas_call | solution.py:359
  (112 shorter events, 10.3 us)
Async XLA Ops:
  0.0 56.3 %copy-start = (bf16[128,128]{1,0:T(8,128)(2,1)S(1)}, bf16[128,128]{1,0:T(8,128)(2,1)}, u32[]{:S(2)}) copy-start(bf16[128,128]{1,0:T(8,128)(2,1)} %param.22) | copy-start | bytes 98308
  0.0 21.5 %copy-start.16 = (s32[2,1024]{1,0:T(2,128)S(1)}, s32[2,1024]{1,0:T(2,128)}, u32[]{:S(2)}) copy-start(s32[2,1024]{1,0:T(2,128)} %param.16) | copy-start | bytes 24580
  0.0 22.1 %copy-start.18 = (f32[4]{0:T(128)S(1)}, f32[4]{0:T(128)}, u32[]{:S(2)}) copy-start(f32[4]{0:T(128)} %param.19) | copy-start | bytes 52
  3.1 23.0 %collective-permute-start.3 = (bf16[560,256]{1,0:T(8,128)(2,1)}, bf16[560,256]{1,0:T(8,128)(2,1)S(1)}, u32[]{:S(2)}, u32[]{:S(2)}) collective-permute-start(bf16[560,256]{1,0:T(8,128)(2,1)} %get-tuple-element.86.v2), channel_id=1, source_target_pairs={{0,2},{1,3},{2,0},{3,1},{4,6},{5,7},{6,4},{7,5},{8,10},{9,11},{10,... | collective-permute-start | bytes 860168 | tf_op jit(solution)/shard_map/ppermute | solution.py:453
  6.3 19.8 %collective-permute-start.4 = (bf16[560,256]{1,0:T(8,128)(2,1)}, bf16[560,256]{1,0:T(8,128)(2,1)S(1)}, u32[]{:S(2)}, u32[]{:S(2)}) collective-permute-start(bf16[560,256]{1,0:T(8,128)(2,1)} %get-tuple-element.87.v3), channel_id=1, source_target_pairs={{0,3},{1,0},{2,1},{3,2},{4,7},{5,4},{6,5},{7,6},{8,11},{9,8},{10,9... | collective-permute-start | bytes 860168 | tf_op jit(solution)/shard_map/ppermute | solution.py:453
  7.4 15.4 %collective-permute-start = (bf16[560,256]{1,0:T(8,128)(2,1)}, bf16[560,256]{1,0:T(8,128)(2,1)S(1)}, u32[]{:S(2)}, u32[]{:S(2)}) collective-permute-start(bf16[560,256]{1,0:T(8,128)(2,1)} %get-tuple-element.85.v1), channel_id=1, source_target_pairs={{0,1},{1,2},{2,3},{3,0},{4,5},{5,6},{6,7},{7,4},{8,9},{9,10},{10,1... | collective-permute-start | bytes 860168 | tf_op jit(solution)/shard_map/ppermute | solution.py:453
  10.9 33.8 %all-to-all-start = ((bf16[32,40,128]{2,1,0:T(8,128)(2,1)}), bf16[32,40,128]{2,1,0:T(8,128)(2,1)S(1)}, u32[]{:S(2)}, u32[]{:S(2)}) async-start(bf16[32,40,128]{2,1,0:T(8,128)(2,1)} %copy.29), calls=%async_computation | async-start | bytes 655360 | tf_op jit(solution)/shard_map/all_to_all | solution.py:389
  22.8 21.9 %collective-permute-start.1 = (bf16[2,560,256]{2,1,0:T(8,128)(2,1)S(1)}, bf16[2,560,256]{2,1,0:T(8,128)(2,1)S(1)}, u32[]{:S(2)}, u32[]{:S(2)}) collective-permute-start(bf16[2,560,256]{2,1,0:T(8,128)(2,1)S(1)} %pack.2.refs_0_), channel_id=1, source_target_pairs={{0,4},{4,8},{8,12},{12,16},{16,20},{20,24},{24,28},{28,0},{1,5},{5... | collective-permute-start | bytes 1720328 | tf_op jit(solution)/shard_map/ppermute | solution.py:465
  24.7 20.0 %collective-permute-start.2 = (bf16[2,560,256]{2,1,0:T(8,128)(2,1)S(1)}, bf16[2,560,256]{2,1,0:T(8,128)(2,1)S(1)}, u32[]{:S(2)}, u32[]{:S(2)}) collective-permute-start(bf16[2,560,256]{2,1,0:T(8,128)(2,1)S(1)} %pack.2.refs_0_), channel_id=1, source_target_pairs={{0,28},{4,0},{8,4},{12,8},{16,12},{20,16},{24,20},{28,24},{1,29},{... | collective-permute-start | bytes 1720328 | tf_op jit(solution)/shard_map/ppermute | solution.py:466
  26.2 29.6 %collective-permute-start.7 = (bf16[2,560,256]{2,1,0:T(8,128)(2,1)S(1)}, bf16[2,560,256]{2,1,0:T(8,128)(2,1)}, u32[]{:S(2)}, u32[]{:S(2)}) collective-permute-start(bf16[2,560,256]{2,1,0:T(8,128)(2,1)S(1)} %pack.3.refs_1_), channel_id=1, source_target_pairs={{0,4},{4,8},{8,12},{12,16},{16,20},{20,24},{24,28},{28,0},{1,5},{5... | collective-permute-start | bytes 1720328 | tf_op jit(solution)/shard_map/ppermute | solution.py:465
  26.8 28.9 %collective-permute-start.8 = (bf16[2,560,256]{2,1,0:T(8,128)(2,1)S(1)}, bf16[2,560,256]{2,1,0:T(8,128)(2,1)}, u32[]{:S(2)}, u32[]{:S(2)}) collective-permute-start(bf16[2,560,256]{2,1,0:T(8,128)(2,1)S(1)} %pack.3.refs_1_), channel_id=1, source_target_pairs={{0,28},{4,0},{8,4},{12,8},{16,12},{20,16},{24,20},{28,24},{1,29},{... | collective-permute-start | bytes 1720328 | tf_op jit(solution)/shard_map/ppermute | solution.py:466
  30.9 32.2 %copy-start.17 = (s32[128]{0:T(128)S(1)}, s32[128]{0:T(128)}, u32[]{:S(2)}) copy-start(s32[128]{0:T(128)} %param.18) | copy-start | bytes 1540
  40.2 28.4 %copy-start.13 = (bf16[128,128]{1,0:T(8,128)(2,1)S(1)}, bf16[128,128]{1,0:T(8,128)(2,1)}, u32[]{:S(2)}) copy-start(bf16[128,128]{1,0:T(8,128)(2,1)} %param.24) | copy-start | bytes 98308
  44.7 24.0 %copy-start.19 = (bf16[2,560,256]{2,1,0:T(8,128)(2,1)}, bf16[2,560,256]{2,1,0:T(8,128)(2,1)S(1)}, u32[]{:S(2)}) copy-start(bf16[2,560,256]{2,1,0:T(8,128)(2,1)S(1)} %collective-permute-done.1.refs_0_) | copy-start | bytes 1720324
  44.7 24.0 %copy-start.20 = (bf16[2,560,256]{2,1,0:T(8,128)(2,1)}, bf16[2,560,256]{2,1,0:T(8,128)(2,1)S(1)}, u32[]{:S(2)}) copy-start(bf16[2,560,256]{2,1,0:T(8,128)(2,1)S(1)} %collective-permute-done.2.refs_2_) | copy-start | bytes 1720324
  56.5 24.4 %collective-permute-start.5 = (bf16[2,560,256]{2,1,0:T(8,128)(2,1)S(1)}, bf16[2,560,256]{2,1,0:T(8,128)(2,1)S(1)}, u32[]{:S(2)}, u32[]{:S(2)}) collective-permute-start(bf16[2,560,256]{2,1,0:T(8,128)(2,1)S(1)} %collective-permute-done.1.refs_0_), channel_id=1, source_target_pairs={{0,4},{4,8},{8,12},{12,16},{16,20},{20,24},{24,28},{28,0},{1,5},{5... | collective-permute-start | bytes 1720328 | tf_op jit(solution)/shard_map/ppermute | solution.py:465
  56.6 24.3 %collective-permute-start.6 = (bf16[2,560,256]{2,1,0:T(8,128)(2,1)S(1)}, bf16[2,560,256]{2,1,0:T(8,128)(2,1)}, u32[]{:S(2)}, u32[]{:S(2)}) collective-permute-start(bf16[2,560,256]{2,1,0:T(8,128)(2,1)S(1)} %collective-permute-done.2.refs_2_), channel_id=1, source_target_pairs={{0,28},{4,0},{8,4},{12,8},{16,12},{20,16},{24,20},{28,24},{1,29},{... | collective-permute-start | bytes 1720328 | tf_op jit(solution)/shard_map/ppermute | solution.py:466
  59.8 24.1 %collective-permute-start.11 = (bf16[2,560,256]{2,1,0:T(8,128)(2,1)}, bf16[2,560,256]{2,1,0:T(8,128)(2,1)}, u32[]{:S(2)}, u32[]{:S(2)}) collective-permute-start(bf16[2,560,256]{2,1,0:T(8,128)(2,1)} %collective-permute-done.7.refs_1_), channel_id=1, source_target_pairs={{0,4},{4,8},{8,12},{12,16},{16,20},{20,24},{24,28},{28,0},{1,5},{5... | collective-permute-start | bytes 1720328 | tf_op jit(solution)/shard_map/ppermute | solution.py:465
  59.8 24.1 %collective-permute-start.12 = (bf16[2,560,256]{2,1,0:T(8,128)(2,1)}, bf16[2,560,256]{2,1,0:T(8,128)(2,1)}, u32[]{:S(2)}, u32[]{:S(2)}) collective-permute-start(bf16[2,560,256]{2,1,0:T(8,128)(2,1)} %collective-permute-done.8.refs_3_), channel_id=1, source_target_pairs={{0,28},{4,0},{8,4},{12,8},{16,12},{20,16},{24,20},{28,24},{1,29},{... | collective-permute-start | bytes 1720328 | tf_op jit(solution)/shard_map/ppermute | solution.py:466
  63.8 17.2 %all-to-all-start.1 = ((bf16[8,8,256]{2,1,0:T(8,128)(2,1)}), bf16[8,8,256]{2,1,0:T(8,128)(2,1)S(1)}, u32[]{:S(2)}, u32[]{:S(2)}) async-start(bf16[8,8,256]{2,1,0:T(8,128)(2,1)} %broadcast_in_dim.90), calls=%async_computation.1 | async-start | bytes 65536 | tf_op jit(solution)/shard_map/all_to_all | solution.py:373
  68.7 22.2 %copy-start.15 = (bf16[128,128]{1,0:T(8,128)(2,1)S(1)}, bf16[128,128]{1,0:T(8,128)(2,1)}, u32[]{:S(2)}) copy-start(bf16[128,128]{1,0:T(8,128)(2,1)} %param.23) | copy-start | bytes 98308
  83.9 20.8 %collective-permute-start.10 = (bf16[2,560,256]{2,1,0:T(8,128)(2,1)}, bf16[2,560,256]{2,1,0:T(8,128)(2,1)S(1)}, u32[]{:S(2)}, u32[]{:S(2)}) collective-permute-start(bf16[2,560,256]{2,1,0:T(8,128)(2,1)} %collective-permute-done.6.refs_2_), channel_id=1, source_target_pairs={{0,28},{4,0},{8,4},{12,8},{16,12},{20,16},{24,20},{28,24},{1,29},{... | collective-permute-start | bytes 1720328 | tf_op jit(solution)/shard_map/ppermute | solution.py:466
  86.8 17.8 %collective-permute-start.9 = (bf16[2,560,256]{2,1,0:T(8,128)(2,1)S(1)}, bf16[2,560,256]{2,1,0:T(8,128)(2,1)S(1)}, u32[]{:S(2)}, u32[]{:S(2)}) collective-permute-start(bf16[2,560,256]{2,1,0:T(8,128)(2,1)S(1)} %collective-permute-done.5.refs_0_), channel_id=1, source_target_pairs={{0,4},{4,8},{8,12},{12,16},{16,20},{20,24},{24,28},{28,0},{1,5},{5... | collective-permute-start | bytes 1720328 | tf_op jit(solution)/shard_map/ppermute | solution.py:465
  86.8 25.7 %collective-permute-start.14 = (bf16[2,560,256]{2,1,0:T(8,128)(2,1)}, bf16[2,560,256]{2,1,0:T(8,128)(2,1)S(1)}, u32[]{:S(2)}, u32[]{:S(2)}) collective-permute-start(bf16[2,560,256]{2,1,0:T(8,128)(2,1)} %collective-permute-done.11.refs_1_), channel_id=1, source_target_pairs={{0,4},{4,8},{8,12},{12,16},{16,20},{20,24},{24,28},{28,0},{1,5},{5... | collective-permute-start | bytes 1720328 | tf_op jit(solution)/shard_map/ppermute | solution.py:465
  87.3 25.2 %collective-permute-start.15 = (bf16[2,560,256]{2,1,0:T(8,128)(2,1)}, bf16[2,560,256]{2,1,0:T(8,128)(2,1)}, u32[]{:S(2)}, u32[]{:S(2)}) collective-permute-start(bf16[2,560,256]{2,1,0:T(8,128)(2,1)} %collective-permute-done.12.refs_3_), channel_id=1, source_target_pairs={{0,28},{4,0},{8,4},{12,8},{16,12},{20,16},{24,20},{28,24},{1,29},{... | collective-permute-start | bytes 1720328 | tf_op jit(solution)/shard_map/ppermute | solution.py:466
  104.7 19.8 %copy-start.22 = (bf16[2,560,256]{2,1,0:T(8,128)(2,1)}, bf16[2,560,256]{2,1,0:T(8,128)(2,1)S(1)}, u32[]{:S(2)}) copy-start(bf16[2,560,256]{2,1,0:T(8,128)(2,1)S(1)} %collective-permute-done.9.refs_0_) | copy-start | bytes 1720324
  113.3 23.3 %collective-permute-start.16 = (bf16[2,560,256]{2,1,0:T(8,128)(2,1)}, bf16[2,560,256]{2,1,0:T(8,128)(2,1)S(1)}, u32[]{:S(2)}, u32[]{:S(2)}) collective-permute-start(bf16[2,560,256]{2,1,0:T(8,128)(2,1)} %collective-permute-done.15.refs_3_), channel_id=1, source_target_pairs={{0,28},{4,0},{8,4},{12,8},{16,12},{20,16},{24,20},{28,24},{1,29},{... | collective-permute-start | bytes 1720328 | tf_op jit(solution)/shard_map/ppermute | solution.py:481
  113.3 23.3 %collective-permute-start.13 = (bf16[2,560,256]{2,1,0:T(8,128)(2,1)S(1)}, bf16[2,560,256]{2,1,0:T(8,128)(2,1)S(1)}, u32[]{:S(2)}, u32[]{:S(2)}) collective-permute-start(bf16[2,560,256]{2,1,0:T(8,128)(2,1)S(1)} %collective-permute-done.9.refs_0_), channel_id=1, source_target_pairs={{0,4},{4,8},{8,12},{12,16},{16,20},{20,24},{24,28},{28,0},{1,5},{5... | collective-permute-start | bytes 1720328 | tf_op jit(solution)/shard_map/ppermute | solution.py:480
  116.5 20.1 %all-to-all-start.2 = ((bf16[32,16,256]{2,1,0:T(8,128)(2,1)}), bf16[32,16,256]{2,1,0:T(8,128)(2,1)S(1)}, u32[]{:S(2)}, u32[]{:S(2)}) async-start(bf16[32,16,256]{2,1,0:T(8,128)(2,1)} %bitcast.12), calls=%async_computation.2 | async-start | bytes 524288 | tf_op jit(solution)/shard_map/all_to_all | solution.py:420
  144.5 14.2 %collective-permute-start.17 = (bf16[512,256]{1,0:T(8,128)(2,1)}, bf16[512,256]{1,0:T(8,128)(2,1)S(1)}, u32[]{:S(2)}, u32[]{:S(2)}) collective-permute-start(bf16[512,256]{1,0:T(8,128)(2,1)} %get-tuple-element.90), channel_id=1, source_target_pairs={{0,3},{1,0},{2,1},{3,2},{4,7},{5,4},{6,5},{7,6},{8,11},{9,8},{10,9... | collective-permute-start | bytes 786440 | tf_op jit(solution)/shard_map/ppermute | solution.py:490
  147.8 10.9 %collective-permute-start.18 = (bf16[512,256]{1,0:T(8,128)(2,1)}, bf16[512,256]{1,0:T(8,128)(2,1)S(1)}, u32[]{:S(2)}, u32[]{:S(2)}) collective-permute-start(bf16[512,256]{1,0:T(8,128)(2,1)} %get-tuple-element.91), channel_id=1, source_target_pairs={{0,2},{1,3},{2,0},{3,1},{4,6},{5,7},{6,4},{7,5},{8,10},{9,11},{10,... | collective-permute-start | bytes 786440 | tf_op jit(solution)/shard_map/ppermute | solution.py:490
  148.7 10.1 %collective-permute-start.19 = (bf16[512,256]{1,0:T(8,128)(2,1)}, bf16[512,256]{1,0:T(8,128)(2,1)S(1)}, u32[]{:S(2)}, u32[]{:S(2)}) collective-permute-start(bf16[512,256]{1,0:T(8,128)(2,1)} %get-tuple-element.92), channel_id=1, source_target_pairs={{0,1},{1,2},{2,3},{3,0},{4,5},{5,6},{6,7},{7,4},{8,9},{9,10},{10,1... | collective-permute-start | bytes 786440 | tf_op jit(solution)/shard_map/ppermute | solution.py:490
  (16 other events, 144.3 us)

commit v3 on v2

--- a/solution.py
+++ b/solution.py
@@ -451,7 +451,9 @@
     back_to = [[(i, (i - s) % COLS) for i in range(COLS)] for s in range(COLS)]
     slots = [messages[0]]
     slots += [lax.ppermute(messages[s], "dev_1", ahead[s]) for s in range(1, COLS)]
-    held = [pack(slots[:HALF]), pack(slots[HALF:])]
+    first_half = pack(slots[:HALF])
+    first_half, level_one = lax.optimization_barrier((first_half, level_one))
+    held = [first_half, pack(slots[HALF:])]
     scales = rates * math.log2(math.e)
     scale = jnp.sum(jnp.where(jnp.arange(COLS) == y, scales, 0.0)).reshape(1)
     cnt, lst = side_lists(near_pairs, z, y)
@@ -479,8 +481,8 @@
     rows_three, acc, _ = after(rows_three, acc, acc)
     low = lax.ppermute(rows_three[0][0], "dev_0", up)
     high = lax.ppermute(rows_three[1][1], "dev_0", down)
+    acc, back = lax.optimization_barrier((acc, back))
     (acc,) = step(3, [*rows_three[0], *rows_three[1]], (acc, dst_aug))
-    low, high, acc, back = lax.optimization_barrier((low, high, acc, back))
     near = step(4, [low, high], (acc, dst_aug), last=True)
     parent_down = back.reshape(ROWS * COLS, BLK, 2, -1).transpose(1, 0, 2, 3)
     parent_down = parent_down.reshape(BLK, 2 * ROWS * COLS, -1)

time: 163 us -> 166 us (1.018); the launches traced: 161 us -> 166 us
  waiting for transfers between devices: 26.4 us -> 34.4 us
  Pallas kernels: 66.5 us -> 63.4 us
    all_to_all x1, starting transfers between devices: 10.6 us -> 16.4 us  [spread_summaries(): return lax.all_to_all(sent, DEV, 0, 0, tiled=True)]
    ppermute x3, waiting for transfers between devices: 0.01 us -> 5.56 us  [per_device(): lax.ppermute(near[s], 'dev_1', back_to[s])]
    all_to_all x1, waiting for transfers between devices: 0.01 us -> 3.8 us  [far_down(): lax.all_to_all(down.reshape(-1, BLK, down.shape[1]), DEV, 0, 0, tiled=True)]
    ppermute x6, waiting for transfers between devices: 26.3 us -> 22.8 us  [onward(): below = [lax.ppermute(half, 'dev_0', up) for half in below]]
    pallas_call x5, Pallas kernels: 53 us -> 49.9 us  [near_step(): pl.pallas_call(functools.partial(near_kernel, number, lengths, first, las...]
    all_to_all x1, starting transfers between devices: 7.89 us -> 4.93 us  [far_down(): lax.all_to_all(down.reshape(-1, BLK, down.shape[1]), DEV, 0, 0, tiled=True)]
    ppermute x3, waiting for transfers between devices: 0.01 us -> 2.22 us  [per_device(): lax.ppermute(messages[s], 'dev_1', ahead[s])]
    ppermute x6, starting transfers between devices: 16.2 us -> 14.2 us  [onward(): return (below, [lax.ppermute(half, 'dev_0', down) for half in above])]
  transfers between devices with their start and end apart: 23 -> 23, of which waited for: 4 -> 6; matrix products, arithmetic and copies ran while one was open for 5% -> 6% of each run, Pallas kernels for 34% -> 31%
where the time goes in v3:
time: 166 us
  Pallas kernels  63.4 us (38%)
  starting transfers between devices  54.5 us (33%)
  waiting for transfers between devices  34.4 us (21%)
  local copies, waits for them, and re-layouts  6.93 us (4%)
  other arithmetic  3.13 us (2%)
  matrix products  2.83 us (2%)
    pallas_call x5, Pallas kernels, near_step(): pl.pallas_call(functools.partial(near_kernel, number, lengths, first, las...  49.9 us
    ppermute x6, waiting for transfers between devices, onward(): below = [lax.ppermute(half, 'dev_0', up) for half in below]  22.8 us
    all_to_all x1, starting transfers between devices, spread_summaries(): return lax.all_to_all(sent, DEV, 0, 0, tiled=True)  16.4 us
    ppermute x6, starting transfers between devices, onward(): return (below, [lax.ppermute(half, 'dev_0', down) for half in above])  14.2 us
    pallas_call x1, Pallas kernels, home(): pl.pallas_call(home_kernel, grid=(BLK // 4,), in_specs=[smem(), smem()] +...  8.11 us
    ppermute x3, starting transfers between devices, per_device(): lax.ppermute(messages[s], 'dev_1', ahead[s])  5.83 us
    ppermute x3, waiting for transfers between devices, per_device(): lax.ppermute(near[s], 'dev_1', back_to[s])  5.56 us
    all_to_all x1, starting transfers between devices, far_down(): lax.all_to_all(down.reshape(-1, BLK, down.shape[1]), DEV, 0, 0, tiled=True)  4.93 us
  transfers between devices with their start and end apart: 23, of which 6 were waited for; matrix products, arithmetic and copies ran while one was open for 6% of the time, Pallas kernels for 31%

profile of v3, /device:TPU:6, one launch (start us, length us, event | category | flops | bytes accessed | tf_op | source)
XLA Modules:
  0.0 165.9 jit_solution(15769465091586909483)
XLA Ops:
  0.0 3.1 %prep.1 = (bf16[560,256]{1,0:T(8,128)(2,1)}, bf16[560,256]{1,0:T(8,128)(2,1)}, bf16[560,256]{1,0:T(8,128)(2,1)}, bf16[560,256]{1,0:T(8,128)(2,1)}, bf16[16,64,128]{2,1,0:T(8,128)(2,1)}) custom-call(s32[1]{0:T(128)} %bitcast.y_ref, bf16[4096,128]{1,0:T(8,128)(2,1)} %f_ref.1, bf16[3,4096]{1,0:T(4,128)(2,1)} %xyz_ref.1, bf16[128,128]{1,0:T(8,128)(2,1)} %wn_ref.1, ...), custom_call_target="tpu_custom_call" | custom-call | tf_op jit(solution)/shard_map/prep/pallas_call | solution.py:66
  3.1 1.6 collective-permute-start
  4.7 2.9 %collective-permute-start.3 = (bf16[560,256]{1,0:T(8,128)(2,1)}, bf16[560,256]{1,0:T(8,128)(2,1)S(1)}, u32[]{:S(2)}, u32[]{:S(2)}) collective-permute-start(bf16[560,256]{1,0:T(8,128)(2,1)} %get-tuple-element.86.v2), channel_id=1, source_target_pairs={{0,2},{1,3},{2,0},{3,1},{4,6},{5,7},{6,4},{7,5},{8,10},{9,11},{10,... | collective-permute-start | bytes 860168 | tf_op jit(solution)/shard_map/ppermute | solution.py:453
  7.6 1.3 collective-permute-start.4
  10.9 2.2 %collective-permute-done.refs_1_ = bf16[560,256]{1,0:T(8,128)(2,1)S(1)} collective-permute-done((bf16[560,256]{1,0:T(8,128)(2,1)}, bf16[560,256]{1,0:T(8,128)(2,1)S(1)}, u32[]{:S(2)}, u32[]{:S(2)}) %collective-permute-start) | collective-permute-done | bytes 286752 | tf_op jit(solution)/shard_map/ppermute | solution.py:453
  14.2 1.2 copy.28
  16.3 16.4 %all-to-all-start = ((bf16[32,40,128]{2,1,0:T(8,128)(2,1)}), bf16[32,40,128]{2,1,0:T(8,128)(2,1)S(1)}, u32[]{:S(2)}, u32[]{:S(2)}) async-start(bf16[32,40,128]{2,1,0:T(8,128)(2,1)} %copy.29), calls=%async_computation | async-start | bytes 655360 | tf_op jit(solution)/shard_map/all_to_all | solution.py:389
  33.3 1.8 %collective-permute-start.1 = (bf16[2,560,256]{2,1,0:T(8,128)(2,1)S(1)}, bf16[2,560,256]{2,1,0:T(8,128)(2,1)}, u32[]{:S(2)}, u32[]{:S(2)}) collective-permute-start(bf16[2,560,256]{2,1,0:T(8,128)(2,1)S(1)} %pack.2.refs_0_), channel_id=1, source_target_pairs={{0,4},{4,8},{8,12},{12,16},{16,20},{20,24},{24,28},{28,0},{1,5},{5... | collective-permute-start | bytes 1720328 | tf_op jit(solution)/shard_map/ppermute | solution.py:467
  35.1 1.4 collective-permute-start.2
  37.2 2.7 %collective-permute-start.8 = (bf16[2,560,256]{2,1,0:T(8,128)(2,1)S(1)}, bf16[2,560,256]{2,1,0:T(8,128)(2,1)S(1)}, u32[]{:S(2)}, u32[]{:S(2)}) collective-permute-start(bf16[2,560,256]{2,1,0:T(8,128)(2,1)S(1)} %pack.3.refs_1_), channel_id=1, source_target_pairs={{0,28},{4,0},{8,4},{12,8},{16,12},{20,16},{24,20},{28,24},{1,29},{... | collective-permute-start | bytes 1720328 | tf_op jit(solution)/shard_map/ppermute | solution.py:468
  41.3 7.8 %near.5 = (f32[65,32,256]{2,1,0:T(8,128)}, bf16[64,16,256]{2,1,0:T(8,128)(2,1)}) custom-call(f32[1]{0:T(128)} %bitcast.1.scale_ref, s32[5]{0:T(128)} %copy-done.6, s32[5,128]{1,0:T(8,128)} %fusion.66.lst, bf16[2,560,256]{2,1,0:T(8,128)(2,1)} %copy-done.1, bf16[2,560,256]{2,1,0:T(8,128)(2,1)} %copy-done.2), custom_call_target="tpu_custom_call" | custom-call | flops 1207959552 | bytes 4194304 | tf_op jit(solution)/shard_map/near/pallas_call | solution.py:236
  49.1 5.6 %collective-permute-done.1.refs_0_ = bf16[2,560,256]{2,1,0:T(8,128)(2,1)} collective-permute-done((bf16[2,560,256]{2,1,0:T(8,128)(2,1)S(1)}, bf16[2,560,256]{2,1,0:T(8,128)(2,1)}, u32[]{:S(2)}, u32[]{:S(2)}) %collective-permute-start.1) | collective-permute-done | bytes 573472 | tf_op jit(solution)/shard_map/ppermute | solution.py:467
  54.8 3.1 %collective-permute-start.6 = (bf16[2,560,256]{2,1,0:T(8,128)(2,1)}, bf16[2,560,256]{2,1,0:T(8,128)(2,1)S(1)}, u32[]{:S(2)}, u32[]{:S(2)}) collective-permute-start(bf16[2,560,256]{2,1,0:T(8,128)(2,1)} %collective-permute-done.2.refs_2_), channel_id=1, source_target_pairs={{0,28},{4,0},{8,4},{12,8},{16,12},{20,16},{24,20},{28,24},{1,29},{... | collective-permute-start | bytes 1720328 | tf_op jit(solution)/shard_map/ppermute | solution.py:468
  57.9 8.9 %collective-permute-done.7.refs_1_ = bf16[2,560,256]{2,1,0:T(8,128)(2,1)S(1)} collective-permute-done((bf16[2,560,256]{2,1,0:T(8,128)(2,1)S(1)}, bf16[2,560,256]{2,1,0:T(8,128)(2,1)S(1)}, u32[]{:S(2)}, u32[]{:S(2)}) %collective-permute-start.7) | collective-permute-done | bytes 573472 | tf_op jit(solution)/shard_map/ppermute | solution.py:467
  67.8 3.1 %collective-permute-start.12 = (bf16[2,560,256]{2,1,0:T(8,128)(2,1)S(1)}, bf16[2,560,256]{2,1,0:T(8,128)(2,1)}, u32[]{:S(2)}, u32[]{:S(2)}) collective-permute-start(bf16[2,560,256]{2,1,0:T(8,128)(2,1)S(1)} %collective-permute-done.8.refs_3_), channel_id=1, source_target_pairs={{0,28},{4,0},{8,4},{12,8},{16,12},{20,16},{24,20},{28,24},{1,29},{... | collective-permute-start | bytes 1720328 | tf_op jit(solution)/shard_map/ppermute | solution.py:468
  71.7 4.8 %all-to-all-start.1 = ((bf16[8,8,256]{2,1,0:T(8,128)(2,1)}), bf16[8,8,256]{2,1,0:T(8,128)(2,1)S(1)}, u32[]{:S(2)}, u32[]{:S(2)}) async-start(bf16[8,8,256]{2,1,0:T(8,128)(2,1)} %broadcast_in_dim.90), calls=%async_computation.1 | async-start | bytes 65536 | tf_op jit(solution)/shard_map/all_to_all | solution.py:373
  76.6 12.1 %near.6.refs_4_ = f32[65,32,256]{2,1,0:T(8,128)} custom-call(f32[1]{0:T(128)} %bitcast.1.scale_ref, s32[5]{0:T(128)} %copy-done.6, s32[5,128]{1,0:T(8,128)} %fusion.66.lst, bf16[2,560,256]{2,1,0:T(8,128)(2,1)} %collective-permute-done.1.refs_0_, bf16[2,560,256]{2,1,0:T(8,128)(2,1)} %copy-done.21, bf16[2,560,256]{2,1,0:T(8,128)(2,1)} %collective-permute-done.2.refs_2_, ...), custom_call_target="tpu_custom_call" | custom-call | flops 2415919104 | bytes 4194304 | tf_op jit(solution)/shard_map/near/pallas_call | solution.py:236
  89.5 1.4 collective-permute-start.9
  91.8 3.2 %collective-permute-start.15 = (bf16[2,560,256]{2,1,0:T(8,128)(2,1)}, bf16[2,560,256]{2,1,0:T(8,128)(2,1)}, u32[]{:S(2)}, u32[]{:S(2)}) collective-permute-start(bf16[2,560,256]{2,1,0:T(8,128)(2,1)} %collective-permute-done.12.refs_3_), channel_id=1, source_target_pairs={{0,28},{4,0},{8,4},{12,8},{16,12},{20,16},{24,20},{28,24},{1,29},{... | collective-permute-start | bytes 1720328 | tf_op jit(solution)/shard_map/ppermute | solution.py:468
  95.2 1.1 convolution_convert_fusion
  96.4 4.9 %all-to-all-start.2 = ((bf16[32,16,256]{2,1,0:T(8,128)(2,1)}), bf16[32,16,256]{2,1,0:T(8,128)(2,1)S(1)}, u32[]{:S(2)}, u32[]{:S(2)}) async-start(bf16[32,16,256]{2,1,0:T(8,128)(2,1)} %bitcast.12), calls=%async_computation.2 | async-start | bytes 524288 | tf_op jit(solution)/shard_map/all_to_all | solution.py:420
  101.3 12.0 %near.7.refs_4_ = f32[65,32,256]{2,1,0:T(8,128)} custom-call(f32[1]{0:T(128)} %bitcast.1.scale_ref, s32[5]{0:T(128)} %copy-done.6, s32[5,128]{1,0:T(8,128)} %fusion.66.lst, bf16[2,560,256]{2,1,0:T(8,128)(2,1)} %copy-done.19, bf16[2,560,256]{2,1,0:T(8,128)(2,1)} %collective-permute-done.11.refs_1_, bf16[2,560,256]{2,1,0:T(8,128)(2,1)} %copy-done.20, ...), custom_call_target="tpu_custom_call" | custom-call | flops 2415919104 | bytes 4194304 | tf_op jit(solution)/shard_map/near/pallas_call | solution.py:236
  113.9 8.3 %collective-permute-done.14.refs_1_ = bf16[2,560,256]{2,1,0:T(8,128)(2,1)S(1)} collective-permute-done((bf16[2,560,256]{2,1,0:T(8,128)(2,1)}, bf16[2,560,256]{2,1,0:T(8,128)(2,1)S(1)}, u32[]{:S(2)}, u32[]{:S(2)}) %collective-permute-start.14) | collective-permute-done | bytes 573472 | tf_op jit(solution)/shard_map/ppermute | solution.py:467
  122.2 3.8 %all-to-all-done.2 = bf16[32,16,256]{2,1,0:T(8,128)(2,1)S(1)} async-done(((bf16[32,16,256]{2,1,0:T(8,128)(2,1)}), bf16[32,16,256]{2,1,0:T(8,128)(2,1)S(1)}, u32[]{:S(2)}, u32[]{:S(2)}) %all-to-all-start.2) | async-done | bytes 262176 | tf_op jit(solution)/shard_map/all_to_all | solution.py:420
  126.4 10.7 %near.8.refs_2_ = f32[65,32,256]{2,1,0:T(8,128)} custom-call(f32[1]{0:T(128)} %bitcast.1.scale_ref, s32[5]{0:T(128)} %copy-done.6, s32[5,128]{1,0:T(8,128)} %fusion.66.lst, bf16[2,560,256]{2,1,0:T(8,128)(2,1)} %collective-permute-done.9.refs_0_, bf16[2,560,256]{2,1,0:T(8,128)(2,1)} %copy-done.23, bf16[2,560,256]{2,1,0:T(8,128)(2,1)} %collective-permute-done.10.refs_2_, ...), custom_call_target="tpu_custom_call" | custom-call | flops 2415919104 | bytes 4194304 | tf_op jit(solution)/shard_map/near/pallas_call | solution.py:236
  137.2 1.7 %copy-done.12 = f32[65,32,256]{2,1,0:T(8,128)S(1)} copy-done((f32[65,32,256]{2,1,0:T(8,128)S(1)}, f32[65,32,256]{2,1,0:T(8,128)}, u32[]{:S(2)}) %copy-start.12) | copy-done | bytes 2129944
  138.9 7.2 %near.9 = (bf16[512,256]{1,0:T(8,128)(2,1)S(1)}, bf16[512,256]{1,0:T(8,128)(2,1)}, bf16[512,256]{1,0:T(8,128)(2,1)}, bf16[512,256]{1,0:T(8,128)(2,1)S(1)}) custom-call(f32[1]{0:T(128)} %bitcast.1.scale_ref, s32[5]{0:T(128)S(1)} %copy-done.7, s32[5,128]{1,0:T(8,128)S(1)} %copy-done.5, bf16[2,560,256]{2,1,0:T(8,128)(2,1)S(1)} %collective-permute-done.13.refs_0_, ...), custom_call_target="tpu_custom_call" | custom-call | flops 1207959552 | bytes 4194304 | tf_op jit(solution)/shard_map/near/pallas_call | solution.py:236
  146.2 1.0 collective-permute-start.17
  147.1 2.1 %collective-permute-start.18 = (bf16[512,256]{1,0:T(8,128)(2,1)}, bf16[512,256]{1,0:T(8,128)(2,1)S(1)}, u32[]{:S(2)}, u32[]{:S(2)}) collective-permute-start(bf16[512,256]{1,0:T(8,128)(2,1)} %get-tuple-element.91), channel_id=1, source_target_pairs={{0,2},{1,3},{2,0},{3,1},{4,6},{5,7},{6,4},{7,5},{8,10},{9,11},{10,... | collective-permute-start | bytes 786440 | tf_op jit(solution)/shard_map/ppermute | solution.py:492
  150.0 8.1 %home.1.home_ref = f32[4096,128]{1,0:T(8,128)S(1)} custom-call(s32[1]{0:T(128)} %bitcast.y_ref, f32[4]{0:T(128)S(1)} %get-tuple-element.102.scale_ref, bf16[560,256]{1,0:T(8,128)(2,1)S(1)} %copy-done.4, bf16[560,256]{1,0:T(8,128)(2,1)S(1)} %copy-done.8, bf16[560,256]{1,0:T(8,128)(2,1)S(1)} %copy-done.9, bf16[560,256]{1,0:T(8,128)(2,1)S(1)} %copy-done.10, ...), custom_call_target="tpu_custom_call" | custom-call | flops 2147483648 | bytes 3145728 | tf_op jit(solution)/shard_map/home/pallas_call | solution.py:327
  158.1 5.6 %collective-permute-done.19.n3 = bf16[512,256]{1,0:T(8,128)(2,1)S(1)} collective-permute-done((bf16[512,256]{1,0:T(8,128)(2,1)S(1)}, bf16[512,256]{1,0:T(8,128)(2,1)S(1)}, u32[]{:S(2)}, u32[]{:S(2)}) %collective-permute-start.19) | collective-permute-done | bytes 262176 | tf_op jit(solution)/shard_map/ppermute | solution.py:492
  163.7 2.2 %final.1 = bf16[4096,128]{1,0:T(8,128)(2,1)} custom-call(s32[1]{0:T(128)} %bitcast.y_ref, f32[4096,128]{1,0:T(8,128)S(1)} %home.1.home_ref, bf16[512,256]{1,0:T(8,128)(2,1)S(1)} %get-tuple-element.89.n0, bf16[512,256]{1,0:T(8,128)(2,1)S(1)} %collective-permute-done.17.n1, bf16[512,256]{1,0:T(8,128)(2,1)S(1)} %collective-permute-done.18.n2, ...), custom_call_target="tpu_custom_call" | custom-call | tf_op jit(solution)/shard_map/final/pallas_call | solution.py:359
  (110 shorter events, 12.0 us)
Async XLA Ops:
  0.0 67.4 %copy-start = (bf16[128,128]{1,0:T(8,128)(2,1)S(1)}, bf16[128,128]{1,0:T(8,128)(2,1)}, u32[]{:S(2)}) copy-start(bf16[128,128]{1,0:T(8,128)(2,1)} %param.22) | copy-start | bytes 98308
  3.1 29.6 %copy-start.18 = (f32[4]{0:T(128)S(1)}, f32[4]{0:T(128)}, u32[]{:S(2)}) copy-start(f32[4]{0:T(128)} %param.19) | copy-start | bytes 52
  3.1 10.1 %collective-permute-start = (bf16[560,256]{1,0:T(8,128)(2,1)}, bf16[560,256]{1,0:T(8,128)(2,1)S(1)}, u32[]{:S(2)}, u32[]{:S(2)}) collective-permute-start(bf16[560,256]{1,0:T(8,128)(2,1)} %get-tuple-element.85.v1), channel_id=1, source_target_pairs={{0,1},{1,2},{2,3},{3,0},{4,5},{5,6},{6,7},{7,4},{8,9},{9,10},{10,1... | collective-permute-start | bytes 860168 | tf_op jit(solution)/shard_map/ppermute | solution.py:453
  4.7 31.8 %collective-permute-start.3 = (bf16[560,256]{1,0:T(8,128)(2,1)}, bf16[560,256]{1,0:T(8,128)(2,1)S(1)}, u32[]{:S(2)}, u32[]{:S(2)}) collective-permute-start(bf16[560,256]{1,0:T(8,128)(2,1)} %get-tuple-element.86.v2), channel_id=1, source_target_pairs={{0,2},{1,3},{2,0},{3,1},{4,6},{5,7},{6,4},{7,5},{8,10},{9,11},{10,... | collective-permute-start | bytes 860168 | tf_op jit(solution)/shard_map/ppermute | solution.py:453
  7.6 28.9 %collective-permute-start.4 = (bf16[560,256]{1,0:T(8,128)(2,1)}, bf16[560,256]{1,0:T(8,128)(2,1)S(1)}, u32[]{:S(2)}, u32[]{:S(2)}) collective-permute-start(bf16[560,256]{1,0:T(8,128)(2,1)} %get-tuple-element.87.v3), channel_id=1, source_target_pairs={{0,3},{1,0},{2,1},{3,2},{4,7},{5,4},{6,5},{7,6},{8,11},{9,8},{10,9... | collective-permute-start | bytes 860168 | tf_op jit(solution)/shard_map/ppermute | solution.py:453
  10.9 29.6 %copy-start.6 = (s32[5]{0:T(128)}, s32[5]{0:T(128)S(1)}, u32[]{:S(2)}) copy-start(s32[5]{0:T(128)S(1)} %get-tuple-element.94.cnt) | copy-start | bytes 64
  14.2 27.1 %copy-start.1 = (bf16[2,560,256]{2,1,0:T(8,128)(2,1)}, bf16[2,560,256]{2,1,0:T(8,128)(2,1)S(1)}, u32[]{:S(2)}) copy-start(bf16[2,560,256]{2,1,0:T(8,128)(2,1)S(1)} %pack.2.refs_0_) | copy-start | bytes 1720324
  16.3 50.5 %all-to-all-start = ((bf16[32,40,128]{2,1,0:T(8,128)(2,1)}), bf16[32,40,128]{2,1,0:T(8,128)(2,1)S(1)}, u32[]{:S(2)}, u32[]{:S(2)}) async-start(bf16[32,40,128]{2,1,0:T(8,128)(2,1)} %copy.29), calls=%async_computation | async-start | bytes 655360 | tf_op jit(solution)/shard_map/all_to_all | solution.py:389
  33.3 21.4 %collective-permute-start.1 = (bf16[2,560,256]{2,1,0:T(8,128)(2,1)S(1)}, bf16[2,560,256]{2,1,0:T(8,128)(2,1)}, u32[]{:S(2)}, u32[]{:S(2)}) collective-permute-start(bf16[2,560,256]{2,1,0:T(8,128)(2,1)S(1)} %pack.2.refs_0_), channel_id=1, source_target_pairs={{0,4},{4,8},{8,12},{12,16},{16,20},{20,24},{24,28},{28,0},{1,5},{5... | collective-permute-start | bytes 1720328 | tf_op jit(solution)/shard_map/ppermute | solution.py:467
  35.1 19.6 %collective-permute-start.2 = (bf16[2,560,256]{2,1,0:T(8,128)(2,1)S(1)}, bf16[2,560,256]{2,1,0:T(8,128)(2,1)}, u32[]{:S(2)}, u32[]{:S(2)}) collective-permute-start(bf16[2,560,256]{2,1,0:T(8,128)(2,1)S(1)} %pack.2.refs_0_), channel_id=1, source_target_pairs={{0,28},{4,0},{8,4},{12,8},{16,12},{20,16},{24,20},{28,24},{1,29},{... | collective-permute-start | bytes 1720328 | tf_op jit(solution)/shard_map/ppermute | solution.py:468
  36.6 30.3 %collective-permute-start.7 = (bf16[2,560,256]{2,1,0:T(8,128)(2,1)S(1)}, bf16[2,560,256]{2,1,0:T(8,128)(2,1)S(1)}, u32[]{:S(2)}, u32[]{:S(2)}) collective-permute-start(bf16[2,560,256]{2,1,0:T(8,128)(2,1)S(1)} %pack.3.refs_1_), channel_id=1, source_target_pairs={{0,4},{4,8},{8,12},{12,16},{16,20},{20,24},{24,28},{28,0},{1,5},{5... | collective-permute-start | bytes 1720328 | tf_op jit(solution)/shard_map/ppermute | solution.py:467
  37.2 29.6 %collective-permute-start.8 = (bf16[2,560,256]{2,1,0:T(8,128)(2,1)S(1)}, bf16[2,560,256]{2,1,0:T(8,128)(2,1)S(1)}, u32[]{:S(2)}, u32[]{:S(2)}) collective-permute-start(bf16[2,560,256]{2,1,0:T(8,128)(2,1)S(1)} %pack.3.refs_1_), channel_id=1, source_target_pairs={{0,28},{4,0},{8,4},{12,8},{16,12},{20,16},{24,20},{28,24},{1,29},{... | collective-permute-start | bytes 1720328 | tf_op jit(solution)/shard_map/ppermute | solution.py:468
  41.3 29.6 %copy-start.17 = (s32[128]{0:T(128)S(1)}, s32[128]{0:T(128)}, u32[]{:S(2)}) copy-start(s32[128]{0:T(128)} %param.18) | copy-start | bytes 1540
  49.1 27.3 %copy-start.14 = (bf16[128,128]{1,0:T(8,128)(2,1)S(1)}, bf16[128,128]{1,0:T(8,128)(2,1)}, u32[]{:S(2)}) copy-start(bf16[128,128]{1,0:T(8,128)(2,1)} %param.24) | copy-start | bytes 98308
  54.7 34.1 %collective-permute-start.5 = (bf16[2,560,256]{2,1,0:T(8,128)(2,1)}, bf16[2,560,256]{2,1,0:T(8,128)(2,1)S(1)}, u32[]{:S(2)}, u32[]{:S(2)}) collective-permute-start(bf16[2,560,256]{2,1,0:T(8,128)(2,1)} %collective-permute-done.1.refs_0_), channel_id=1, source_target_pairs={{0,4},{4,8},{8,12},{12,16},{16,20},{20,24},{24,28},{28,0},{1,5},{5... | collective-permute-start | bytes 1720328 | tf_op jit(solution)/shard_map/ppermute | solution.py:467
  54.8 33.9 %collective-permute-start.6 = (bf16[2,560,256]{2,1,0:T(8,128)(2,1)}, bf16[2,560,256]{2,1,0:T(8,128)(2,1)S(1)}, u32[]{:S(2)}, u32[]{:S(2)}) collective-permute-start(bf16[2,560,256]{2,1,0:T(8,128)(2,1)} %collective-permute-done.2.refs_2_), channel_id=1, source_target_pairs={{0,28},{4,0},{8,4},{12,8},{16,12},{20,16},{24,20},{28,24},{1,29},{... | collective-permute-start | bytes 1720328 | tf_op jit(solution)/shard_map/ppermute | solution.py:468
  67.6 23.3 %collective-permute-start.11 = (bf16[2,560,256]{2,1,0:T(8,128)(2,1)S(1)}, bf16[2,560,256]{2,1,0:T(8,128)(2,1)}, u32[]{:S(2)}, u32[]{:S(2)}) collective-permute-start(bf16[2,560,256]{2,1,0:T(8,128)(2,1)S(1)} %collective-permute-done.7.refs_1_), channel_id=1, source_target_pairs={{0,4},{4,8},{8,12},{12,16},{16,20},{20,24},{24,28},{28,0},{1,5},{5... | collective-permute-start | bytes 1720328 | tf_op jit(solution)/shard_map/ppermute | solution.py:467
  67.8 23.1 %collective-permute-start.12 = (bf16[2,560,256]{2,1,0:T(8,128)(2,1)S(1)}, bf16[2,560,256]{2,1,0:T(8,128)(2,1)}, u32[]{:S(2)}, u32[]{:S(2)}) collective-permute-start(bf16[2,560,256]{2,1,0:T(8,128)(2,1)S(1)} %collective-permute-done.8.refs_3_), channel_id=1, source_target_pairs={{0,28},{4,0},{8,4},{12,8},{16,12},{20,16},{24,20},{28,24},{1,29},{... | collective-permute-start | bytes 1720328 | tf_op jit(solution)/shard_map/ppermute | solution.py:468
  71.7 19.3 %all-to-all-start.1 = ((bf16[8,8,256]{2,1,0:T(8,128)(2,1)}), bf16[8,8,256]{2,1,0:T(8,128)(2,1)S(1)}, u32[]{:S(2)}, u32[]{:S(2)}) async-start(bf16[8,8,256]{2,1,0:T(8,128)(2,1)} %broadcast_in_dim.90), calls=%async_computation.1 | async-start | bytes 65536 | tf_op jit(solution)/shard_map/all_to_all | solution.py:373
  76.6 18.5 %copy-start.16 = (bf16[128,128]{1,0:T(8,128)(2,1)S(1)}, bf16[128,128]{1,0:T(8,128)(2,1)}, u32[]{:S(2)}) copy-start(bf16[128,128]{1,0:T(8,128)(2,1)} %param.23) | copy-start | bytes 98308
  88.8 24.6 %collective-permute-start.10 = (bf16[2,560,256]{2,1,0:T(8,128)(2,1)S(1)}, bf16[2,560,256]{2,1,0:T(8,128)(2,1)}, u32[]{:S(2)}, u32[]{:S(2)}) collective-permute-start(bf16[2,560,256]{2,1,0:T(8,128)(2,1)S(1)} %collective-permute-done.6.refs_2_), channel_id=1, source_target_pairs={{0,28},{4,0},{8,4},{12,8},{16,12},{20,16},{24,20},{28,24},{1,29},{... | collective-permute-start | bytes 1720328 | tf_op jit(solution)/shard_map/ppermute | solution.py:468
  89.5 23.8 %collective-permute-start.9 = (bf16[2,560,256]{2,1,0:T(8,128)(2,1)S(1)}, bf16[2,560,256]{2,1,0:T(8,128)(2,1)}, u32[]{:S(2)}, u32[]{:S(2)}) collective-permute-start(bf16[2,560,256]{2,1,0:T(8,128)(2,1)S(1)} %collective-permute-done.5.refs_0_), channel_id=1, source_target_pairs={{0,4},{4,8},{8,12},{12,16},{16,20},{20,24},{24,28},{28,0},{1,5},{5... | collective-permute-start | bytes 1720328 | tf_op jit(solution)/shard_map/ppermute | solution.py:467
  91.7 30.5 %collective-permute-start.14 = (bf16[2,560,256]{2,1,0:T(8,128)(2,1)}, bf16[2,560,256]{2,1,0:T(8,128)(2,1)S(1)}, u32[]{:S(2)}, u32[]{:S(2)}) collective-permute-start(bf16[2,560,256]{2,1,0:T(8,128)(2,1)} %collective-permute-done.11.refs_1_), channel_id=1, source_target_pairs={{0,4},{4,8},{8,12},{12,16},{16,20},{20,24},{24,28},{28,0},{1,5},{5... | collective-permute-start | bytes 1720328 | tf_op jit(solution)/shard_map/ppermute | solution.py:467
  91.8 30.4 %collective-permute-start.15 = (bf16[2,560,256]{2,1,0:T(8,128)(2,1)}, bf16[2,560,256]{2,1,0:T(8,128)(2,1)}, u32[]{:S(2)}, u32[]{:S(2)}) collective-permute-start(bf16[2,560,256]{2,1,0:T(8,128)(2,1)} %collective-permute-done.12.refs_3_), channel_id=1, source_target_pairs={{0,28},{4,0},{8,4},{12,8},{16,12},{20,16},{24,20},{28,24},{1,29},{... | collective-permute-start | bytes 1720328 | tf_op jit(solution)/shard_map/ppermute | solution.py:468
  96.4 29.6 %all-to-all-start.2 = ((bf16[32,16,256]{2,1,0:T(8,128)(2,1)}), bf16[32,16,256]{2,1,0:T(8,128)(2,1)S(1)}, u32[]{:S(2)}, u32[]{:S(2)}) async-start(bf16[32,16,256]{2,1,0:T(8,128)(2,1)} %bitcast.12), calls=%async_computation.2 | async-start | bytes 524288 | tf_op jit(solution)/shard_map/all_to_all | solution.py:420
  113.4 23.8 %collective-permute-start.13 = (bf16[2,560,256]{2,1,0:T(8,128)(2,1)}, bf16[2,560,256]{2,1,0:T(8,128)(2,1)S(1)}, u32[]{:S(2)}, u32[]{:S(2)}) collective-permute-start(bf16[2,560,256]{2,1,0:T(8,128)(2,1)} %collective-permute-done.9.refs_0_), channel_id=1, source_target_pairs={{0,4},{4,8},{8,12},{12,16},{16,20},{20,24},{24,28},{28,0},{1,5},{5... | collective-permute-start | bytes 1720328 | tf_op jit(solution)/shard_map/ppermute | solution.py:482
  122.2 15.0 %collective-permute-start.16 = (bf16[2,560,256]{2,1,0:T(8,128)(2,1)}, bf16[2,560,256]{2,1,0:T(8,128)(2,1)S(1)}, u32[]{:S(2)}, u32[]{:S(2)}) collective-permute-start(bf16[2,560,256]{2,1,0:T(8,128)(2,1)} %collective-permute-done.15.refs_3_), channel_id=1, source_target_pairs={{0,28},{4,0},{8,4},{12,8},{16,12},{20,16},{24,20},{28,24},{1,29},{... | collective-permute-start | bytes 1720328 | tf_op jit(solution)/shard_map/ppermute | solution.py:483
  126.4 23.4 %copy-start.15 = (bf16[256,64]{0,1:T(8,128)(2,1)S(1)}, bf16[256,64]{0,1:T(8,128)(2,1)}, u32[]{:S(2)}) copy-start(bf16[256,64]{0,1:T(8,128)(2,1)} %param.26) | copy-start | bytes 98308
  137.1 12.8 %copy-start.4 = (bf16[560,256]{1,0:T(8,128)(2,1)S(1)}, bf16[560,256]{1,0:T(8,128)(2,1)}, u32[]{:S(2)}) copy-start(bf16[560,256]{1,0:T(8,128)(2,1)} %get-tuple-element.84.refs_0_.v0.x_ref.y_row.z_ref) | copy-start | bytes 860164
  146.2 11.9 %collective-permute-start.17 = (bf16[512,256]{1,0:T(8,128)(2,1)}, bf16[512,256]{1,0:T(8,128)(2,1)S(1)}, u32[]{:S(2)}, u32[]{:S(2)}) collective-permute-start(bf16[512,256]{1,0:T(8,128)(2,1)} %get-tuple-element.90), channel_id=1, source_target_pairs={{0,3},{1,0},{2,1},{3,2},{4,7},{5,4},{6,5},{7,6},{8,11},{9,8},{10,9... | collective-permute-start | bytes 786440 | tf_op jit(solution)/shard_map/ppermute | solution.py:492
  147.1 10.9 %collective-permute-start.18 = (bf16[512,256]{1,0:T(8,128)(2,1)}, bf16[512,256]{1,0:T(8,128)(2,1)S(1)}, u32[]{:S(2)}, u32[]{:S(2)}) collective-permute-start(bf16[512,256]{1,0:T(8,128)(2,1)} %get-tuple-element.91), channel_id=1, source_target_pairs={{0,2},{1,3},{2,0},{3,1},{4,6},{5,7},{6,4},{7,5},{8,10},{9,11},{10,... | collective-permute-start | bytes 786440 | tf_op jit(solution)/shard_map/ppermute | solution.py:492
  149.2 14.4 %collective-permute-start.19 = (bf16[512,256]{1,0:T(8,128)(2,1)S(1)}, bf16[512,256]{1,0:T(8,128)(2,1)S(1)}, u32[]{:S(2)}, u32[]{:S(2)}) collective-permute-start(bf16[512,256]{1,0:T(8,128)(2,1)S(1)} %get-tuple-element.92), channel_id=1, source_target_pairs={{0,1},{1,2},{2,3},{3,0},{4,5},{5,6},{6,7},{7,4},{8,9},{9,10},{10,1... | collective-permute-start | bytes 786440 | tf_op jit(solution)/shard_map/ppermute | solution.py:492
  (15 other events, 139.8 us)

commit v4 on v3

--- a/solution.py
+++ b/solution.py
@@ -422,8 +422,8 @@
 
 def after(rows, acc, extra):
     (below_a, below_b), (above_a, above_b) = rows
-    below_a, above_a, acc = lax.optimization_barrier((below_a, above_a, acc))
-    below_b, above_b, acc, extra = lax.optimization_barrier((below_b, above_b, acc, extra))
+    below_a, above_a, acc, extra = lax.optimization_barrier((below_a, above_a, acc, extra))
+    below_b, above_b, acc = lax.optimization_barrier((below_b, above_b, acc))
     return ([below_a, below_b], [above_a, above_b]), acc, extra
 
 

time: 166 us -> 155 us (0.934)
  the two profiles are of different devices: /device:TPU:6 before, /device:TPU:36 now
where the time goes in v4:
time: 155 us; the launch traced here: 154 us
  starting transfers between devices  61.8 us (40%)
  Pallas kernels  60.9 us (39%)
  waiting for transfers between devices  17.4 us (11%)
  local copies, waits for them, and re-layouts  7.52 us (5%)
  other arithmetic  3.17 us (2%)
  matrix products  2.84 us (2%)
    pallas_call x5, Pallas kernels, near_step(): pl.pallas_call(functools.partial(near_kernel, number, lengths, first, las...  47.4 us
    all_to_all x1, starting transfers between devices, spread_summaries(): return lax.all_to_all(sent, DEV, 0, 0, tiled=True)  17.4 us
    ppermute x6, starting transfers between devices, onward(): below = [lax.ppermute(half, 'dev_0', up) for half in below]  13.4 us
    all_to_all x1, starting transfers between devices, far_down(): lax.all_to_all(down.reshape(-1, BLK, down.shape[1]), DEV, 0, 0, tiled=True)  10.8 us
    pallas_call x1, Pallas kernels, home(): pl.pallas_call(home_kernel, grid=(BLK // 4,), in_specs=[smem(), smem()] +...  8.11 us
    ppermute x3, waiting for transfers between devices, per_device(): lax.ppermute(near[s], 'dev_1', back_to[s])  6.55 us
    ppermute x3, starting transfers between devices, per_device(): lax.ppermute(messages[s], 'dev_1', ahead[s])  5.83 us
    all_to_all x1, starting transfers between devices, copies(): return lax.all_to_all(sent, axis, 0, 0, tiled=True)  4.8 us
  transfers between devices with their start and end apart: 23, of which 7 were waited for; matrix products, arithmetic and copies ran while one was open for 6% of the time, Pallas kernels for 32%

profile of v4, /device:TPU:36, one launch (start us, length us, event | category | flops | bytes accessed | tf_op | source)
XLA Modules:
  0.0 154.2 jit_solution(3829434460564871310)
XLA Ops:
  0.0 3.1 %prep.1 = (bf16[560,256]{1,0:T(8,128)(2,1)}, bf16[560,256]{1,0:T(8,128)(2,1)}, bf16[560,256]{1,0:T(8,128)(2,1)}, bf16[560,256]{1,0:T(8,128)(2,1)}, bf16[16,64,128]{2,1,0:T(8,128)(2,1)}) custom-call(s32[1]{0:T(128)} %bitcast.y_ref, bf16[4096,128]{1,0:T(8,128)(2,1)} %f_ref.1, bf16[3,4096]{1,0:T(4,128)(2,1)} %xyz_ref.1, bf16[128,128]{1,0:T(8,128)(2,1)} %wn_ref.1, ...), custom_call_target="tpu_custom_call" | custom-call | tf_op jit(solution)/shard_map/prep/pallas_call | solution.py:66
  3.1 1.6 %collective-permute-start = (bf16[560,256]{1,0:T(8,128)(2,1)}, bf16[560,256]{1,0:T(8,128)(2,1)S(1)}, u32[]{:S(2)}, u32[]{:S(2)}) collective-permute-start(bf16[560,256]{1,0:T(8,128)(2,1)} %get-tuple-element.85.v1), channel_id=1, source_target_pairs={{0,1},{1,2},{2,3},{3,0},{4,5},{5,6},{6,7},{7,4},{8,9},{9,10},{10,1... | collective-permute-start | bytes 860168 | tf_op jit(solution)/shard_map/ppermute | solution.py:453
  4.7 2.9 %collective-permute-start.3 = (bf16[560,256]{1,0:T(8,128)(2,1)}, bf16[560,256]{1,0:T(8,128)(2,1)S(1)}, u32[]{:S(2)}, u32[]{:S(2)}) collective-permute-start(bf16[560,256]{1,0:T(8,128)(2,1)} %get-tuple-element.86.v2), channel_id=1, source_target_pairs={{0,2},{1,3},{2,0},{3,1},{4,6},{5,7},{6,4},{7,5},{8,10},{9,11},{10,... | collective-permute-start | bytes 860168 | tf_op jit(solution)/shard_map/ppermute | solution.py:453
  7.6 1.3 collective-permute-start.4
  10.9 2.2 %collective-permute-done.refs_1_ = bf16[560,256]{1,0:T(8,128)(2,1)S(1)} collective-permute-done((bf16[560,256]{1,0:T(8,128)(2,1)}, bf16[560,256]{1,0:T(8,128)(2,1)S(1)}, u32[]{:S(2)}, u32[]{:S(2)}) %collective-permute-start) | collective-permute-done | bytes 286752 | tf_op jit(solution)/shard_map/ppermute | solution.py:453
  14.2 2.0 %collective-permute-start.1 = (bf16[2,560,256]{2,1,0:T(8,128)(2,1)S(1)}, bf16[2,560,256]{2,1,0:T(8,128)(2,1)S(1)}, u32[]{:S(2)}, u32[]{:S(2)}) collective-permute-start(bf16[2,560,256]{2,1,0:T(8,128)(2,1)S(1)} %pack.2.refs_0_), channel_id=1, source_target_pairs={{0,4},{4,8},{8,12},{12,16},{16,20},{20,24},{24,28},{28,0},{1,5},{5... | collective-permute-start | bytes 1720328 | tf_op jit(solution)/shard_map/ppermute | solution.py:467
  16.3 1.0 copy.28
  18.2 17.4 %all-to-all-start = ((bf16[32,40,128]{2,1,0:T(8,128)(2,1)}), bf16[32,40,128]{2,1,0:T(8,128)(2,1)S(1)}, u32[]{:S(2)}, u32[]{:S(2)}) async-start(bf16[32,40,128]{2,1,0:T(8,128)(2,1)} %copy.29), calls=%async_computation | async-start | bytes 655360 | tf_op jit(solution)/shard_map/all_to_all | solution.py:389
  37.7 1.5 collective-permute-start.7
  39.8 7.9 %near.5 = (f32[65,32,256]{2,1,0:T(8,128)}, bf16[64,16,256]{2,1,0:T(8,128)(2,1)}) custom-call(f32[1]{0:T(128)} %bitcast.1.scale_ref, s32[5]{0:T(128)} %copy-done.6, s32[5,128]{1,0:T(8,128)} %fusion.66.lst, bf16[2,560,256]{2,1,0:T(8,128)(2,1)} %copy-done.1, bf16[2,560,256]{2,1,0:T(8,128)(2,1)} %copy-done.2), custom_call_target="tpu_custom_call" | custom-call | flops 1207959552 | bytes 4194304 | tf_op jit(solution)/shard_map/near/pallas_call | solution.py:236
  48.7 2.7 %collective-permute-start.5 = (bf16[2,560,256]{2,1,0:T(8,128)(2,1)S(1)}, bf16[2,560,256]{2,1,0:T(8,128)(2,1)}, u32[]{:S(2)}, u32[]{:S(2)}) collective-permute-start(bf16[2,560,256]{2,1,0:T(8,128)(2,1)S(1)} %collective-permute-done.1.refs_0_), channel_id=1, source_target_pairs={{0,4},{4,8},{8,12},{12,16},{16,20},{20,24},{24,28},{28,0},{1,5},{5... | collective-permute-start | bytes 1720328 | tf_op jit(solution)/shard_map/ppermute | solution.py:467
  52.2 4.8 %all-to-all-start.1 = ((bf16[8,8,256]{2,1,0:T(8,128)(2,1)}), bf16[8,8,256]{2,1,0:T(8,128)(2,1)S(1)}, u32[]{:S(2)}, u32[]{:S(2)}) async-start(bf16[8,8,256]{2,1,0:T(8,128)(2,1)} %broadcast_in_dim.90), calls=%async_computation.1 | async-start | bytes 65536 | tf_op jit(solution)/shard_map/all_to_all | solution.py:373
  57.0 2.4 %collective-permute-start.11 = (bf16[2,560,256]{2,1,0:T(8,128)(2,1)}, bf16[2,560,256]{2,1,0:T(8,128)(2,1)S(1)}, u32[]{:S(2)}, u32[]{:S(2)}) collective-permute-start(bf16[2,560,256]{2,1,0:T(8,128)(2,1)} %collective-permute-done.7.refs_1_), channel_id=1, source_target_pairs={{0,4},{4,8},{8,12},{12,16},{16,20},{20,24},{24,28},{28,0},{1,5},{5... | collective-permute-start | bytes 1720328 | tf_op jit(solution)/shard_map/ppermute | solution.py:467
  59.7 10.7 %near.6.refs_4_ = f32[65,32,256]{2,1,0:T(8,128)} custom-call(f32[1]{0:T(128)} %bitcast.1.scale_ref, s32[5]{0:T(128)} %copy-done.6, s32[5,128]{1,0:T(8,128)} %fusion.66.lst, bf16[2,560,256]{2,1,0:T(8,128)(2,1)} %copy-done.19, bf16[2,560,256]{2,1,0:T(8,128)(2,1)} %collective-permute-done.7.refs_1_, bf16[2,560,256]{2,1,0:T(8,128)(2,1)} %copy-done.20, ...), custom_call_target="tpu_custom_call" | custom-call | flops 2415919104 | bytes 4194304 | tf_op jit(solution)/shard_map/near/pallas_call | solution.py:236
  71.3 2.7 %collective-permute-done.11.refs_1_ = bf16[2,560,256]{2,1,0:T(8,128)(2,1)S(1)} collective-permute-done((bf16[2,560,256]{2,1,0:T(8,128)(2,1)}, bf16[2,560,256]{2,1,0:T(8,128)(2,1)S(1)}, u32[]{:S(2)}, u32[]{:S(2)}) %collective-permute-start.11) | collective-permute-done | bytes 573472 | tf_op jit(solution)/shard_map/ppermute | solution.py:467
  74.0 1.1 collective-permute-done.12.refs_3_
  75.1 1.1 collective-permute-start.10
  76.3 1.8 %collective-permute-start.9 = (bf16[2,560,256]{2,1,0:T(8,128)(2,1)}, bf16[2,560,256]{2,1,0:T(8,128)(2,1)}, u32[]{:S(2)}, u32[]{:S(2)}) collective-permute-start(bf16[2,560,256]{2,1,0:T(8,128)(2,1)} %collective-permute-done.5.refs_0_), channel_id=1, source_target_pairs={{0,4},{4,8},{8,12},{12,16},{16,20},{20,24},{24,28},{28,0},{1,5},{5... | collective-permute-start | bytes 1720328 | tf_op jit(solution)/shard_map/ppermute | solution.py:467
  78.1 3.0 %collective-permute-start.14 = (bf16[2,560,256]{2,1,0:T(8,128)(2,1)S(1)}, bf16[2,560,256]{2,1,0:T(8,128)(2,1)S(1)}, u32[]{:S(2)}, u32[]{:S(2)}) collective-permute-start(bf16[2,560,256]{2,1,0:T(8,128)(2,1)S(1)} %collective-permute-done.11.refs_1_), channel_id=1, source_target_pairs={{0,4},{4,8},{8,12},{12,16},{16,20},{20,24},{24,28},{28,0},{1,5},{5... | collective-permute-start | bytes 1720328 | tf_op jit(solution)/shard_map/ppermute | solution.py:467
  81.2 1.2 convolution_convert_fusion
  82.4 10.8 %all-to-all-start.2 = ((bf16[32,16,256]{2,1,0:T(8,128)(2,1)}), bf16[32,16,256]{2,1,0:T(8,128)(2,1)S(1)}, u32[]{:S(2)}, u32[]{:S(2)}) async-start(bf16[32,16,256]{2,1,0:T(8,128)(2,1)} %bitcast.12), calls=%async_computation.2 | async-start | bytes 524288 | tf_op jit(solution)/shard_map/all_to_all | solution.py:420
  93.2 12.1 %near.7.refs_4_ = f32[65,32,256]{2,1,0:T(8,128)} custom-call(f32[1]{0:T(128)} %bitcast.1.scale_ref, s32[5]{0:T(128)} %copy-done.6, s32[5,128]{1,0:T(8,128)} %fusion.66.lst, bf16[2,560,256]{2,1,0:T(8,128)(2,1)} %collective-permute-done.5.refs_0_, bf16[2,560,256]{2,1,0:T(8,128)(2,1)} %copy-done.21, bf16[2,560,256]{2,1,0:T(8,128)(2,1)} %collective-permute-done.6.refs_2_, ...), custom_call_target="tpu_custom_call" | custom-call | flops 2415919104 | bytes 4194304 | tf_op jit(solution)/shard_map/near/pallas_call | solution.py:236
  105.4 1.2 collective-permute-done.14.refs_1_
  107.4 4.4 %collective-permute-start.16 = (bf16[2,560,256]{2,1,0:T(8,128)(2,1)}, bf16[2,560,256]{2,1,0:T(8,128)(2,1)S(1)}, u32[]{:S(2)}, u32[]{:S(2)}) collective-permute-start(bf16[2,560,256]{2,1,0:T(8,128)(2,1)} %collective-permute-done.15.refs_3_), channel_id=1, source_target_pairs={{0,28},{4,0},{8,4},{12,8},{16,12},{20,16},{24,20},{28,24},{1,29},{... | collective-permute-start | bytes 1720328 | tf_op jit(solution)/shard_map/ppermute | solution.py:483
  111.9 3.3 %all-to-all-done.2 = bf16[32,16,256]{2,1,0:T(8,128)(2,1)S(1)} async-done(((bf16[32,16,256]{2,1,0:T(8,128)(2,1)}), bf16[32,16,256]{2,1,0:T(8,128)(2,1)S(1)}, u32[]{:S(2)}, u32[]{:S(2)}) %all-to-all-start.2) | async-done | bytes 262176 | tf_op jit(solution)/shard_map/all_to_all | solution.py:420
  115.6 10.7 %near.8.refs_2_ = f32[65,32,256]{2,1,0:T(8,128)} custom-call(f32[1]{0:T(128)} %bitcast.1.scale_ref, s32[5]{0:T(128)} %copy-done.6, s32[5,128]{1,0:T(8,128)} %fusion.66.lst, bf16[2,560,256]{2,1,0:T(8,128)(2,1)} %collective-permute-done.9.refs_0_, bf16[2,560,256]{2,1,0:T(8,128)(2,1)} %copy-done.23, bf16[2,560,256]{2,1,0:T(8,128)(2,1)} %copy-done.22, ...), custom_call_target="tpu_custom_call" | custom-call | flops 2415919104 | bytes 4194304 | tf_op jit(solution)/shard_map/near/pallas_call | solution.py:236
  126.5 1.7 %copy-done.12 = f32[65,32,256]{2,1,0:T(8,128)S(1)} copy-done((f32[65,32,256]{2,1,0:T(8,128)S(1)}, f32[65,32,256]{2,1,0:T(8,128)}, u32[]{:S(2)}) %copy-start.12) | copy-done | bytes 2129944
  128.1 6.0 %near.9 = (bf16[512,256]{1,0:T(8,128)(2,1)S(1)}, bf16[512,256]{1,0:T(8,128)(2,1)}, bf16[512,256]{1,0:T(8,128)(2,1)}, bf16[512,256]{1,0:T(8,128)(2,1)S(1)}) custom-call(f32[1]{0:T(128)} %bitcast.1.scale_ref, s32[5]{0:T(128)S(1)} %copy-done.7, s32[5,128]{1,0:T(8,128)S(1)} %copy-done.5, bf16[2,560,256]{2,1,0:T(8,128)(2,1)S(1)} %collective-permute-done.13.refs_0_, ...), custom_call_target="tpu_custom_call" | custom-call | flops 1207959552 | bytes 4194304 | tf_op jit(solution)/shard_map/near/pallas_call | solution.py:236
  134.1 1.5 collective-permute-start.17
  137.3 8.1 %home.1.home_ref = f32[4096,128]{1,0:T(8,128)S(1)} custom-call(s32[1]{0:T(128)} %bitcast.y_ref, f32[4]{0:T(128)S(1)} %get-tuple-element.102.scale_ref, bf16[560,256]{1,0:T(8,128)(2,1)S(1)} %copy-done.4, bf16[560,256]{1,0:T(8,128)(2,1)S(1)} %copy-done.8, bf16[560,256]{1,0:T(8,128)(2,1)S(1)} %copy-done.9, bf16[560,256]{1,0:T(8,128)(2,1)S(1)} %copy-done.10, ...), custom_call_target="tpu_custom_call" | custom-call | flops 2147483648 | bytes 3145728 | tf_op jit(solution)/shard_map/home/pallas_call | solution.py:327
  145.5 6.5 %collective-permute-done.19.n3 = bf16[512,256]{1,0:T(8,128)(2,1)S(1)} collective-permute-done((bf16[512,256]{1,0:T(8,128)(2,1)S(1)}, bf16[512,256]{1,0:T(8,128)(2,1)S(1)}, u32[]{:S(2)}, u32[]{:S(2)}) %collective-permute-start.19) | collective-permute-done | bytes 262176 | tf_op jit(solution)/shard_map/ppermute | solution.py:492
  152.0 2.2 %final.1 = bf16[4096,128]{1,0:T(8,128)(2,1)} custom-call(s32[1]{0:T(128)} %bitcast.y_ref, f32[4096,128]{1,0:T(8,128)S(1)} %home.1.home_ref, bf16[512,256]{1,0:T(8,128)(2,1)S(1)} %get-tuple-element.89.n0, bf16[512,256]{1,0:T(8,128)(2,1)S(1)} %collective-permute-done.17.n1, bf16[512,256]{1,0:T(8,128)(2,1)S(1)} %collective-permute-done.18.n2, ...), custom_call_target="tpu_custom_call" | custom-call | tf_op jit(solution)/shard_map/final/pallas_call | solution.py:359
  (110 shorter events, 12.4 us)
Async XLA Ops:
  0.0 48.5 %copy-start = (bf16[128,128]{1,0:T(8,128)(2,1)S(1)}, bf16[128,128]{1,0:T(8,128)(2,1)}, u32[]{:S(2)}) copy-start(bf16[128,128]{1,0:T(8,128)(2,1)} %param.22) | copy-start | bytes 98308
  3.1 33.3 %copy-start.18 = (f32[4]{0:T(128)S(1)}, f32[4]{0:T(128)}, u32[]{:S(2)}) copy-start(f32[4]{0:T(128)} %param.19) | copy-start | bytes 52
  3.1 10.1 %collective-permute-start = (bf16[560,256]{1,0:T(8,128)(2,1)}, bf16[560,256]{1,0:T(8,128)(2,1)S(1)}, u32[]{:S(2)}, u32[]{:S(2)}) collective-permute-start(bf16[560,256]{1,0:T(8,128)(2,1)} %get-tuple-element.85.v1), channel_id=1, source_target_pairs={{0,1},{1,2},{2,3},{3,0},{4,5},{5,6},{6,7},{7,4},{8,9},{9,10},{10,1... | collective-permute-start | bytes 860168 | tf_op jit(solution)/shard_map/ppermute | solution.py:453
  4.7 33.0 %collective-permute-start.3 = (bf16[560,256]{1,0:T(8,128)(2,1)}, bf16[560,256]{1,0:T(8,128)(2,1)S(1)}, u32[]{:S(2)}, u32[]{:S(2)}) collective-permute-start(bf16[560,256]{1,0:T(8,128)(2,1)} %get-tuple-element.86.v2), channel_id=1, source_target_pairs={{0,2},{1,3},{2,0},{3,1},{4,6},{5,7},{6,4},{7,5},{8,10},{9,11},{10,... | collective-permute-start | bytes 860168 | tf_op jit(solution)/shard_map/ppermute | solution.py:453
  7.6 30.1 %collective-permute-start.4 = (bf16[560,256]{1,0:T(8,128)(2,1)}, bf16[560,256]{1,0:T(8,128)(2,1)S(1)}, u32[]{:S(2)}, u32[]{:S(2)}) collective-permute-start(bf16[560,256]{1,0:T(8,128)(2,1)} %get-tuple-element.87.v3), channel_id=1, source_target_pairs={{0,3},{1,0},{2,1},{3,2},{4,7},{5,4},{6,5},{7,6},{8,11},{9,8},{10,9... | collective-permute-start | bytes 860168 | tf_op jit(solution)/shard_map/ppermute | solution.py:453
  10.9 26.8 %copy-start.6 = (s32[5]{0:T(128)}, s32[5]{0:T(128)S(1)}, u32[]{:S(2)}) copy-start(s32[5]{0:T(128)S(1)} %get-tuple-element.94.cnt) | copy-start | bytes 64
  14.2 25.7 %copy-start.1 = (bf16[2,560,256]{2,1,0:T(8,128)(2,1)}, bf16[2,560,256]{2,1,0:T(8,128)(2,1)S(1)}, u32[]{:S(2)}) copy-start(bf16[2,560,256]{2,1,0:T(8,128)(2,1)S(1)} %pack.2.refs_0_) | copy-start | bytes 1720324
  14.2 33.5 %collective-permute-start.1 = (bf16[2,560,256]{2,1,0:T(8,128)(2,1)S(1)}, bf16[2,560,256]{2,1,0:T(8,128)(2,1)S(1)}, u32[]{:S(2)}, u32[]{:S(2)}) collective-permute-start(bf16[2,560,256]{2,1,0:T(8,128)(2,1)S(1)} %pack.2.refs_0_), channel_id=1, source_target_pairs={{0,4},{4,8},{8,12},{12,16},{16,20},{20,24},{24,28},{28,0},{1,5},{5... | collective-permute-start | bytes 1720328 | tf_op jit(solution)/shard_map/ppermute | solution.py:467
  16.2 31.6 %collective-permute-start.2 = (bf16[2,560,256]{2,1,0:T(8,128)(2,1)S(1)}, bf16[2,560,256]{2,1,0:T(8,128)(2,1)S(1)}, u32[]{:S(2)}, u32[]{:S(2)}) collective-permute-start(bf16[2,560,256]{2,1,0:T(8,128)(2,1)S(1)} %pack.2.refs_0_), channel_id=1, source_target_pairs={{0,28},{4,0},{8,4},{12,8},{16,12},{20,16},{24,20},{28,24},{1,29},{... | collective-permute-start | bytes 1720328 | tf_op jit(solution)/shard_map/ppermute | solution.py:468
  18.2 29.8 %all-to-all-start = ((bf16[32,40,128]{2,1,0:T(8,128)(2,1)}), bf16[32,40,128]{2,1,0:T(8,128)(2,1)S(1)}, u32[]{:S(2)}, u32[]{:S(2)}) async-start(bf16[32,40,128]{2,1,0:T(8,128)(2,1)} %copy.29), calls=%async_computation | async-start | bytes 655360 | tf_op jit(solution)/shard_map/all_to_all | solution.py:389
  37.7 19.3 %collective-permute-start.7 = (bf16[2,560,256]{2,1,0:T(8,128)(2,1)S(1)}, bf16[2,560,256]{2,1,0:T(8,128)(2,1)}, u32[]{:S(2)}, u32[]{:S(2)}) collective-permute-start(bf16[2,560,256]{2,1,0:T(8,128)(2,1)S(1)} %pack.3.refs_1_), channel_id=1, source_target_pairs={{0,4},{4,8},{8,12},{12,16},{16,20},{20,24},{24,28},{28,0},{1,5},{5... | collective-permute-start | bytes 1720328 | tf_op jit(solution)/shard_map/ppermute | solution.py:467
  39.3 17.7 %collective-permute-start.8 = (bf16[2,560,256]{2,1,0:T(8,128)(2,1)S(1)}, bf16[2,560,256]{2,1,0:T(8,128)(2,1)}, u32[]{:S(2)}, u32[]{:S(2)}) collective-permute-start(bf16[2,560,256]{2,1,0:T(8,128)(2,1)S(1)} %pack.3.refs_1_), channel_id=1, source_target_pairs={{0,28},{4,0},{8,4},{12,8},{16,12},{20,16},{24,20},{28,24},{1,29},{... | collective-permute-start | bytes 1720328 | tf_op jit(solution)/shard_map/ppermute | solution.py:468
  47.7 12.0 %copy-start.19 = (bf16[2,560,256]{2,1,0:T(8,128)(2,1)}, bf16[2,560,256]{2,1,0:T(8,128)(2,1)S(1)}, u32[]{:S(2)}) copy-start(bf16[2,560,256]{2,1,0:T(8,128)(2,1)S(1)} %collective-permute-done.1.refs_0_) | copy-start | bytes 1720324
  47.7 11.9 %copy-start.20 = (bf16[2,560,256]{2,1,0:T(8,128)(2,1)}, bf16[2,560,256]{2,1,0:T(8,128)(2,1)S(1)}, u32[]{:S(2)}) copy-start(bf16[2,560,256]{2,1,0:T(8,128)(2,1)S(1)} %collective-permute-done.2.refs_2_) | copy-start | bytes 1720324
  48.7 21.8 %collective-permute-start.5 = (bf16[2,560,256]{2,1,0:T(8,128)(2,1)S(1)}, bf16[2,560,256]{2,1,0:T(8,128)(2,1)}, u32[]{:S(2)}, u32[]{:S(2)}) collective-permute-start(bf16[2,560,256]{2,1,0:T(8,128)(2,1)S(1)} %collective-permute-done.1.refs_0_), channel_id=1, source_target_pairs={{0,4},{4,8},{8,12},{12,16},{16,20},{20,24},{24,28},{28,0},{1,5},{5... | collective-permute-start | bytes 1720328 | tf_op jit(solution)/shard_map/ppermute | solution.py:467
  51.4 19.0 %collective-permute-start.6 = (bf16[2,560,256]{2,1,0:T(8,128)(2,1)S(1)}, bf16[2,560,256]{2,1,0:T(8,128)(2,1)}, u32[]{:S(2)}, u32[]{:S(2)}) collective-permute-start(bf16[2,560,256]{2,1,0:T(8,128)(2,1)S(1)} %collective-permute-done.2.refs_2_), channel_id=1, source_target_pairs={{0,28},{4,0},{8,4},{12,8},{16,12},{20,16},{24,20},{28,24},{1,29},{... | collective-permute-start | bytes 1720328 | tf_op jit(solution)/shard_map/ppermute | solution.py:468
  52.2 18.3 %all-to-all-start.1 = ((bf16[8,8,256]{2,1,0:T(8,128)(2,1)}), bf16[8,8,256]{2,1,0:T(8,128)(2,1)S(1)}, u32[]{:S(2)}, u32[]{:S(2)}) async-start(bf16[8,8,256]{2,1,0:T(8,128)(2,1)} %broadcast_in_dim.90), calls=%async_computation.1 | async-start | bytes 65536 | tf_op jit(solution)/shard_map/all_to_all | solution.py:373
  57.0 17.0 %collective-permute-start.11 = (bf16[2,560,256]{2,1,0:T(8,128)(2,1)}, bf16[2,560,256]{2,1,0:T(8,128)(2,1)S(1)}, u32[]{:S(2)}, u32[]{:S(2)}) collective-permute-start(bf16[2,560,256]{2,1,0:T(8,128)(2,1)} %collective-permute-done.7.refs_1_), channel_id=1, source_target_pairs={{0,4},{4,8},{8,12},{12,16},{16,20},{20,24},{24,28},{28,0},{1,5},{5... | collective-permute-start | bytes 1720328 | tf_op jit(solution)/shard_map/ppermute | solution.py:467
  59.4 15.8 %collective-permute-start.12 = (bf16[2,560,256]{2,1,0:T(8,128)(2,1)}, bf16[2,560,256]{2,1,0:T(8,128)(2,1)}, u32[]{:S(2)}, u32[]{:S(2)}) collective-permute-start(bf16[2,560,256]{2,1,0:T(8,128)(2,1)} %collective-permute-done.8.refs_3_), channel_id=1, source_target_pairs={{0,28},{4,0},{8,4},{12,8},{16,12},{20,16},{24,20},{28,24},{1,29},{... | collective-permute-start | bytes 1720328 | tf_op jit(solution)/shard_map/ppermute | solution.py:468
  59.7 21.4 %copy-start.16 = (bf16[128,128]{1,0:T(8,128)(2,1)S(1)}, bf16[128,128]{1,0:T(8,128)(2,1)}, u32[]{:S(2)}) copy-start(bf16[128,128]{1,0:T(8,128)(2,1)} %param.23) | copy-start | bytes 98308
  74.0 19.2 %copy-start.21 = (bf16[2,560,256]{2,1,0:T(8,128)(2,1)}, bf16[2,560,256]{2,1,0:T(8,128)(2,1)S(1)}, u32[]{:S(2)}) copy-start(bf16[2,560,256]{2,1,0:T(8,128)(2,1)S(1)} %collective-permute-done.11.refs_1_) | copy-start | bytes 1720324
  75.1 30.2 %collective-permute-start.10 = (bf16[2,560,256]{2,1,0:T(8,128)(2,1)}, bf16[2,560,256]{2,1,0:T(8,128)(2,1)S(1)}, u32[]{:S(2)}, u32[]{:S(2)}) collective-permute-start(bf16[2,560,256]{2,1,0:T(8,128)(2,1)} %collective-permute-done.6.refs_2_), channel_id=1, source_target_pairs={{0,28},{4,0},{8,4},{12,8},{16,12},{20,16},{24,20},{28,24},{1,29},{... | collective-permute-start | bytes 1720328 | tf_op jit(solution)/shard_map/ppermute | solution.py:468
  76.3 29.1 %collective-permute-start.9 = (bf16[2,560,256]{2,1,0:T(8,128)(2,1)}, bf16[2,560,256]{2,1,0:T(8,128)(2,1)}, u32[]{:S(2)}, u32[]{:S(2)}) collective-permute-start(bf16[2,560,256]{2,1,0:T(8,128)(2,1)} %collective-permute-done.5.refs_0_), channel_id=1, source_target_pairs={{0,4},{4,8},{8,12},{12,16},{16,20},{20,24},{24,28},{28,0},{1,5},{5... | collective-permute-start | bytes 1720328 | tf_op jit(solution)/shard_map/ppermute | solution.py:467
  78.1 28.5 %collective-permute-start.14 = (bf16[2,560,256]{2,1,0:T(8,128)(2,1)S(1)}, bf16[2,560,256]{2,1,0:T(8,128)(2,1)S(1)}, u32[]{:S(2)}, u32[]{:S(2)}) collective-permute-start(bf16[2,560,256]{2,1,0:T(8,128)(2,1)S(1)} %collective-permute-done.11.refs_1_), channel_id=1, source_target_pairs={{0,4},{4,8},{8,12},{12,16},{16,20},{20,24},{24,28},{28,0},{1,5},{5... | collective-permute-start | bytes 1720328 | tf_op jit(solution)/shard_map/ppermute | solution.py:467
  81.1 25.5 %collective-permute-start.15 = (bf16[2,560,256]{2,1,0:T(8,128)(2,1)}, bf16[2,560,256]{2,1,0:T(8,128)(2,1)}, u32[]{:S(2)}, u32[]{:S(2)}) collective-permute-start(bf16[2,560,256]{2,1,0:T(8,128)(2,1)} %collective-permute-done.12.refs_3_), channel_id=1, source_target_pairs={{0,28},{4,0},{8,4},{12,8},{16,12},{20,16},{24,20},{28,24},{1,29},{... | collective-permute-start | bytes 1720328 | tf_op jit(solution)/shard_map/ppermute | solution.py:468
  82.4 32.8 %all-to-all-start.2 = ((bf16[32,16,256]{2,1,0:T(8,128)(2,1)}), bf16[32,16,256]{2,1,0:T(8,128)(2,1)S(1)}, u32[]{:S(2)}, u32[]{:S(2)}) async-start(bf16[32,16,256]{2,1,0:T(8,128)(2,1)} %bitcast.12), calls=%async_computation.2 | async-start | bytes 524288 | tf_op jit(solution)/shard_map/all_to_all | solution.py:420
  107.4 19.0 %collective-permute-start.16 = (bf16[2,560,256]{2,1,0:T(8,128)(2,1)}, bf16[2,560,256]{2,1,0:T(8,128)(2,1)S(1)}, u32[]{:S(2)}, u32[]{:S(2)}) collective-permute-start(bf16[2,560,256]{2,1,0:T(8,128)(2,1)} %collective-permute-done.15.refs_3_), channel_id=1, source_target_pairs={{0,28},{4,0},{8,4},{12,8},{16,12},{20,16},{24,20},{28,24},{1,29},{... | collective-permute-start | bytes 1720328 | tf_op jit(solution)/shard_map/ppermute | solution.py:483
  111.9 14.5 %collective-permute-start.13 = (bf16[2,560,256]{2,1,0:T(8,128)(2,1)}, bf16[2,560,256]{2,1,0:T(8,128)(2,1)S(1)}, u32[]{:S(2)}, u32[]{:S(2)}) collective-permute-start(bf16[2,560,256]{2,1,0:T(8,128)(2,1)} %collective-permute-done.9.refs_0_), channel_id=1, source_target_pairs={{0,4},{4,8},{8,12},{12,16},{16,20},{20,24},{24,28},{28,0},{1,5},{5... | collective-permute-start | bytes 1720328 | tf_op jit(solution)/shard_map/ppermute | solution.py:482
  115.6 21.6 %copy-start.15 = (bf16[256,64]{0,1:T(8,128)(2,1)S(1)}, bf16[256,64]{0,1:T(8,128)(2,1)}, u32[]{:S(2)}) copy-start(bf16[256,64]{0,1:T(8,128)(2,1)} %param.26) | copy-start | bytes 98308
  134.1 11.4 %collective-permute-start.17 = (bf16[512,256]{1,0:T(8,128)(2,1)}, bf16[512,256]{1,0:T(8,128)(2,1)S(1)}, u32[]{:S(2)}, u32[]{:S(2)}) collective-permute-start(bf16[512,256]{1,0:T(8,128)(2,1)} %get-tuple-element.90), channel_id=1, source_target_pairs={{0,3},{1,0},{2,1},{3,2},{4,7},{5,4},{6,5},{7,6},{8,11},{9,8},{10,9... | collective-permute-start | bytes 786440 | tf_op jit(solution)/shard_map/ppermute | solution.py:492
  135.6 9.9 %collective-permute-start.18 = (bf16[512,256]{1,0:T(8,128)(2,1)}, bf16[512,256]{1,0:T(8,128)(2,1)S(1)}, u32[]{:S(2)}, u32[]{:S(2)}) collective-permute-start(bf16[512,256]{1,0:T(8,128)(2,1)} %get-tuple-element.91), channel_id=1, source_target_pairs={{0,2},{1,3},{2,0},{3,1},{4,6},{5,7},{6,4},{7,5},{8,10},{9,11},{10,... | collective-permute-start | bytes 786440 | tf_op jit(solution)/shard_map/ppermute | solution.py:492
  136.2 15.8 %collective-permute-start.19 = (bf16[512,256]{1,0:T(8,128)(2,1)S(1)}, bf16[512,256]{1,0:T(8,128)(2,1)S(1)}, u32[]{:S(2)}, u32[]{:S(2)}) collective-permute-start(bf16[512,256]{1,0:T(8,128)(2,1)S(1)} %get-tuple-element.92), channel_id=1, source_target_pairs={{0,1},{1,2},{2,3},{3,0},{4,5},{5,6},{6,7},{7,4},{8,9},{9,10},{10,1... | collective-permute-start | bytes 786440 | tf_op jit(solution)/shard_map/ppermute | solution.py:492
  (15 other events, 126.5 us)
